TPU v7x, 32 devices: a whole 2x2x4 slice. The times are simulated.
32 devices in a mesh: groups: 2 (over x), ctx: 16 (over z, y, core).
Axes of the slice: x: 2, y: 2, z: 4, core: 2. Of those that a mesh axis runs over, the one named last changes fastest.
Arguments:
- tokens: bfloat16 [3072, 1152], P(('groups', 'ctx')), parts along dimension 0, may hold values from -100 to 100
- owner: int32 [3072, 1], P(('groups', 'ctx')), parts along dimension 0, may hold values from 0 to 15; in each aligned block of 96 rows (0 to 95, 96 to 191, ...) at most 12 rows name the same one
- slot_map: int32 [32, 16, 12], P(('groups', 'ctx')), parts along dimension 0, may hold values from 0 to 47
- sizes: int32 [3072], P(('groups', 'ctx')), parts along dimension 0, may hold values from 1 to 4
- w_query: bfloat16 [1152, 576], replicated, may hold values from -0.1875 to 0.1875
- w_key: bfloat16 [1152, 576], replicated, may hold values from -0.1875 to 0.1875
- w_value: bfloat16 [1152, 576], replicated, may hold values from -0.1875 to 0.1875
- w_out: bfloat16 [576, 1152], replicated, may hold values from -0.25 to 0.25
Outputs:
- mixed: bfloat16 [3072, 1152], P(('groups', 'ctx')), parts along dimension 0
There are 2 independent parts, one for each index of `groups`. A program takes and returns all parts, laid end to end along the dimension named above; an argument that names none is the same for every part. Nothing has to cross between parts.
Inputs may be any that keep to these rules, and one draw needn't show every extreme that they name: Among the source tokens of one index of ctx, at most 12 name the same owner, and in some index exactly 12 do.
All inputs are finite; a program needn't handle non-finite values.
Results may differ from a plain program's by a relative error of at most 0.0085.
The roundings to bfloat16 on the way count: a program that leaves them out, or rounds other values in their place, can miss the bound.
Values may be sent and summed in bfloat16 or wider, within the bound.
No kernel may reach another device: no remote copies, remote signals or barrier semaphores. Data moves between devices by JAX's collectives and lax.ppermute only.
A program may use at most 128 MiB of HBM per device.

v0:
```python
import math

import jax
import jax.numpy as jnp
from jax import lax
from jax.sharding import PartitionSpec as P

HEADS = 8
HEAD = 72


def on_device(tokens, owner, slot_map, sizes, w_query, w_key, w_value, w_out):
    tok_rows = tokens.shape[0]
    shards = lax.axis_size("ctx")
    slots = slot_map.shape[2]
    places = shards * slots
    merged_rows = tok_rows // 2
    owners = owner[:, 0]
    marks = (owners[:, None] == jnp.arange(shards, dtype=jnp.int32)[None, :]).astype(jnp.int32)
    ranking = jnp.sum((jnp.cumsum(marks, axis=0) - marks) * marks, axis=1)
    bucket = owners * slots + ranking
    to_bucket = (bucket[:, None] == jnp.arange(places, dtype=jnp.int32)[None, :]).astype(
        jnp.bfloat16
    )
    outgoing = jnp.einsum(
        "tp,td->pd", to_bucket, tokens, preferred_element_type=jnp.float32
    ).astype(jnp.bfloat16)
    out_weights = jnp.einsum(
        "tp,t->p", to_bucket, sizes.astype(jnp.bfloat16), preferred_element_type=jnp.float32
    ).astype(jnp.bfloat16)
    received, in_weights = (
        lax.all_to_all(
            outgoing.reshape(shards, slots, -1), "ctx", split_axis=0, concat_axis=0, tiled=True
        ),
        lax.all_to_all(
            out_weights.reshape(shards, slots), "ctx", split_axis=0, concat_axis=0, tiled=True
        ),
    )
    targets = slot_map[0].reshape(places)
    landing = targets[None, :] == jnp.arange(merged_rows, dtype=jnp.int32)[:, None]
    weighted = jnp.where(landing, in_weights.reshape(places)[None, :], 0)
    merged_sum = jnp.dot(weighted, received.reshape(places, -1), preferred_element_type=jnp.float32)
    counts = jnp.sum(weighted.astype(jnp.float32), axis=1)
    merged = (merged_sum / jnp.maximum(counts, 1.0)[:, None]).astype(jnp.bfloat16)
    key_bias = jnp.where(counts > 0, jnp.log(jnp.maximum(counts, 1.0)), -1e30).astype(jnp.bfloat16)
    queries = jnp.dot(merged, w_query, preferred_element_type=jnp.float32).astype(jnp.bfloat16)
    query_heads = queries.reshape(merged_rows, HEADS, HEAD)
    inverse = 1.0 / math.sqrt(HEAD)

    def attend_block(carry, item):
        row_max, total, accum = carry
        key_heads, value_heads, bias = item
        scores = (
            jnp.einsum("qhd,khd->hqk", query_heads, key_heads, preferred_element_type=jnp.float32)
            * inverse
        )
        scores = scores + bias.astype(jnp.float32)[None, None, :]
        new_max = jnp.maximum(row_max, jnp.max(scores, axis=2))
        factor = jnp.exp(row_max - new_max)
        expo = jnp.exp(scores - new_max[:, :, None])
        total = total * factor + jnp.sum(expo, axis=2)
        accum = accum * factor[:, :, None] + jnp.einsum(
            "hqk,khd->hqd",
            expo.astype(jnp.bfloat16),
            value_heads,
            preferred_element_type=jnp.float32,
        )
        return ((new_max, total, accum), None)

    start_state = (
        jnp.full((HEADS, merged_rows), -jnp.inf, jnp.float32),
        jnp.zeros((HEADS, merged_rows), jnp.float32),
        jnp.zeros((HEADS, merged_rows, HEAD), jnp.float32),
    )
    own_keys = jnp.dot(merged, w_key, preferred_element_type=jnp.float32).astype(jnp.bfloat16)
    own_values = jnp.dot(merged, w_value, preferred_element_type=jnp.float32).astype(jnp.bfloat16)
    carry = start_state
    keys = lax.all_gather(own_keys, "ctx", axis=0, tiled=True)
    values = lax.all_gather(own_values, "ctx", axis=0, tiled=True)
    bias = lax.all_gather(key_bias, "ctx", axis=0, tiled=True)
    length = keys.shape[0]
    block = math.gcd(length, 1536)
    turns = length // block
    items = (
        keys.reshape(turns, block, HEADS, HEAD),
        values.reshape(turns, block, HEADS, HEAD),
        bias.reshape(turns, block),
    )
    carry, unused = lax.scan(attend_block, carry, items)
    row_max, total, accum = carry
    attended = (
        jnp.transpose(accum / total[:, :, None], (1, 0, 2))
        .reshape(merged_rows, HEADS * HEAD)
        .astype(jnp.bfloat16)
    )
    landing_rows = landing.astype(jnp.bfloat16)
    leaving = jnp.einsum(
        "mp,md->pd", landing_rows, attended, preferred_element_type=jnp.float32
    ).astype(jnp.bfloat16)
    returned = lax.all_to_all(
        leaving.reshape(shards, slots, -1), "ctx", split_axis=0, concat_axis=0, tiled=True
    )
    picked = jnp.einsum(
        "tp,pd->td", to_bucket, returned.reshape(places, -1), preferred_element_type=jnp.float32
    ).astype(jnp.bfloat16)
    mixed = jnp.dot(picked, w_out, preferred_element_type=jnp.float32).astype(jnp.bfloat16)
    return mixed


def solution(mesh):
    in_specs = (
        P(("groups", "ctx"), None),
        P(("groups", "ctx"), None),
        P(("groups", "ctx"), None, None),
        P(("groups", "ctx")),
        P(),
        P(),
        P(),
        P(),
    )
    out_specs = P(("groups", "ctx"), None)
    return jax.shard_map(
        on_device, mesh=mesh, in_specs=in_specs, out_specs=out_specs, check_vma=False
    )
```

profile of v0, /device:TPU:0, one launch (start us, length us, event | category | flops | bytes accessed | tf_op | source)
XLA Modules:
  0.0 126.5 jit_solution(1130961317788527914)
XLA Ops:
  0.0 0.0 copy-start
  0.0 0.8 fusion.16
  0.8 0.1 reduce_window_sum.11
  1.0 0.8 select_reduce_fusion
  1.8 0.7 fusion.23
  2.5 0.8 fusion.10
  3.3 0.7 all_to_all.16
  4.1 7.4 %all-to-all-start = ((bf16[16,1,12]{2,1,0:T(2,128)(2,1)}), bf16[16,1,12]{2,1,0:T(2,128)(2,1)S(1)}, u32[]{:S(2)}, u32[]{:S(2)}) async-start(bf16[16,1,12]{2,1,0:T(2,128)(2,1)} %all_to_all.16), calls=%async_computation | async-start | bytes 16384 | tf_op jit(solution)/shard_map/all_to_all | solution.py:35
  11.5 0.0 copy-start.3
  11.5 0.0 copy-start.4
  11.5 1.3 %convolution_convert_fusion = bf16[192,1152]{1,0:T(8,128)(2,1)S(1)} fusion(bf16[96,1152]{1,0:T(8,128)(2,1)} %param.8, s32[96]{0:T(128)S(1)} %fusion.23), kind=kOutput, calls=%fused_computation | convolution fusion | flops 42706944 | bytes 663936 | tf_op jit(solution)/shard_map/tp,td->pd/dot_general | solution.py:25
  12.8 0.9 reshape.49
  13.7 4.1 %all-to-all-done = bf16[16,1,12]{2,1,0:T(2,128)(2,1)S(1)} async-done(((bf16[16,1,12]{2,1,0:T(2,128)(2,1)}), bf16[16,1,12]{2,1,0:T(2,128)(2,1)S(1)}, u32[]{:S(2)}, u32[]{:S(2)}) %all-to-all-start) | async-done | bytes 416 | tf_op jit(solution)/shard_map/all_to_all | solution.py:35
  17.8 3.6 %all-to-all-start.1 = ((bf16[16,12,1152]{2,1,0:T(8,128)(2,1)}), bf16[16,12,1152]{2,1,0:T(8,128)(2,1)S(1)}, u32[]{:S(2)}, u32[]{:S(2)}) async-start(bf16[16,12,1152]{2,1,0:T(8,128)(2,1)} %reshape.49), calls=%async_computation.1 | async-start | bytes 1179648 | tf_op jit(solution)/shard_map/all_to_all | solution.py:32
  21.4 0.0 copy-start.1
  21.4 0.0 copy-done.3
  21.4 0.1 copy.23
  21.5 0.1 eq.53
  21.6 0.0 copy-done.4
  21.6 0.6 dynamic-slice.1
  22.9 0.1 broadcast_in_dim.39
  23.0 0.1 convert_reduce_fusion
  23.1 0.2 dynamic-update-slice
  23.3 35.8 %all-reduce = bf16[768]{0:T(1024)(128)(2,1)S(1)} all-reduce(bf16[768]{0:T(1024)(128)(2,1)S(1)} %dynamic-update-slice), channel_id=1, replica_groups=mesh['groups'=2,'ctx'=16] {'ctx'}, use_global_device_ids=true, to_apply=%add | all-reduce | flops 768 | bytes 3072
  59.1 0.0 all-to-all-done.1
  59.1 0.9 reshape.50
  60.0 1.2 fusion
  61.2 0.0 copy-done.1
  61.2 0.5 convolution_convert_fusion.4
  61.7 20.4 %all_gather.11 = bf16[768,576]{1,0:T(8,128)(2,1)S(1)} all-gather(bf16[48,576]{1,0:T(8,128)(2,1)S(1)} %convolution_convert_fusion.4), channel_id=1, replica_groups=mesh['groups'=2,'ctx'=16] {'ctx'}, dimensions={0}, use_global_device_ids=true | all-gather | bytes 940032 | tf_op jit(solution)/shard_map/all_gather | solution.py:79
  82.1 1.3 %copy.27 = bf16[768,576]{0,1:T(8,128)(2,1)} copy(bf16[768,576]{1,0:T(8,128)(2,1)S(1)} %all_gather.11) | data formatting | bytes 1769472 | tf_op jit(solution)/shard_map/all_gather | solution.py:79
  83.4 1.8 %convolution_convert_fusion.5 = bf16[48,576]{1,0:T(8,128)(2,1)S(1)} fusion(bf16[48,1152]{1,0:T(8,128)(2,1)S(1)} %fusion, bf16[1152,576]{0,1:T(8,128)(2,1)} %param.13), kind=kOutput, calls=%fused_computation.14 | convolution fusion | flops 63728640 | bytes 1492992 | tf_op jit(solution)/shard_map/dot_general | solution.py:75
  85.2 21.6 %all_gather.9 = bf16[768,576]{1,0:T(8,128)(2,1)S(1)} all-gather(bf16[48,576]{1,0:T(8,128)(2,1)S(1)} %convolution_convert_fusion.5), channel_id=1, replica_groups=mesh['groups'=2,'ctx'=16] {'ctx'}, dimensions={0}, use_global_device_ids=true | all-gather | bytes 940032 | tf_op jit(solution)/shard_map/all_gather | solution.py:78
  106.8 0.6 copy.25
  107.4 1.8 %convolution_convert_fusion.6 = bf16[48,576]{1,0:T(8,128)(2,1)S(1)} fusion(bf16[48,1152]{1,0:T(8,128)(2,1)S(1)} %fusion, bf16[1152,576]{0,1:T(8,128)(2,1)} %param.12), kind=kOutput, calls=%fused_computation.15 | convolution fusion | flops 63728640 | bytes 1492992 | tf_op jit(solution)/shard_map/dot_general | solution.py:46
  109.2 0.1 reshape.51
  109.3 0.0 copy-start.2
  109.3 0.4 fusion.25
  109.7 0.4 fusion.5
  110.1 0.4 copy-done.2
  110.5 0.4 fusion.4
  111.0 0.1 convert_element_type.72
  111.1 0.3 convolution_convert_fusion.2
  111.4 0.1 reshape.52
  111.5 13.7 %all_to_all.20 = bf16[16,12,576]{2,1,0:T(8,128)(2,1)S(1)} all-to-all(bf16[16,12,576]{2,1,0:T(8,128)(2,1)S(1)} %reshape.52), channel_id=1, replica_groups=mesh['groups'=2,'ctx'=16] {'ctx'}, dimensions={0} | all-to-all | bytes 442368 | tf_op jit(solution)/shard_map/all_to_all | solution.py:100
  125.2 0.1 reshape.53
  125.3 0.0 copy-done
  125.3 1.2 convolution_convert_fusion.1
  (8 shorter events, 0.1 us)
Async XLA Ops:
  0.0 125.3 %copy-start = (bf16[576,1152]{1,0:T(8,128)(2,1)S(1)}, bf16[576,1152]{1,0:T(8,128)(2,1)}, u32[]{:S(2)}) copy-start(bf16[576,1152]{1,0:T(8,128)(2,1)} %param.15) | copy-start | bytes 3981316
  4.1 13.7 %all-to-all-start = ((bf16[16,1,12]{2,1,0:T(2,128)(2,1)}), bf16[16,1,12]{2,1,0:T(2,128)(2,1)S(1)}, u32[]{:S(2)}, u32[]{:S(2)}) async-start(bf16[16,1,12]{2,1,0:T(2,128)(2,1)} %all_to_all.16), calls=%async_computation | async-start | bytes 16384 | tf_op jit(solution)/shard_map/all_to_all | solution.py:35
  11.5 9.9 %copy-start.3 = (s32[1,16,12]{1,0,2:T(1,128)S(1)}, s32[1,16,12]{1,0,2:T(1,128)}, u32[]{:S(2)}) copy-start(s32[1,16,12]{1,0,2:T(1,128)} %param.10) | copy-start | bytes 2308
  11.5 10.1 %copy-start.4 = (u32[32]{0:T(128)S(1)}, u32[32]{0:T(128)}, u32[]{:S(2)}) copy-start(u32[32]{0:T(128)} %constant.40) | copy-start | bytes 388
  17.8 41.4 %all-to-all-start.1 = ((bf16[16,12,1152]{2,1,0:T(8,128)(2,1)}), bf16[16,12,1152]{2,1,0:T(8,128)(2,1)S(1)}, u32[]{:S(2)}, u32[]{:S(2)}) async-start(bf16[16,12,1152]{2,1,0:T(8,128)(2,1)} %reshape.49), calls=%async_computation.1 | async-start | bytes 1179648 | tf_op jit(solution)/shard_map/all_to_all | solution.py:32
  21.4 39.9 %copy-start.1 = (bf16[1152,576]{0,1:T(8,128)(2,1)S(1)}, bf16[1152,576]{0,1:T(8,128)(2,1)}, u32[]{:S(2)}) copy-start(bf16[1152,576]{0,1:T(8,128)(2,1)} %param.14) | copy-start | bytes 3981316
  109.3 1.2 copy-start.2
where the time goes:
time: 127 us
  blocking collectives  91.5 us (72%)
  starting transfers between devices  11 us (9%)
  matrix products  9.81 us (8%)
  local copies, waits for them, and re-layouts  6.33 us (5%)
  waiting for transfers between devices  4.06 us (3%)
  other arithmetic  3.01 us (2%)
    unnamed x1, blocking collectives  35.8 us
    all_gather x1, blocking collectives, on_device(): keys = lax.all_gather(own_keys, 'ctx', axis=0, tiled=True)  21.6 us
    all_gather x1, blocking collectives, on_device(): values = lax.all_gather(own_values, 'ctx', axis=0, tiled=True)  20.4 us
    all_to_all x1, blocking collectives, on_device(): lax.all_to_all(leaving.reshape(shards, slots, -1), 'ctx', split_axis=0, c...  13.7 us
    all_to_all x1, starting transfers between devices, on_device(): lax.all_to_all(out_weights.reshape(shards, slots), 'ctx', split_axis=0, c...  7.39 us
    all_to_all x1, waiting for transfers between devices, on_device(): lax.all_to_all(out_weights.reshape(shards, slots), 'ctx', split_axis=0, c...  4.06 us
    all_to_all x1, starting transfers between devices, on_device(): lax.all_to_all(outgoing.reshape(shards, slots, -1), 'ctx', split_axis=0,...  3.58 us
  transfers between devices with their start and end apart: 2, of which 1 were waited for; matrix products, arithmetic and copies ran while one was open for 3% of the time, Pallas kernels for 0%

commit v1 on v0

--- a/solution.py
+++ b/solution.py
@@ -1,23 +1,244 @@
+import functools
 import math
 
 import jax
 import jax.numpy as jnp
 from jax import lax
+from jax.experimental import pallas as pl
+from jax.experimental.pallas import tpu as pltpu
 from jax.sharding import PartitionSpec as P
 
 HEADS = 8
 HEAD = 72
-
-
-def on_device(tokens, owner, slot_map, sizes, w_query, w_key, w_value, w_out):
+META = 16
+LANES = 128
+GATHERED_MAX = 8 << 20
+VMEM_PREP = 16 << 20
+VMEM_TAIL = 44 << 20
+F32 = jnp.float32
+BF16 = jnp.bfloat16
+NT = (((1,), (1,)), ((), ()))
+TN = (((0,), (0,)), ((), ()))
+NN = (((1,), (0,)), ((), ()))
+
+
+def dot(a, b, dims=NN):
+    return lax.dot_general(a, b, dims, preferred_element_type=F32)
+
+
+def ring_index(k, core, rows):
+    k = k % (2 * rows)
+    row, column = (k, 0) if k < rows else (2 * rows - 1 - k, 1)
+    return row * 4 + column * 2 + core
+
+
+def ring_moves(shards):
+    rows = shards // 4
+    moves = []
+    for k in range(2 * rows):
+        for core, step in ((0, 1), (1, -1)):
+            moves.append((ring_index(k, core, rows), ring_index(k + step, core, rows)))
+    return moves
+
+
+def sender_table(shards):
+    rows = shards // 4
+    position = {ring_index(k, c, rows): (k, c) for k in range(2 * rows) for c in (0, 1)}
+    table = []
+    for me in range(shards):
+        k, c = position[me]
+        d = -1 if c == 0 else 1
+        row = [me, me ^ 1]
+        for s in range(1, rows):
+            row += [
+                ring_index(k + d * s, c, rows),
+                ring_index(k + d * s, c ^ 1, rows),
+                ring_index(k - d * s, c ^ 1, rows),
+                ring_index(k - d * s, c, rows),
+            ]
+        row += [ring_index(k + d * rows, c, rows), ring_index(k - d * rows, c ^ 1, rows)]
+        table.append(row)
+    return table
+
+
+def meta_kernel(slots, owner_col_ref, owner_row_ref, sizes_ref, map_ref, out_ref):
+    tok = owner_row_ref.shape[1]
+    row = owner_row_ref[...]
+    earlier = lax.broadcasted_iota(jnp.int32, (tok, tok), 0) < lax.broadcasted_iota(
+        jnp.int32, (tok, tok), 1
+    )
+    same = jnp.where(owner_col_ref[...] == row, 1, 0)
+    rank = jnp.sum(jnp.where(earlier, same, 0), axis=0, keepdims=True)
+    sub = lax.broadcasted_iota(jnp.int32, (META, LANES), 0)
+
+    def wide(x, rows):
+        x = x.astype(F32)
+        x = jnp.concatenate([x, jnp.zeros((x.shape[0], LANES - x.shape[1]), F32)], axis=1)
+        if x.shape[0] == 1:
+            return jnp.broadcast_to(x, (META, LANES))
+        return jnp.concatenate([x, jnp.zeros((META - rows, LANES), F32)], axis=0)
+
+    out = wide(map_ref[...], slots)
+    out = jnp.where(sub == slots, wide(row, 1), out)
+    out = jnp.where(sub == slots + 1, wide(rank, 1), out)
+    out = jnp.where(sub == slots + 2, wide(sizes_ref[...], 1), out)
+    out_ref[...] = out.astype(BF16)
+
+
+def prep_kernel(
+    shards, slots, tok, merged_rows, me_ref, table_ref, g_ref,
+    m_ref, inv_ref, bias_ref, pick_ref, gf, dest_row, size_row,
+):
+    me = me_ref[0]
+    total = merged_rows * shards
+    gf[...] = g_ref[...].astype(F32)
+    by_sender = jnp.transpose(gf[...], (1, 0))[:shards].astype(BF16)
+    places = shards * META
+    bucket = lax.broadcasted_iota(jnp.int32, (places, LANES), 0)
+    sender_iota = lax.broadcasted_iota(jnp.int32, (shards, LANES), 0)
+    for j in range(shards):
+        e = table_ref[j]
+        base = (e ^ me) * META
+        own = gf[pl.ds(base + slots, 1), :].astype(jnp.int32)
+        rank = gf[pl.ds(base + slots + 1, 1), :].astype(jnp.int32)
+        size = gf[pl.ds(base + slots + 2, 1), :]
+        hot = jnp.where(bucket == (own ^ me) * META + rank, 1.0, 0.0).astype(BF16)
+        found = dot(by_sender, hot)
+        slot = jnp.sum(jnp.where(sender_iota == e, found, 0.0), axis=0, keepdims=True)
+        dest = own.astype(F32) * merged_rows + slot
+        dest_row[:, j * tok : (j + 1) * tok] = dest[:, :tok]
+        size_row[:, j * tok : (j + 1) * tok] = size[:, :tok]
+    places_iota = lax.broadcasted_iota(jnp.int32, (total, LANES), 0).astype(F32)
+    count = jnp.zeros((total, LANES), F32)
+    for b in range(shards * tok // LANES):
+        cols = slice(b * LANES, (b + 1) * LANES)
+        piece = jnp.where(places_iota == dest_row[:, cols], size_row[:, cols], 0.0)
+        count = count + piece
+        m_ref[:, cols] = piece.astype(BF16)
+    inv_ref[...] = 1.0 / jnp.maximum(jnp.sum(count, axis=1, keepdims=True), 1.0)
+    count_row = dot(jnp.ones((8, LANES), BF16), count.astype(BF16), NT)[0:1]
+    bias = jnp.where(count_row > 0, jnp.log(jnp.maximum(count_row, 1.0)), -1e30)
+    bias_ref[...] = bias.astype(BF16).astype(F32)
+    mine = jnp.broadcast_to(dest_row[:, :LANES], (8, LANES))
+    mine = jnp.transpose(mine, (1, 0))[:tok, 0:1]
+    lane = lax.broadcasted_iota(jnp.int32, (tok, total), 1).astype(F32)
+    pick_ref[...] = jnp.where(lane == mine, 1.0, 0.0).astype(BF16)
+
+
+def tail_kernel(n_blocks, *refs):
+    blocks = refs[:n_blocks]
+    (m_ref, inv_ref, bias_ref, pick_ref, wq_ref, wk_ref, wv_ref, wo_ref, out_ref,
+     tok_s, merged_s, att_s) = refs[n_blocks:]
+    tok = blocks[0].shape[0]
+    for j in range(n_blocks):
+        tok_s[j * tok : (j + 1) * tok, :] = blocks[j][...]
+    total = m_ref.shape[0]
+    tile = 256
+
+    def merge(i, _):
+        rows = pl.ds(pl.multiple_of(i * tile, tile), tile)
+        acc = dot(m_ref[rows, :], tok_s[...])
+        merged_s[rows, :] = (acc * inv_ref[rows, :]).astype(BF16)
+        return 0
+
+    lax.fori_loop(0, total // tile, merge, 0)
+    merged = merged_s[...]
+    picked = dot(pick_ref[...], merged).astype(BF16)
+    q_t = dot(wq_ref[...], picked, NT).astype(BF16)
+    inverse = 1.0 / math.sqrt(HEAD)
+    bias = bias_ref[...]
+    k_t = dot(wk_ref[...], merged, NT)
+    v_t = dot(wv_ref[...], merged, NT)
+    for h in range(HEADS):
+        rows = slice(h * HEAD, (h + 1) * HEAD)
+        q_h = q_t[rows].astype(BF16)
+        scores = dot(q_h, k_t[rows].astype(BF16), TN) * inverse + bias
+        top = jnp.max(scores, axis=1, keepdims=True)
+        expo = jnp.exp(scores - top)
+        whole = jnp.sum(expo, axis=1, keepdims=True)
+        att = dot(expo.astype(BF16), v_t[rows].astype(BF16), NT) / whole
+        att_s[:, rows] = att
+    out_ref[...] = dot(att_s[...].astype(BF16), wo_ref[...]).astype(BF16)
+
+
+def on_device_gathered(tokens, owner, slot_map, sizes, w_query, w_key, w_value, w_out):
+    tok, width = tokens.shape
+    shards = lax.axis_size("ctx")
+    slots = slot_map.shape[2]
+    merged_rows = tok // 2
+    total = merged_rows * shards
+    vmem = pl.BlockSpec(memory_space=pltpu.VMEM)
+    smem = pl.BlockSpec(memory_space=pltpu.SMEM)
+    me = lax.axis_index("ctx")
+    moves = ring_moves(shards)
+    swap = [(i, i ^ 1) for i in range(shards)]
+
+    def send(x, pairs):
+        return lax.ppermute(x, "ctx", pairs)
+
+    meta = pl.pallas_call(
+        functools.partial(meta_kernel, slots),
+        out_shape=jax.ShapeDtypeStruct((META, LANES), BF16),
+        in_specs=[vmem] * 4,
+        out_specs=vmem,
+    )(owner, owner.reshape(1, tok), sizes.reshape(1, tok), jnp.transpose(slot_map[0], (1, 0)))
+    bit = 1
+    while bit < shards:
+        meta = jnp.concatenate([meta, send(meta, [(i, i ^ bit) for i in range(shards)])], axis=0)
+        bit *= 2
+
+    other = send(tokens, swap)
+    a, b = tokens, other
+    blocks = [tokens, other]
+    for s in range(1, shards // 4):
+        a = send(a, moves)
+        b = send(b, moves)
+        blocks += [a, b, send(a, swap), send(b, swap)]
+    a = send(a, moves)
+    blocks += [a, send(a, swap)]
+
+    table = jnp.array(sender_table(shards), jnp.int32)[me]
+    m, inv, bias, pick = pl.pallas_call(
+        functools.partial(prep_kernel, shards, slots, tok, merged_rows),
+        out_shape=(
+            jax.ShapeDtypeStruct((total, shards * tok), BF16),
+            jax.ShapeDtypeStruct((total, 1), F32),
+            jax.ShapeDtypeStruct((1, total), F32),
+            jax.ShapeDtypeStruct((tok, total), BF16),
+        ),
+        in_specs=[smem, smem, vmem],
+        out_specs=(vmem,) * 4,
+        scratch_shapes=[
+            pltpu.VMEM((shards * META, LANES), F32),
+            pltpu.VMEM((1, shards * tok), F32),
+            pltpu.VMEM((1, shards * tok), F32),
+        ],
+        compiler_params=pltpu.CompilerParams(vmem_limit_bytes=VMEM_PREP),
+    )(me.reshape(1), table, meta)
+    return pl.pallas_call(
+        functools.partial(tail_kernel, len(blocks)),
+        out_shape=jax.ShapeDtypeStruct((tok, width), BF16),
+        in_specs=[vmem] * (len(blocks) + 8),
+        out_specs=vmem,
+        scratch_shapes=[
+            pltpu.VMEM((shards * tok, width), BF16),
+            pltpu.VMEM((total, width), BF16),
+            pltpu.VMEM((tok, HEADS * HEAD), F32),
+        ],
+        compiler_params=pltpu.CompilerParams(vmem_limit_bytes=VMEM_TAIL),
+    )(*blocks, m, inv, bias, pick, w_query.T, w_key.T, w_value.T, w_out)
+
+
+def on_device_exchanged(tokens, owner, slot_map, sizes, w_query, w_key, w_value, w_out):
     tok_rows = tokens.shape[0]
     shards = lax.axis_size("ctx")
     slots = slot_map.shape[2]
     places = shards * slots
     merged_rows = tok_rows // 2
     owners = owner[:, 0]
-    marks = (owners[:, None] == jnp.arange(shards, dtype=jnp.int32)[None, :]).astype(jnp.int32)
-    ranking = jnp.sum((jnp.cumsum(marks, axis=0) - marks) * marks, axis=1)
+    order = jnp.arange(tok_rows)
+    earlier = order[None, :] < order[:, None]
+    ranking = jnp.sum(jnp.where(earlier & (owners[:, None] == owners[None, :]), 1, 0), axis=1)
     bucket = owners * slots + ranking
     to_bucket = (bucket[:, None] == jnp.arange(places, dtype=jnp.int32)[None, :]).astype(
         jnp.bfloat16
@@ -107,6 +328,16 @@
     return mixed
 
 
+def on_device(tokens, owner, slot_map, *weights):
+    tok, width = tokens.shape
+    shards = lax.axis_size("ctx")
+    fits = shards * tok * width * tokens.dtype.itemsize <= GATHERED_MAX
+    paired = shards >= 8 and shards & (shards - 1) == 0 and shards <= LANES
+    shaped = slot_map.shape[2] + 3 <= META and tok <= LANES and (shards * tok) % LANES == 0
+    plan = on_device_gathered if fits and paired and shaped else on_device_exchanged
+    return plan(tokens, owner, slot_map, *weights)
+
+
 def solution(mesh):
     in_specs = (
         P(("groups", "ctx"), None),

time: 127 us -> 52.2 us (0.41)
  blocking collectives: 91.5 us -> 0 us
  Pallas kernels: 0 us -> 14.6 us
  matrix products: 9.81 us -> 0 us
  starting transfers between devices: 11 us -> 17.5 us
  local copies, waits for them, and re-layouts: 6.33 us -> 11.7 us
  waiting for transfers between devices: 4.06 us -> 5.7 us
    all_gather x2 -> x0, blocking collectives: 42 us -> none  [the longest x1 21.6 us: on_device(): keys = lax.all_gather(own_keys, 'ctx', axis=0, tiled=True)]
    unnamed x1 -> x0, blocking collectives: 35.8 us -> none
    ppermute x0 -> x19, starting transfers between devices: none -> 17.5 us  [send(): return lax.ppermute(x, 'ctx', pairs)]
    pallas_call x0 -> x3, Pallas kernels: none -> 14.6 us  [the longest x1 11.4 us: on_device_gathered(): pl.pallas_call(functools.partial(tail_kernel, len(blocks)), out_shape=jax...]
    all_to_all x1 -> x0, blocking collectives: 13.7 us -> none  [on_device(): lax.all_to_all(leaving.reshape(shards, slots, -1), 'ctx', split_axis=0, c...]
    all_to_all x2 -> x0, starting transfers between devices: 11 us -> none  [the longest x1 7.39 us: on_device(): lax.all_to_all(out_weights.reshape(shards, slots), 'ctx', split_axis=0, c...]
    dot_general x10 -> x0, matrix products: 9.81 us -> none  [the longest x1 1.8 us: on_device(): jnp.dot(merged, w_query, preferred_element_type=jnp.float32)]
    unnamed x14 -> x18, local copies, waits for them, and re-layouts: 1.32 us -> 11 us
  transfers between devices with their start and end apart: 2 -> 19, of which waited for: 1 -> 4; matrix products, arithmetic and copies ran while one was open for 3% -> 12% of each run, Pallas kernels for 0% -> 6%
where the time goes in v1:
time: 52.2 us; the launch traced here: 51.6 us
  starting transfers between devices  17.5 us (34%)
  Pallas kernels  14.6 us (28%)
  local copies, waits for them, and re-layouts  11.7 us (22%)
  waiting for transfers between devices  5.7 us (11%)
  other arithmetic  2.06 us (4%)
    ppermute x19, starting transfers between devices, send(): return lax.ppermute(x, 'ctx', pairs)  17.5 us
    pallas_call x1, Pallas kernels, on_device_gathered(): pl.pallas_call(functools.partial(tail_kernel, len(blocks)), out_shape=jax...  11.4 us
    unnamed x18, local copies, waits for them, and re-layouts  11 us
    ppermute x19, waiting for transfers between devices, send(): return lax.ppermute(x, 'ctx', pairs)  5.7 us
    concatenate x3, other arithmetic, on_device_gathered(): jnp.concatenate([meta, send(meta, [(i, i ^ bit) for i in range(shards)])]...  2.06 us
    pallas_call x1, Pallas kernels, on_device_gathered(): pl.pallas_call(functools.partial(prep_kernel, shards, slots, tok, merged_...  1.67 us
    pallas_call x1, Pallas kernels, on_device_gathered(): pl.pallas_call(functools.partial(meta_kernel, slots), out_shape=jax.Shape...  1.51 us
  transfers between devices with their start and end apart: 19, of which 4 were waited for; matrix products, arithmetic and copies ran while one was open for 12% of the time, Pallas kernels for 6%

profile of v1, /device:TPU:0, one launch (start us, length us, event | category | flops | bytes accessed | tf_op | source)
XLA Modules:
  0.0 51.6 jit_solution(16898163683890267481)
XLA Ops:
  0.0 0.5 collective-permute-start
  0.5 2.6 %collective-permute-start.1 = (bf16[96,1152]{1,0:T(8,128)(2,1)}, bf16[96,1152]{1,0:T(8,128)(2,1)S(1)}, u32[]{:S(2)}, u32[]{:S(2)}) collective-permute-start(bf16[96,1152]{1,0:T(8,128)(2,1)} %refs_0_.1), channel_id=1, source_target_pairs={{0,4},{1,3},{4,8},{5,1},{8,12},{9,5},{12,14},{13,9},{14,10},{15,13... | collective-permute-start | bytes 663560 | tf_op jit(solution)/shard_map/ppermute | solution.py:177
  3.0 1.3 %copy.13 = s32[1,16,12]{1,2,0:T(8,128)} copy(s32[1,16,12]{1,0,2:T(1,128)} %param.11) | data formatting | bytes 1536
  4.3 1.4 %copy.10.owner_col_ref = s32[96,1]{1,0:T(8,128)} copy(s32[96,1]{0,1:T(1,128)} %param.10) | data formatting | bytes 768 | tf_op args[1]
  5.7 1.5 %shard_map.91 = bf16[16,128]{1,0:T(8,128)(2,1)} custom-call(s32[96,1]{1,0:T(8,128)} %copy.10.owner_col_ref, s32[1,96]{1,0:T(1,128)} %bitcast.17, s32[1,96]{1,0:T(1,128)} %bitcast.18, s32[12,16]{1,0:T(8,128)} %bitcast.16), custom_call_target="tpu_custom_call" | custom-call | tf_op jit(solution)/shard_map/pallas_call | solution.py:179
  7.2 0.2 collective-permute-start.15
  7.4 0.7 %constant_dynamic-update-slice_fusion.4 = bf16[256,128]{1,0:T(8,128)(2,1)S(1)} fusion(bf16[16,128]{1,0:T(8,128)(2,1)} %shard_map.91), kind=kLoop, calls=%fused_computation.6 | loop fusion | bytes 8192
  8.1 0.0 collective-permute-done.refs_1_
  8.1 1.4 %collective-permute-start.2 = (bf16[96,1152]{1,0:T(8,128)(2,1)S(1)}, bf16[96,1152]{1,0:T(8,128)(2,1)S(1)}, u32[]{:S(2)}, u32[]{:S(2)}) collective-permute-start(bf16[96,1152]{1,0:T(8,128)(2,1)S(1)} %collective-permute-done.refs_1_), channel_id=1, source_target_pairs={{0,4},{1,3},{4,8},{5,1},{8,12},{9,5},{12,14},{13,9},{14,10},{15,13... | collective-permute-start | bytes 663560 | tf_op jit(solution)/shard_map/ppermute | solution.py:177
  9.5 0.0 collective-permute-done.1.refs_2_
  9.5 1.6 %collective-permute-start.5 = (bf16[96,1152]{1,0:T(8,128)(2,1)S(1)}, bf16[96,1152]{1,0:T(8,128)(2,1)S(1)}, u32[]{:S(2)}, u32[]{:S(2)}) collective-permute-start(bf16[96,1152]{1,0:T(8,128)(2,1)S(1)} %collective-permute-done.1.refs_2_), channel_id=1, source_target_pairs={{0,4},{1,3},{4,8},{5,1},{8,12},{9,5},{12,14},{13,9},{14,10},{15,13... | collective-permute-start | bytes 663560 | tf_op jit(solution)/shard_map/ppermute | solution.py:177
  11.1 0.0 collective-permute-done.15
  11.1 0.7 %pad_maximum_fusion.2 = bf16[32,128]{1,0:T(8,128)(2,1)S(1)} fusion(bf16[16,128]{1,0:T(8,128)(2,1)S(1)} %collective-permute-done.15, bf16[16,128]{1,0:T(8,128)(2,1)} %shard_map.91), kind=kLoop, calls=%fused_computation.7 | loop fusion | flops 16384 | bytes 16384 | tf_op jit(solution)/shard_map/concatenate | solution.py:187
  11.7 0.4 collective-permute-start.16
  12.2 0.7 %dynamic-slice_bitcast_fusion.table_ref = s32[16]{0:T(128)S(1)} fusion(s32[16,16]{1,0:T(8,128)} %constant.10.clone, s32[]{:T(128)S(6)} %select_n.3), kind=kLoop, calls=%fused_computation.9 | loop fusion | bytes 132 | tf_op jit(solution)/shard_map/squeeze | solution.py:200
  12.9 1.1 %collective-permute-done.2.refs_3_ = bf16[96,1152]{1,0:T(8,128)(2,1)S(1)} collective-permute-done((bf16[96,1152]{1,0:T(8,128)(2,1)S(1)}, bf16[96,1152]{1,0:T(8,128)(2,1)S(1)}, u32[]{:S(2)}, u32[]{:S(2)}) %collective-permute-start.2) | collective-permute-done | bytes 221216 | tf_op jit(solution)/shard_map/ppermute | solution.py:177
  14.0 1.4 %collective-permute-start.6 = (bf16[96,1152]{1,0:T(8,128)(2,1)S(1)}, bf16[96,1152]{1,0:T(8,128)(2,1)S(1)}, u32[]{:S(2)}, u32[]{:S(2)}) collective-permute-start(bf16[96,1152]{1,0:T(8,128)(2,1)S(1)} %collective-permute-done.2.refs_3_), channel_id=1, source_target_pairs={{0,4},{1,3},{4,8},{5,1},{8,12},{9,5},{12,14},{13,9},{14,10},{15,13... | collective-permute-start | bytes 663560 | tf_op jit(solution)/shard_map/ppermute | solution.py:177
  15.4 1.0 %collective-permute-done.5.refs_6_ = bf16[96,1152]{1,0:T(8,128)(2,1)S(1)} collective-permute-done((bf16[96,1152]{1,0:T(8,128)(2,1)S(1)}, bf16[96,1152]{1,0:T(8,128)(2,1)S(1)}, u32[]{:S(2)}, u32[]{:S(2)}) %collective-permute-start.5) | collective-permute-done | bytes 221216 | tf_op jit(solution)/shard_map/ppermute | solution.py:177
  16.5 1.3 %collective-permute-start.9 = (bf16[96,1152]{1,0:T(8,128)(2,1)S(1)}, bf16[96,1152]{1,0:T(8,128)(2,1)S(1)}, u32[]{:S(2)}, u32[]{:S(2)}) collective-permute-start(bf16[96,1152]{1,0:T(8,128)(2,1)S(1)} %collective-permute-done.5.refs_6_), channel_id=1, source_target_pairs={{0,4},{1,3},{4,8},{5,1},{8,12},{9,5},{12,14},{13,9},{14,10},{15,13... | collective-permute-start | bytes 663560 | tf_op jit(solution)/shard_map/ppermute | solution.py:177
  17.8 0.0 collective-permute-done.16
  17.8 0.7 %pad_maximum_fusion.1 = bf16[64,128]{1,0:T(8,128)(2,1)S(1)} fusion(bf16[32,128]{1,0:T(8,128)(2,1)S(1)} %collective-permute-done.16, bf16[16,128]{1,0:T(8,128)(2,1)S(1)} %collective-permute-done.15, bf16[16,128]{1,0:T(8,128)(2,1)} %shard_map.91), kind=kLoop, calls=%fused_computation.1 | loop fusion | flops 49152 | bytes 32768 | tf_op jit(solution)/shard_map/concatenate | solution.py:187
  18.5 1.6 %collective-permute-start.17 = (bf16[64,128]{1,0:T(8,128)(2,1)S(1)}, bf16[64,128]{1,0:T(8,128)(2,1)S(1)}, u32[]{:S(2)}, u32[]{:S(2)}) collective-permute-start(bf16[64,128]{1,0:T(8,128)(2,1)S(1)} %pad_maximum_fusion.1), channel_id=1, source_target_pairs={{0,4},{1,5},{2,6},{3,7},{4,0},{5,1},{6,2},{7,3},{8,12},{9,13},{10,... | collective-permute-start | bytes 49160 | tf_op jit(solution)/shard_map/ppermute | solution.py:177
  20.1 0.5 collective-permute-start.4
  20.6 0.0 collective-permute-done.6.refs_7_
  20.6 0.9 %collective-permute-start.10 = (bf16[96,1152]{1,0:T(8,128)(2,1)S(1)}, bf16[96,1152]{1,0:T(8,128)(2,1)S(1)}, u32[]{:S(2)}, u32[]{:S(2)}) collective-permute-start(bf16[96,1152]{1,0:T(8,128)(2,1)S(1)} %collective-permute-done.6.refs_7_), channel_id=1, source_target_pairs={{0,4},{1,3},{4,8},{5,1},{8,12},{9,5},{12,14},{13,9},{14,10},{15,13... | collective-permute-start | bytes 663560 | tf_op jit(solution)/shard_map/ppermute | solution.py:177
  21.5 0.9 %collective-permute-done.9.refs_10_ = bf16[96,1152]{1,0:T(8,128)(2,1)S(1)} collective-permute-done((bf16[96,1152]{1,0:T(8,128)(2,1)S(1)}, bf16[96,1152]{1,0:T(8,128)(2,1)S(1)}, u32[]{:S(2)}, u32[]{:S(2)}) %collective-permute-start.9) | collective-permute-done | bytes 221216 | tf_op jit(solution)/shard_map/ppermute | solution.py:177
  22.4 1.5 %collective-permute-start.13 = (bf16[96,1152]{1,0:T(8,128)(2,1)S(1)}, bf16[96,1152]{1,0:T(8,128)(2,1)S(1)}, u32[]{:S(2)}, u32[]{:S(2)}) collective-permute-start(bf16[96,1152]{1,0:T(8,128)(2,1)S(1)} %collective-permute-done.9.refs_10_), channel_id=1, source_target_pairs={{0,4},{1,3},{4,8},{5,1},{8,12},{9,5},{12,14},{13,9},{14,10},{15,13... | collective-permute-start | bytes 663560 | tf_op jit(solution)/shard_map/ppermute | solution.py:177
  23.9 0.0 collective-permute-done.17
  23.9 0.7 %pad_maximum_fusion = bf16[128,128]{1,0:T(8,128)(2,1)S(1)} fusion(bf16[64,128]{1,0:T(8,128)(2,1)S(1)} %collective-permute-done.17, bf16[32,128]{1,0:T(8,128)(2,1)S(1)} %collective-permute-done.16, bf16[16,128]{1,0:T(8,128)(2,1)S(1)} %collective-permute-done.15, bf16[16,128]{1,0:T(8,128)(2,1)} %shard_map.91), kind=kLoop, calls=%fused_computation | loop fusion | flops 131072 | bytes 65536 | tf_op jit(solution)/shard_map/concatenate | solution.py:187
  24.6 2.5 %collective-permute-start.18 = (bf16[128,128]{1,0:T(8,128)(2,1)S(1)}, bf16[128,128]{1,0:T(8,128)(2,1)S(1)}, u32[]{:S(2)}, u32[]{:S(2)}) collective-permute-start(bf16[128,128]{1,0:T(8,128)(2,1)S(1)} %pad_maximum_fusion), channel_id=1, source_target_pairs={{0,8},{1,9},{2,10},{3,11},{4,12},{5,13},{6,14},{7,15},{8,0},{9,1},... | collective-permute-start | bytes 98312 | tf_op jit(solution)/shard_map/ppermute | solution.py:177
  27.1 2.6 %collective-permute-done.18 = bf16[128,128]{1,0:T(8,128)(2,1)S(1)} collective-permute-done((bf16[128,128]{1,0:T(8,128)(2,1)S(1)}, bf16[128,128]{1,0:T(8,128)(2,1)S(1)}, u32[]{:S(2)}, u32[]{:S(2)}) %collective-permute-start.18) | collective-permute-done | bytes 32800 | tf_op jit(solution)/shard_map/ppermute | solution.py:177
  29.7 0.5 collective-permute-start.8
  30.3 0.1 collective-permute-start.11
  30.3 0.4 collective-permute-start.12
  30.8 0.1 collective-permute-start.14
  30.9 1.7 %shard_map.92 = (bf16[768,1536]{1,0:T(8,128)(2,1)S(1)}, f32[768,1]{1,0:T(8,128)S(1)}, f32[1,768]{1,0:T(1,128)S(1)}, bf16[96,768]{1,0:T(8,128)(2,1)S(1)}) custom-call(s32[1]{0:T(128)} %bitcast.me_ref, s32[16]{0:T(128)S(1)} %dynamic-slice_bitcast_fusion.table_ref, bf16[256,128]{1,0:T(8,128)(2,1)S(1)} %constant_dynamic-update-slice_fusion.g_ref), custom_call_target="tpu_custom_call" | custom-call | tf_op jit(solution)/shard_map/pallas_call | solution.py:201
  32.6 1.4 %copy-done = bf16[768,1536]{1,0:T(8,128)(2,1)} copy-done((bf16[768,1536]{1,0:T(8,128)(2,1)}, bf16[768,1536]{1,0:T(8,128)(2,1)S(1)}, u32[]{:S(2)}) %copy-start) | copy-done | bytes 2359320
  34.0 0.0 collective-permute-done.7.refs_8_
  34.0 0.0 collective-permute-done.8.refs_9_
  34.0 0.0 collective-permute-done.11.refs_12_
  34.0 0.0 collective-permute-done.14.refs_15_
  34.0 0.0 copy-start.1
  34.0 1.3 %copy-done.1 = bf16[1152,576]{0,1:T(8,128)(2,1)S(1)} copy-done((bf16[1152,576]{0,1:T(8,128)(2,1)S(1)}, bf16[1152,576]{0,1:T(8,128)(2,1)}, u32[]{:S(2)}) %copy-start.1) | copy-done | bytes 1327128
  35.3 1.3 %copy-done.2 = bf16[1152,576]{0,1:T(8,128)(2,1)S(1)} copy-done((bf16[1152,576]{0,1:T(8,128)(2,1)S(1)}, bf16[1152,576]{0,1:T(8,128)(2,1)}, u32[]{:S(2)}) %copy-start.2) | copy-done | bytes 1327128
  36.7 1.3 %copy-done.3 = bf16[1152,576]{0,1:T(8,128)(2,1)S(1)} copy-done((bf16[1152,576]{0,1:T(8,128)(2,1)S(1)}, bf16[1152,576]{0,1:T(8,128)(2,1)}, u32[]{:S(2)}) %copy-start.3) | copy-done | bytes 1327128
  38.0 1.3 %copy-done.4 = bf16[576,1152]{1,0:T(8,128)(2,1)S(1)} copy-done((bf16[576,1152]{1,0:T(8,128)(2,1)S(1)}, bf16[576,1152]{1,0:T(8,128)(2,1)}, u32[]{:S(2)}) %copy-start.4) | copy-done | bytes 1327128
  39.3 0.9 %copy-done.5 = bf16[96,1152]{1,0:T(8,128)(2,1)S(1)} copy-done((bf16[96,1152]{1,0:T(8,128)(2,1)S(1)}, bf16[96,1152]{1,0:T(8,128)(2,1)}, u32[]{:S(2)}) %copy-start.5) | copy-done | bytes 221208
  40.2 11.4 %shard_map.93 = bf16[96,1152]{1,0:T(8,128)(2,1)} custom-call(bf16[96,1152]{1,0:T(8,128)(2,1)S(1)} %copy-done.5, bf16[96,1152]{1,0:T(8,128)(2,1)S(1)} %collective-permute-done.refs_1_, bf16[96,1152]{1,0:T(8,128)(2,1)S(1)} %collective-permute-done.1.refs_2_, bf16[96,1152]{1,0:T(8,128)(2,1)S(1)} %collective-permute-done.2.refs_3_, ...), custom_call_target="tpu_custom_call" | custom-call | tf_op jit(solution)/shard_map/pallas_call | solution.py:218
  (16 shorter events, 0.1 us)
Async XLA Ops:
  0.0 8.1 %collective-permute-start = (bf16[96,1152]{1,0:T(8,128)(2,1)}, bf16[96,1152]{1,0:T(8,128)(2,1)S(1)}, u32[]{:S(2)}, u32[]{:S(2)}) collective-permute-start(bf16[96,1152]{1,0:T(8,128)(2,1)} %refs_0_.1), channel_id=1, source_target_pairs={{0,1},{1,0},{2,3},{3,2},{4,5},{5,4},{6,7},{7,6},{8,9},{9,8},{10,11... | collective-permute-start | bytes 663560 | tf_op jit(solution)/shard_map/ppermute | solution.py:177
  0.5 9.0 %collective-permute-start.1 = (bf16[96,1152]{1,0:T(8,128)(2,1)}, bf16[96,1152]{1,0:T(8,128)(2,1)S(1)}, u32[]{:S(2)}, u32[]{:S(2)}) collective-permute-start(bf16[96,1152]{1,0:T(8,128)(2,1)} %refs_0_.1), channel_id=1, source_target_pairs={{0,4},{1,3},{4,8},{5,1},{8,12},{9,5},{12,14},{13,9},{14,10},{15,13... | collective-permute-start | bytes 663560 | tf_op jit(solution)/shard_map/ppermute | solution.py:177
  7.2 3.9 %collective-permute-start.15 = (bf16[16,128]{1,0:T(8,128)(2,1)}, bf16[16,128]{1,0:T(8,128)(2,1)S(1)}, u32[]{:S(2)}, u32[]{:S(2)}) collective-permute-start(bf16[16,128]{1,0:T(8,128)(2,1)} %shard_map.91), channel_id=1, source_target_pairs={{0,1},{1,0},{2,3},{3,2},{4,5},{5,4},{6,7},{7,6},{8,9},{9,8},{10,11... | collective-permute-start | bytes 12296 | tf_op jit(solution)/shard_map/ppermute | solution.py:177
  8.1 5.9 %collective-permute-start.2 = (bf16[96,1152]{1,0:T(8,128)(2,1)S(1)}, bf16[96,1152]{1,0:T(8,128)(2,1)S(1)}, u32[]{:S(2)}, u32[]{:S(2)}) collective-permute-start(bf16[96,1152]{1,0:T(8,128)(2,1)S(1)} %collective-permute-done.refs_1_), channel_id=1, source_target_pairs={{0,4},{1,3},{4,8},{5,1},{8,12},{9,5},{12,14},{13,9},{14,10},{15,13... | collective-permute-start | bytes 663560 | tf_op jit(solution)/shard_map/ppermute | solution.py:177
  9.5 7.0 %collective-permute-start.5 = (bf16[96,1152]{1,0:T(8,128)(2,1)S(1)}, bf16[96,1152]{1,0:T(8,128)(2,1)S(1)}, u32[]{:S(2)}, u32[]{:S(2)}) collective-permute-start(bf16[96,1152]{1,0:T(8,128)(2,1)S(1)} %collective-permute-done.1.refs_2_), channel_id=1, source_target_pairs={{0,4},{1,3},{4,8},{5,1},{8,12},{9,5},{12,14},{13,9},{14,10},{15,13... | collective-permute-start | bytes 663560 | tf_op jit(solution)/shard_map/ppermute | solution.py:177
  11.7 6.0 %collective-permute-start.16 = (bf16[32,128]{1,0:T(8,128)(2,1)S(1)}, bf16[32,128]{1,0:T(8,128)(2,1)S(1)}, u32[]{:S(2)}, u32[]{:S(2)}) collective-permute-start(bf16[32,128]{1,0:T(8,128)(2,1)S(1)} %pad_maximum_fusion.2), channel_id=1, source_target_pairs={{0,2},{1,3},{2,0},{3,1},{4,6},{5,7},{6,4},{7,5},{8,10},{9,11},{10,... | collective-permute-start | bytes 24584 | tf_op jit(solution)/shard_map/ppermute | solution.py:177
  14.0 6.6 %collective-permute-start.6 = (bf16[96,1152]{1,0:T(8,128)(2,1)S(1)}, bf16[96,1152]{1,0:T(8,128)(2,1)S(1)}, u32[]{:S(2)}, u32[]{:S(2)}) collective-permute-start(bf16[96,1152]{1,0:T(8,128)(2,1)S(1)} %collective-permute-done.2.refs_3_), channel_id=1, source_target_pairs={{0,4},{1,3},{4,8},{5,1},{8,12},{9,5},{12,14},{13,9},{14,10},{15,13... | collective-permute-start | bytes 663560 | tf_op jit(solution)/shard_map/ppermute | solution.py:177
  16.5 5.9 %collective-permute-start.9 = (bf16[96,1152]{1,0:T(8,128)(2,1)S(1)}, bf16[96,1152]{1,0:T(8,128)(2,1)S(1)}, u32[]{:S(2)}, u32[]{:S(2)}) collective-permute-start(bf16[96,1152]{1,0:T(8,128)(2,1)S(1)} %collective-permute-done.5.refs_6_), channel_id=1, source_target_pairs={{0,4},{1,3},{4,8},{5,1},{8,12},{9,5},{12,14},{13,9},{14,10},{15,13... | collective-permute-start | bytes 663560 | tf_op jit(solution)/shard_map/ppermute | solution.py:177
  18.5 5.4 %collective-permute-start.17 = (bf16[64,128]{1,0:T(8,128)(2,1)S(1)}, bf16[64,128]{1,0:T(8,128)(2,1)S(1)}, u32[]{:S(2)}, u32[]{:S(2)}) collective-permute-start(bf16[64,128]{1,0:T(8,128)(2,1)S(1)} %pad_maximum_fusion.1), channel_id=1, source_target_pairs={{0,4},{1,5},{2,6},{3,7},{4,0},{5,1},{6,2},{7,3},{8,12},{9,13},{10,... | collective-permute-start | bytes 49160 | tf_op jit(solution)/shard_map/ppermute | solution.py:177
  20.1 9.7 %collective-permute-start.3 = (bf16[96,1152]{1,0:T(8,128)(2,1)S(1)}, bf16[96,1152]{1,0:T(8,128)(2,1)S(1)}, u32[]{:S(2)}, u32[]{:S(2)}) collective-permute-start(bf16[96,1152]{1,0:T(8,128)(2,1)S(1)} %collective-permute-done.1.refs_2_), channel_id=1, source_target_pairs={{0,1},{1,0},{2,3},{3,2},{4,5},{5,4},{6,7},{7,6},{8,9},{9,8},{10,11... | collective-permute-start | bytes 663560 | tf_op jit(solution)/shard_map/ppermute | solution.py:177
  20.1 10.2 %collective-permute-start.4 = (bf16[96,1152]{1,0:T(8,128)(2,1)S(1)}, bf16[96,1152]{1,0:T(8,128)(2,1)S(1)}, u32[]{:S(2)}, u32[]{:S(2)}) collective-permute-start(bf16[96,1152]{1,0:T(8,128)(2,1)S(1)} %collective-permute-done.2.refs_3_), channel_id=1, source_target_pairs={{0,1},{1,0},{2,3},{3,2},{4,5},{5,4},{6,7},{7,6},{8,9},{9,8},{10,11... | collective-permute-start | bytes 663560 | tf_op jit(solution)/shard_map/ppermute | solution.py:177
  20.6 9.8 %collective-permute-start.10 = (bf16[96,1152]{1,0:T(8,128)(2,1)S(1)}, bf16[96,1152]{1,0:T(8,128)(2,1)S(1)}, u32[]{:S(2)}, u32[]{:S(2)}) collective-permute-start(bf16[96,1152]{1,0:T(8,128)(2,1)S(1)} %collective-permute-done.6.refs_7_), channel_id=1, source_target_pairs={{0,4},{1,3},{4,8},{5,1},{8,12},{9,5},{12,14},{13,9},{14,10},{15,13... | collective-permute-start | bytes 663560 | tf_op jit(solution)/shard_map/ppermute | solution.py:177
  22.4 8.4 %collective-permute-start.13 = (bf16[96,1152]{1,0:T(8,128)(2,1)S(1)}, bf16[96,1152]{1,0:T(8,128)(2,1)S(1)}, u32[]{:S(2)}, u32[]{:S(2)}) collective-permute-start(bf16[96,1152]{1,0:T(8,128)(2,1)S(1)} %collective-permute-done.9.refs_10_), channel_id=1, source_target_pairs={{0,4},{1,3},{4,8},{5,1},{8,12},{9,5},{12,14},{13,9},{14,10},{15,13... | collective-permute-start | bytes 663560 | tf_op jit(solution)/shard_map/ppermute | solution.py:177
  24.6 5.2 %collective-permute-start.18 = (bf16[128,128]{1,0:T(8,128)(2,1)S(1)}, bf16[128,128]{1,0:T(8,128)(2,1)S(1)}, u32[]{:S(2)}, u32[]{:S(2)}) collective-permute-start(bf16[128,128]{1,0:T(8,128)(2,1)S(1)} %pad_maximum_fusion), channel_id=1, source_target_pairs={{0,8},{1,9},{2,10},{3,11},{4,12},{5,13},{6,14},{7,15},{8,0},{9,1},... | collective-permute-start | bytes 98312 | tf_op jit(solution)/shard_map/ppermute | solution.py:177
  29.7 4.2 %collective-permute-start.7 = (bf16[96,1152]{1,0:T(8,128)(2,1)S(1)}, bf16[96,1152]{1,0:T(8,128)(2,1)S(1)}, u32[]{:S(2)}, u32[]{:S(2)}) collective-permute-start(bf16[96,1152]{1,0:T(8,128)(2,1)S(1)} %collective-permute-done.5.refs_6_), channel_id=1, source_target_pairs={{0,1},{1,0},{2,3},{3,2},{4,5},{5,4},{6,7},{7,6},{8,9},{9,8},{10,11... | collective-permute-start | bytes 663560 | tf_op jit(solution)/shard_map/ppermute | solution.py:177
  29.7 4.2 %collective-permute-start.8 = (bf16[96,1152]{1,0:T(8,128)(2,1)S(1)}, bf16[96,1152]{1,0:T(8,128)(2,1)S(1)}, u32[]{:S(2)}, u32[]{:S(2)}) collective-permute-start(bf16[96,1152]{1,0:T(8,128)(2,1)S(1)} %collective-permute-done.6.refs_7_), channel_id=1, source_target_pairs={{0,1},{1,0},{2,3},{3,2},{4,5},{5,4},{6,7},{7,6},{8,9},{9,8},{10,11... | collective-permute-start | bytes 663560 | tf_op jit(solution)/shard_map/ppermute | solution.py:177
  30.3 3.7 %collective-permute-start.11 = (bf16[96,1152]{1,0:T(8,128)(2,1)S(1)}, bf16[96,1152]{1,0:T(8,128)(2,1)S(1)}, u32[]{:S(2)}, u32[]{:S(2)}) collective-permute-start(bf16[96,1152]{1,0:T(8,128)(2,1)S(1)} %collective-permute-done.9.refs_10_), channel_id=1, source_target_pairs={{0,1},{1,0},{2,3},{3,2},{4,5},{5,4},{6,7},{7,6},{8,9},{9,8},{10,11... | collective-permute-start | bytes 663560 | tf_op jit(solution)/shard_map/ppermute | solution.py:177
  30.3 3.7 %collective-permute-start.12 = (bf16[96,1152]{1,0:T(8,128)(2,1)S(1)}, bf16[96,1152]{1,0:T(8,128)(2,1)S(1)}, u32[]{:S(2)}, u32[]{:S(2)}) collective-permute-start(bf16[96,1152]{1,0:T(8,128)(2,1)S(1)} %collective-permute-done.10.refs_11_), channel_id=1, source_target_pairs={{0,1},{1,0},{2,3},{3,2},{4,5},{5,4},{6,7},{7,6},{8,9},{9,8},{10,11... | collective-permute-start | bytes 663560 | tf_op jit(solution)/shard_map/ppermute | solution.py:177
  30.8 3.2 %collective-permute-start.14 = (bf16[96,1152]{1,0:T(8,128)(2,1)S(1)}, bf16[96,1152]{1,0:T(8,128)(2,1)S(1)}, u32[]{:S(2)}, u32[]{:S(2)}) collective-permute-start(bf16[96,1152]{1,0:T(8,128)(2,1)S(1)} %collective-permute-done.13.refs_14_), channel_id=1, source_target_pairs={{0,1},{1,0},{2,3},{3,2},{4,5},{5,4},{6,7},{7,6},{8,9},{9,8},{10,11... | collective-permute-start | bytes 663560 | tf_op jit(solution)/shard_map/ppermute | solution.py:177
  32.5 1.4 %copy-start = (bf16[768,1536]{1,0:T(8,128)(2,1)}, bf16[768,1536]{1,0:T(8,128)(2,1)S(1)}, u32[]{:S(2)}) copy-start(bf16[768,1536]{1,0:T(8,128)(2,1)S(1)} %get-tuple-element.9.refs_16_) | copy-start | bytes 7077892
  34.0 1.3 %copy-start.1 = (bf16[1152,576]{0,1:T(8,128)(2,1)S(1)}, bf16[1152,576]{0,1:T(8,128)(2,1)}, u32[]{:S(2)}) copy-start(bf16[1152,576]{0,1:T(8,128)(2,1)} %param.13) | copy-start | bytes 3981316
  35.3 1.3 %copy-start.2 = (bf16[1152,576]{0,1:T(8,128)(2,1)S(1)}, bf16[1152,576]{0,1:T(8,128)(2,1)}, u32[]{:S(2)}) copy-start(bf16[1152,576]{0,1:T(8,128)(2,1)} %param.14) | copy-start | bytes 3981316
  36.7 1.3 %copy-start.3 = (bf16[1152,576]{0,1:T(8,128)(2,1)S(1)}, bf16[1152,576]{0,1:T(8,128)(2,1)}, u32[]{:S(2)}) copy-start(bf16[1152,576]{0,1:T(8,128)(2,1)} %param.15) | copy-start | bytes 3981316
  38.0 1.3 %copy-start.4 = (bf16[576,1152]{1,0:T(8,128)(2,1)S(1)}, bf16[576,1152]{1,0:T(8,128)(2,1)}, u32[]{:S(2)}) copy-start(bf16[576,1152]{1,0:T(8,128)(2,1)} %refs_23_.1) | copy-start | bytes 3981316
  39.3 0.9 %copy-start.5 = (bf16[96,1152]{1,0:T(8,128)(2,1)S(1)}, bf16[96,1152]{1,0:T(8,128)(2,1)}, u32[]{:S(2)}) copy-start(bf16[96,1152]{1,0:T(8,128)(2,1)} %refs_0_.1) | copy-start | bytes 663556

commit v2 on v1

--- a/solution.py
+++ b/solution.py
@@ -14,7 +14,8 @@
 LANES = 128
 GATHERED_MAX = 8 << 20
 VMEM_PREP = 16 << 20
-VMEM_TAIL = 44 << 20
+VMEM_MERGE = 12 << 20
+VMEM_TAIL = 20 << 20
 F32 = jnp.float32
 BF16 = jnp.bfloat16
 NT = (((1,), (1,)), ((), ()))
@@ -32,77 +33,78 @@
     return row * 4 + column * 2 + core
 
 
-def ring_moves(shards):
+def ring_moves(shards, crossing):
     rows = shards // 4
     moves = []
     for k in range(2 * rows):
         for core, step in ((0, 1), (1, -1)):
-            moves.append((ring_index(k, core, rows), ring_index(k + step, core, rows)))
+            source = ring_index(k, core ^ crossing, rows)
+            moves.append((source, ring_index(k + step, core, rows)))
     return moves
 
 
-def sender_table(shards):
+def senders(shards, me):
     rows = shards // 4
-    position = {ring_index(k, c, rows): (k, c) for k in range(2 * rows) for c in (0, 1)}
-    table = []
-    for me in range(shards):
-        k, c = position[me]
-        d = -1 if c == 0 else 1
-        row = [me, me ^ 1]
-        for s in range(1, rows):
-            row += [
-                ring_index(k + d * s, c, rows),
-                ring_index(k + d * s, c ^ 1, rows),
-                ring_index(k - d * s, c ^ 1, rows),
-                ring_index(k - d * s, c, rows),
-            ]
-        row += [ring_index(k + d * rows, c, rows), ring_index(k - d * rows, c ^ 1, rows)]
-        table.append(row)
-    return table
-
-
-def meta_kernel(slots, owner_col_ref, owner_row_ref, sizes_ref, map_ref, out_ref):
-    tok = owner_row_ref.shape[1]
-    row = owner_row_ref[...]
-    earlier = lax.broadcasted_iota(jnp.int32, (tok, tok), 0) < lax.broadcasted_iota(
-        jnp.int32, (tok, tok), 1
-    )
-    same = jnp.where(owner_col_ref[...] == row, 1, 0)
-    rank = jnp.sum(jnp.where(earlier, same, 0), axis=0, keepdims=True)
+    row, column, core = me // 4, (me // 2) % 2, me % 2
+    k = jnp.where(column == 0, row, 2 * rows - 1 - row)
+    d = 2 * core - 1
+
+    def at(offset, core):
+        p = (k + offset + 2 * rows) % (2 * rows)
+        back = p >= rows
+        row = jnp.where(back, 2 * rows - 1 - p, p)
+        return row * 4 + jnp.where(back, 2, 0) + core
+
+    swapped = 1 - core
+    found = [me, me ^ 1]
+    for s in range(1, rows):
+        found += [at(d * s, core), at(-d * s, swapped), at(d * s, swapped), at(-d * s, core)]
+    return found + [at(d * rows, core), at(-d * rows, swapped)]
+
+
+def flip(x, shards):
+    return x % 2 * (shards // 2) + x // 2 % 2 * (shards // 4) + x // 4
+
+
+def meta_kernel(slots, owner_ref, sizes_ref, map_ref, out_ref):
+    tok = owner_ref.shape[1]
+
+    def wide(x):
+        x = x.astype(F32)
+        return jnp.concatenate([x, jnp.zeros((1, LANES - x.shape[1]), F32)], axis=1)
+
+    row = wide(owner_ref[...])
+    column = jnp.transpose(jnp.broadcast_to(row, (8, LANES)), (1, 0))[:, 0:1]
+    first = lax.broadcasted_iota(jnp.int32, (LANES, LANES), 0)
+    second = lax.broadcasted_iota(jnp.int32, (LANES, LANES), 1)
+    earlier = (first < second) & (column == row)
+    rank = jnp.sum(jnp.where(earlier, 1.0, 0.0), axis=0, keepdims=True)
+    rows = [wide(map_ref[r]) for r in range(slots)] + [row, rank, wide(sizes_ref[...])]
     sub = lax.broadcasted_iota(jnp.int32, (META, LANES), 0)
-
-    def wide(x, rows):
-        x = x.astype(F32)
-        x = jnp.concatenate([x, jnp.zeros((x.shape[0], LANES - x.shape[1]), F32)], axis=1)
-        if x.shape[0] == 1:
-            return jnp.broadcast_to(x, (META, LANES))
-        return jnp.concatenate([x, jnp.zeros((META - rows, LANES), F32)], axis=0)
-
-    out = wide(map_ref[...], slots)
-    out = jnp.where(sub == slots, wide(row, 1), out)
-    out = jnp.where(sub == slots + 1, wide(rank, 1), out)
-    out = jnp.where(sub == slots + 2, wide(sizes_ref[...], 1), out)
+    out = jnp.zeros((META, LANES), F32)
+    for r, x in enumerate(rows):
+        out = jnp.where(sub == r, x, out)
     out_ref[...] = out.astype(BF16)
 
 
 def prep_kernel(
-    shards, slots, tok, merged_rows, me_ref, table_ref, g_ref,
+    shards, slots, tok, merged_rows, g_ref,
     m_ref, inv_ref, bias_ref, pick_ref, gf, dest_row, size_row,
 ):
-    me = me_ref[0]
+    me = lax.axis_index("ctx")
+    me_flipped = flip(me, shards)
     total = merged_rows * shards
     gf[...] = g_ref[...].astype(F32)
     by_sender = jnp.transpose(gf[...], (1, 0))[:shards].astype(BF16)
     places = shards * META
     bucket = lax.broadcasted_iota(jnp.int32, (places, LANES), 0)
     sender_iota = lax.broadcasted_iota(jnp.int32, (shards, LANES), 0)
-    for j in range(shards):
-        e = table_ref[j]
-        base = (e ^ me) * META
+    for j, e in enumerate(senders(shards, me)):
+        base = flip(e ^ me, shards) * META
         own = gf[pl.ds(base + slots, 1), :].astype(jnp.int32)
         rank = gf[pl.ds(base + slots + 1, 1), :].astype(jnp.int32)
         size = gf[pl.ds(base + slots + 2, 1), :]
-        hot = jnp.where(bucket == (own ^ me) * META + rank, 1.0, 0.0).astype(BF16)
+        hot = jnp.where(bucket == (flip(own, shards) ^ me_flipped) * META + rank, 1.0, 0.0).astype(BF16)
         found = dot(by_sender, hot)
         slot = jnp.sum(jnp.where(sender_iota == e, found, 0.0), axis=0, keepdims=True)
         dest = own.astype(F32) * merged_rows + slot
@@ -125,39 +127,45 @@
     pick_ref[...] = jnp.where(lane == mine, 1.0, 0.0).astype(BF16)
 
 
-def tail_kernel(n_blocks, *refs):
+def cost(flops, nbytes):
+    return pl.CostEstimate(flops=flops, bytes_accessed=nbytes, transcendentals=0)
+
+
+def gather_blocks(blocks, tok_s):
+    tok = blocks[0].shape[0]
+    for j, block in enumerate(blocks):
+        tok_s[j * tok : (j + 1) * tok, :] = block[...]
+
+
+def merge_kernel(n_blocks, first, *refs):
+    blocks, (m_ref, *before, acc_ref, tok_s) = refs[:n_blocks], refs[n_blocks:]
+    gather_blocks(blocks, tok_s)
+    cols = slice(first, first + tok_s.shape[0])
+    acc = dot(m_ref[:, cols], tok_s[...])
+    acc_ref[...] = acc + before[0][...] if before else acc
+
+
+def tail_kernel(n_blocks, first, *refs):
     blocks = refs[:n_blocks]
-    (m_ref, inv_ref, bias_ref, pick_ref, wq_ref, wk_ref, wv_ref, wo_ref, out_ref,
+    (acc_ref, m_ref, inv_ref, bias_ref, pick_ref, wq_ref, wk_ref, wv_ref, wo_ref, out_ref,
      tok_s, merged_s, att_s) = refs[n_blocks:]
-    tok = blocks[0].shape[0]
-    for j in range(n_blocks):
-        tok_s[j * tok : (j + 1) * tok, :] = blocks[j][...]
-    total = m_ref.shape[0]
-    tile = 256
-
-    def merge(i, _):
-        rows = pl.ds(pl.multiple_of(i * tile, tile), tile)
-        acc = dot(m_ref[rows, :], tok_s[...])
-        merged_s[rows, :] = (acc * inv_ref[rows, :]).astype(BF16)
-        return 0
-
-    lax.fori_loop(0, total // tile, merge, 0)
+    gather_blocks(blocks, tok_s)
+    acc = acc_ref[...] + dot(m_ref[:, first:], tok_s[...])
+    merged_s[...] = (acc * inv_ref[...]).astype(BF16)
     merged = merged_s[...]
     picked = dot(pick_ref[...], merged).astype(BF16)
-    q_t = dot(wq_ref[...], picked, NT).astype(BF16)
+    q_t = dot(wq_ref[...], picked, NT)
     inverse = 1.0 / math.sqrt(HEAD)
     bias = bias_ref[...]
     k_t = dot(wk_ref[...], merged, NT)
     v_t = dot(wv_ref[...], merged, NT)
     for h in range(HEADS):
         rows = slice(h * HEAD, (h + 1) * HEAD)
-        q_h = q_t[rows].astype(BF16)
-        scores = dot(q_h, k_t[rows].astype(BF16), TN) * inverse + bias
+        scores = dot(q_t[rows].astype(BF16), k_t[rows].astype(BF16), TN) * inverse + bias
         top = jnp.max(scores, axis=1, keepdims=True)
         expo = jnp.exp(scores - top)
         whole = jnp.sum(expo, axis=1, keepdims=True)
-        att = dot(expo.astype(BF16), v_t[rows].astype(BF16), NT) / whole
-        att_s[:, rows] = att
+        att_s[:, rows] = dot(expo.astype(BF16), v_t[rows].astype(BF16), NT) / whole
     out_ref[...] = dot(att_s[...].astype(BF16), wo_ref[...]).astype(BF16)
 
 
@@ -168,36 +176,45 @@
     merged_rows = tok // 2
     total = merged_rows * shards
     vmem = pl.BlockSpec(memory_space=pltpu.VMEM)
-    smem = pl.BlockSpec(memory_space=pltpu.SMEM)
-    me = lax.axis_index("ctx")
-    moves = ring_moves(shards)
     swap = [(i, i ^ 1) for i in range(shards)]
-
-    def send(x, pairs):
+    along, across = ring_moves(shards, 0), ring_moves(shards, 1)
+
+    def send(x, pairs, *after):
+        if after:
+            x, *_ = lax.optimization_barrier((x, *after))
         return lax.ppermute(x, "ctx", pairs)
 
+    a, b = send(tokens, along), send(tokens, across)
+    other = send(tokens, swap)
     meta = pl.pallas_call(
         functools.partial(meta_kernel, slots),
         out_shape=jax.ShapeDtypeStruct((META, LANES), BF16),
-        in_specs=[vmem] * 4,
+        in_specs=[vmem] * 3,
         out_specs=vmem,
-    )(owner, owner.reshape(1, tok), sizes.reshape(1, tok), jnp.transpose(slot_map[0], (1, 0)))
-    bit = 1
-    while bit < shards:
-        meta = jnp.concatenate([meta, send(meta, [(i, i ^ bit) for i in range(shards)])], axis=0)
-        bit *= 2
-
-    other = send(tokens, swap)
-    a, b = tokens, other
+    )(owner.reshape(1, tok), sizes.reshape(1, tok), jnp.transpose(slot_map, (2, 0, 1)))
+    metas = [meta]
+    bit = shards // 2
+
+    def spread(*after):
+        nonlocal bit
+        if bit:
+            pairs = [(i, i ^ bit) for i in range(shards)]
+            metas.append(send(jnp.concatenate(metas, axis=0), pairs, *after))
+            bit //= 2
+
+    a1 = a
+    def xor(x, d, *after):
+        return send(x, [(i, i ^ d) for i in range(shards)], *after)
+
+    row = jnp.concatenate([meta] + [xor(meta, d, *(other,)) for d in range(4, shards, 4)], axis=0)
+    plane = jnp.concatenate([row, xor(row, 2)], axis=0)
+    metas = [plane, xor(plane, 1)]
     blocks = [tokens, other]
     for s in range(1, shards // 4):
-        a = send(a, moves)
-        b = send(b, moves)
-        blocks += [a, b, send(a, swap), send(b, swap)]
-    a = send(a, moves)
-    blocks += [a, send(a, swap)]
-
-    table = jnp.array(sender_table(shards), jnp.int32)[me]
+        blocks += [a, send(a, swap), b, send(b, swap)]
+        a = send(a, along)
+        if s < shards // 4 - 1:
+            b = send(b, along)
     m, inv, bias, pick = pl.pallas_call(
         functools.partial(prep_kernel, shards, slots, tok, merged_rows),
         out_shape=(
@@ -206,7 +223,7 @@
             jax.ShapeDtypeStruct((1, total), F32),
             jax.ShapeDtypeStruct((tok, total), BF16),
         ),
-        in_specs=[smem, smem, vmem],
+        in_specs=[vmem],
         out_specs=(vmem,) * 4,
         scratch_shapes=[
             pltpu.VMEM((shards * META, LANES), F32),
@@ -214,19 +231,38 @@
             pltpu.VMEM((1, shards * tok), F32),
         ],
         compiler_params=pltpu.CompilerParams(vmem_limit_bytes=VMEM_PREP),
-    )(me.reshape(1), table, meta)
+    )(jnp.concatenate(metas, axis=0))
+    cuts = [0, shards // 2, shards - 4, shards]
+    acc = []
+    for low, high in zip(cuts[:-2], cuts[1:-1]):
+        n = high - low
+        acc = [
+            pl.pallas_call(
+                functools.partial(merge_kernel, n, low * tok),
+                out_shape=jax.ShapeDtypeStruct((total, width), F32),
+                in_specs=[vmem] * (n + 1 + len(acc)),
+                out_specs=vmem,
+                scratch_shapes=[pltpu.VMEM((n * tok, width), BF16)],
+                input_output_aliases={n + 1: 0} if acc else {},
+                compiler_params=pltpu.CompilerParams(vmem_limit_bytes=VMEM_MERGE),
+            )(*blocks[low:high], m, *acc)
+        ]
+    blocks += [a, send(a, swap, *acc)]
+    low, high = cuts[-2:]
+    n = high - low
     return pl.pallas_call(
-        functools.partial(tail_kernel, len(blocks)),
+        functools.partial(tail_kernel, n, low * tok),
         out_shape=jax.ShapeDtypeStruct((tok, width), BF16),
-        in_specs=[vmem] * (len(blocks) + 8),
+        in_specs=[vmem] * (n + 9),
         out_specs=vmem,
         scratch_shapes=[
-            pltpu.VMEM((shards * tok, width), BF16),
+            pltpu.VMEM((n * tok, width), BF16),
             pltpu.VMEM((total, width), BF16),
             pltpu.VMEM((tok, HEADS * HEAD), F32),
         ],
         compiler_params=pltpu.CompilerParams(vmem_limit_bytes=VMEM_TAIL),
-    )(*blocks, m, inv, bias, pick, w_query.T, w_key.T, w_value.T, w_out)
+        cost_estimate=cost(4 * total * width * HEADS * HEAD, 8 * width * HEADS * HEAD),
+    )(*blocks[low:high], *acc, m, inv, bias, pick, w_query.T, w_key.T, w_value.T, w_out)
 
 
 def on_device_exchanged(tokens, owner, slot_map, sizes, w_query, w_key, w_value, w_out):

time: 52.2 us -> 39.1 us (0.75)
  local copies, waits for them, and re-layouts: 11.7 us -> 1.73 us
  waiting for transfers between devices: 5.7 us -> 11 us
  starting transfers between devices: 17.5 us -> 12.3 us
  Pallas kernels: 14.6 us -> 12.9 us
  other arithmetic: 2.06 us -> 0.69 us
    unnamed x18 -> x14, local copies, waits for them, and re-layouts: 11 us -> 1.71 us
    ppermute x19 -> x20, waiting for transfers between devices: 5.7 us -> 11 us  [send(): return lax.ppermute(x, 'ctx', pairs)]
    ppermute x19 -> x20, starting transfers between devices: 17.5 us -> 12.3 us  [send(): return lax.ppermute(x, 'ctx', pairs)]
    concatenate x3 -> x1, other arithmetic: 2.06 us -> 0.69 us  [on_device_gathered(): jnp.concatenate([meta] + [xor(meta, d, *(other,)) for d in range(4, shard...]
    pallas_call x1 -> x3, Pallas kernels: 11.4 us -> 10.2 us  [the longest x1 6.98 us: on_device_gathered(): pl.pallas_call(functools.partial(tail_kernel, n, low * tok), out_shape=ja...]
    squeeze x1 -> x0, local copies, waits for them, and re-layouts: 0.69 us -> none  [on_device_gathered(): table = jnp.array(sender_table(shards), jnp.int32)[me]]
  transfers between devices with their start and end apart: 19 -> 20, of which waited for: 4 -> 7; matrix products, arithmetic and copies ran while one was open for 12% -> 4% of each run, Pallas kernels for 6% -> 15%
where the time goes in v2:
time: 39.1 us; the launch traced here: 38.8 us
  Pallas kernels  12.9 us (33%)
  starting transfers between devices  12.3 us (31%)
  waiting for transfers between devices  11 us (28%)
  local copies, waits for them, and re-layouts  1.73 us (4%)
  other arithmetic  0.69 us (2%)
    ppermute x20, starting transfers between devices, send(): return lax.ppermute(x, 'ctx', pairs)  12.3 us
    ppermute x20, waiting for transfers between devices, send(): return lax.ppermute(x, 'ctx', pairs)  11 us
    pallas_call x1, Pallas kernels, on_device_gathered(): pl.pallas_call(functools.partial(tail_kernel, n, low * tok), out_shape=ja...  6.98 us
    pallas_call x2, Pallas kernels, on_device_gathered(): pl.pallas_call(functools.partial(merge_kernel, n, low * tok), out_shape=j...  3.2 us
    unnamed x14, local copies, waits for them, and re-layouts  1.71 us
    pallas_call x1, Pallas kernels, on_device_gathered(): pl.pallas_call(functools.partial(meta_kernel, slots), out_shape=jax.Shape...  1.5 us
    pallas_call x1, Pallas kernels, on_device_gathered(): pl.pallas_call(functools.partial(prep_kernel, shards, slots, tok, merged_...  1.26 us
  transfers between devices with their start and end apart: 20, of which 7 were waited for; matrix products, arithmetic and copies ran while one was open for 4% of the time, Pallas kernels for 15%

profile of v2, /device:TPU:0, one launch (start us, length us, event | category | flops | bytes accessed | tf_op | source)
XLA Modules:
  0.0 38.8 jit_solution(5893511676179275054)
XLA Ops:
  0.0 0.5 %collective-permute-start.10 = (bf16[96,1152]{1,0:T(8,128)(2,1)}, bf16[96,1152]{1,0:T(8,128)(2,1)S(1)}, u32[]{:S(2)}, u32[]{:S(2)}) collective-permute-start(bf16[96,1152]{1,0:T(8,128)(2,1)} %refs_0_.1), channel_id=1, source_target_pairs={{0,1},{1,0},{2,3},{3,2},{4,5},{5,4},{6,7},{7,6},{8,9},{9,8},{10,11... | collective-permute-start | bytes 663560 | tf_op jit(solution)/shard_map/ppermute | solution.py:185
  0.5 2.6 %collective-permute-start.4 = (bf16[96,1152]{1,0:T(8,128)(2,1)}, bf16[96,1152]{1,0:T(8,128)(2,1)S(1)}, u32[]{:S(2)}, u32[]{:S(2)}) collective-permute-start(bf16[96,1152]{1,0:T(8,128)(2,1)} %refs_0_.1), channel_id=1, source_target_pairs={{0,4},{1,3},{4,8},{5,1},{8,12},{9,5},{12,14},{13,9},{14,10},{15,13... | collective-permute-start | bytes 663560 | tf_op jit(solution)/shard_map/ppermute | solution.py:185
  3.0 1.4 %collective-permute-start = (bf16[96,1152]{1,0:T(8,128)(2,1)}, bf16[96,1152]{1,0:T(8,128)(2,1)S(1)}, u32[]{:S(2)}, u32[]{:S(2)}) collective-permute-start(bf16[96,1152]{1,0:T(8,128)(2,1)} %refs_0_.1), channel_id=1, source_target_pairs={{1,4},{0,3},{5,8},{4,1},{9,12},{8,5},{13,14},{12,9},{15,10},{14,13... | collective-permute-start | bytes 663560 | tf_op jit(solution)/shard_map/ppermute | solution.py:185
  4.4 1.5 %shard_map.82 = bf16[16,128]{1,0:T(8,128)(2,1)} custom-call(s32[1,96]{1,0:T(1,128)} %bitcast.10, s32[1,96]{1,0:T(1,128)} %bitcast.11, s32[12,1,16]{2,1,0:T(1,128)} %bitcast.9), custom_call_target="tpu_custom_call" | custom-call | tf_op jit(solution)/shard_map/pallas_call | solution.py:189
  5.9 0.0 collective-permute-done.10.refs_1_
  5.9 0.5 %collective-permute-start.11 = (bf16[16,128]{1,0:T(8,128)(2,1)}, bf16[16,128]{1,0:T(8,128)(2,1)S(1)}, u32[]{:S(2)}, u32[]{:S(2)}) collective-permute-start(bf16[16,128]{1,0:T(8,128)(2,1)} %shard_map.82), channel_id=1, source_target_pairs={{0,4},{1,5},{2,6},{3,7},{4,0},{5,1},{6,2},{7,3},{8,12},{9,13},{10,... | collective-permute-start | bytes 12296 | tf_op jit(solution)/shard_map/ppermute | solution.py:185
  6.3 2.3 %collective-permute-start.12 = (bf16[16,128]{1,0:T(8,128)(2,1)}, bf16[16,128]{1,0:T(8,128)(2,1)S(1)}, u32[]{:S(2)}, u32[]{:S(2)}) collective-permute-start(bf16[16,128]{1,0:T(8,128)(2,1)} %shard_map.82), channel_id=1, source_target_pairs={{0,8},{1,9},{2,10},{3,11},{4,12},{5,13},{6,14},{7,15},{8,0},{9,1},... | collective-permute-start | bytes 12296 | tf_op jit(solution)/shard_map/ppermute | solution.py:185
  8.6 1.6 %collective-permute-start.13 = (bf16[16,128]{1,0:T(8,128)(2,1)}, bf16[16,128]{1,0:T(8,128)(2,1)S(1)}, u32[]{:S(2)}, u32[]{:S(2)}) collective-permute-start(bf16[16,128]{1,0:T(8,128)(2,1)} %shard_map.82), channel_id=1, source_target_pairs={{0,12},{1,13},{2,14},{3,15},{4,8},{5,9},{6,10},{7,11},{8,4},{9,5},... | collective-permute-start | bytes 12296 | tf_op jit(solution)/shard_map/ppermute | solution.py:185
  10.3 0.7 %constant_dynamic-update-slice_fusion.4 = (bf16[128,128]{1,0:T(8,128)(2,1)S(1)}, bf16[256,128]{1,0:T(8,128)(2,1)S(1)}) fusion(bf16[16,128]{1,0:T(8,128)(2,1)} %shard_map.82), kind=kLoop, calls=%fused_computation.4 | loop fusion | bytes 12288
  11.0 0.0 collective-permute-done.4.refs_2_
  11.0 0.0 collective-permute-start.5
  11.0 0.0 collective-permute-done.refs_4_
  11.0 0.1 collective-permute-start.16
  11.1 0.0 collective-permute-done.11
  11.1 0.5 %collective-permute-start.17 = (bf16[96,1152]{1,0:T(8,128)(2,1)S(1)}, bf16[96,1152]{1,0:T(8,128)(2,1)S(1)}, u32[]{:S(2)}, u32[]{:S(2)}) collective-permute-start(bf16[96,1152]{1,0:T(8,128)(2,1)S(1)} %collective-permute-done.refs_4_), channel_id=1, source_target_pairs={{0,1},{1,0},{2,3},{3,2},{4,5},{5,4},{6,7},{7,6},{8,9},{9,8},{10,11... | collective-permute-start | bytes 663560 | tf_op jit(solution)/shard_map/ppermute | solution.py:185
  11.6 0.0 collective-permute-done.12
  11.6 1.1 %collective-permute-start.1 = (bf16[96,1152]{1,0:T(8,128)(2,1)S(1)}, bf16[96,1152]{1,0:T(8,128)(2,1)S(1)}, u32[]{:S(2)}, u32[]{:S(2)}) collective-permute-start(bf16[96,1152]{1,0:T(8,128)(2,1)S(1)} %collective-permute-done.refs_4_), channel_id=1, source_target_pairs={{0,4},{1,3},{4,8},{5,1},{8,12},{9,5},{12,14},{13,9},{14,10},{15,13... | collective-permute-start | bytes 663560 | tf_op jit(solution)/shard_map/ppermute | solution.py:185
  12.6 1.7 %collective-permute-done.13 = bf16[16,128]{1,0:T(8,128)(2,1)S(1)} collective-permute-done((bf16[16,128]{1,0:T(8,128)(2,1)}, bf16[16,128]{1,0:T(8,128)(2,1)S(1)}, u32[]{:S(2)}, u32[]{:S(2)}) %collective-permute-start.13) | collective-permute-done | bytes 4128 | tf_op jit(solution)/shard_map/ppermute | solution.py:185
  14.3 0.7 %pad_maximum_fusion = bf16[64,128]{1,0:T(8,128)(2,1)S(1)} fusion(bf16[16,128]{1,0:T(8,128)(2,1)S(1)} %collective-permute-done.13, bf16[16,128]{1,0:T(8,128)(2,1)S(1)} %collective-permute-done.12, bf16[16,128]{1,0:T(8,128)(2,1)S(1)} %collective-permute-done.11, bf16[16,128]{1,0:T(8,128)(2,1)} %shard_map.82), kind=kLoop, calls=%fused_computation.11 | loop fusion | flops 65536 | bytes 32768 | tf_op jit(solution)/shard_map/concatenate | solution.py:209
  15.0 0.7 %collective-permute-start.14 = (bf16[64,128]{1,0:T(8,128)(2,1)S(1)}, bf16[64,128]{1,0:T(8,128)(2,1)S(1)}, u32[]{:S(2)}, u32[]{:S(2)}) collective-permute-start(bf16[64,128]{1,0:T(8,128)(2,1)S(1)} %pad_maximum_fusion), channel_id=1, source_target_pairs={{0,2},{1,3},{2,0},{3,1},{4,6},{5,7},{6,4},{7,5},{8,10},{9,11},{10,... | collective-permute-start | bytes 49160 | tf_op jit(solution)/shard_map/ppermute | solution.py:185
  15.8 1.4 %collective-permute-done.5.refs_6_ = bf16[96,1152]{1,0:T(8,128)(2,1)S(1)} collective-permute-done((bf16[96,1152]{1,0:T(8,128)(2,1)S(1)}, bf16[96,1152]{1,0:T(8,128)(2,1)S(1)}, u32[]{:S(2)}, u32[]{:S(2)}) %collective-permute-start.5) | collective-permute-done | bytes 221216 | tf_op jit(solution)/shard_map/ppermute | solution.py:185
  17.1 2.5 %collective-permute-done.14 = bf16[64,128]{1,0:T(8,128)(2,1)S(1)} collective-permute-done((bf16[64,128]{1,0:T(8,128)(2,1)S(1)}, bf16[64,128]{1,0:T(8,128)(2,1)S(1)}, u32[]{:S(2)}, u32[]{:S(2)}) %collective-permute-start.14) | collective-permute-done | bytes 16416 | tf_op jit(solution)/shard_map/ppermute | solution.py:185
  19.7 0.1 collective-permute-start.15
  19.7 0.1 collective-permute-start.2
  19.8 1.1 %collective-permute-done.15 = bf16[128,128]{1,0:T(8,128)(2,1)S(1)} collective-permute-done((bf16[128,128]{1,0:T(8,128)(2,1)S(1)}, bf16[128,128]{1,0:T(8,128)(2,1)S(1)}, u32[]{:S(2)}, u32[]{:S(2)}) %collective-permute-start.15) | collective-permute-done | bytes 32800 | tf_op jit(solution)/shard_map/ppermute | solution.py:185
  20.9 0.2 collective-permute-start.18
  21.1 0.3 collective-permute-start.8
  21.4 1.6 %collective-permute-done.6.refs_2_ = bf16[96,1152]{1,0:T(8,128)(2,1)S(1)} collective-permute-done((bf16[96,1152]{1,0:T(8,128)(2,1)S(1)}, bf16[96,1152]{1,0:T(8,128)(2,1)S(1)}, u32[]{:S(2)}, u32[]{:S(2)}) %collective-permute-start.6) | collective-permute-done | bytes 221216 | tf_op jit(solution)/shard_map/ppermute | solution.py:185
  23.0 0.0 collective-permute-start.9
  23.0 0.0 collective-permute-start.7
  23.1 1.3 %shard_map.83 = (bf16[768,1536]{1,0:T(8,128)(2,1)S(1)}, f32[768,1]{1,0:T(8,128)S(1)}, f32[1,768]{1,0:T(1,128)S(1)}, bf16[96,768]{1,0:T(8,128)(2,1)S(1)}) custom-call(bf16[256,128]{1,0:T(8,128)(2,1)S(1)} %constant_dynamic-update-slice_fusion.5.g_ref), custom_call_target="tpu_custom_call" | custom-call | tf_op jit(solution)/shard_map/pallas_call | solution.py:218
  24.3 1.4 %collective-permute-done.2.refs_0_ = bf16[96,1152]{1,0:T(8,128)(2,1)S(1)} collective-permute-done((bf16[96,1152]{1,0:T(8,128)(2,1)S(1)}, bf16[96,1152]{1,0:T(8,128)(2,1)S(1)}, u32[]{:S(2)}, u32[]{:S(2)}) %collective-permute-start.2) | collective-permute-done | bytes 221216 | tf_op jit(solution)/shard_map/ppermute | solution.py:185
  25.7 0.3 collective-permute-start.3
  26.0 0.0 collective-permute-done.18.refs_7_
  26.0 0.9 %copy-done.4 = bf16[96,1152]{1,0:T(8,128)(2,1)S(1)} copy-done((bf16[96,1152]{1,0:T(8,128)(2,1)S(1)}, bf16[96,1152]{1,0:T(8,128)(2,1)}, u32[]{:S(2)}) %copy-start.4) | copy-done | bytes 221208
  27.0 1.8 %shard_map.84.refs_5_ = f32[768,1152]{1,0:T(8,128)S(1)} custom-call(bf16[96,1152]{1,0:T(8,128)(2,1)S(1)} %copy-done.4, bf16[96,1152]{1,0:T(8,128)(2,1)S(1)} %collective-permute-done.10.refs_1_, bf16[96,1152]{1,0:T(8,128)(2,1)S(1)} %collective-permute-done.4.refs_2_, bf16[96,1152]{1,0:T(8,128)(2,1)S(1)} %collective-permute-done.16.refs_3_, ...), custom_call_target="tpu_custom_call" | custom-call | tf_op jit(solution)/shard_map/pallas_call | solution.py:240
  28.7 0.0 copy-start
  28.7 0.0 copy-start.1
  28.7 0.0 copy-start.2
  28.8 0.0 copy-start.3
  28.8 0.0 collective-permute-done.8.refs_1_
  28.8 0.0 collective-permute-done.9.refs_3_
  28.8 1.4 %shard_map.85.refs_4_ = f32[768,1152]{1,0:T(8,128)S(1)} custom-call(bf16[96,1152]{1,0:T(8,128)(2,1)S(1)} %collective-permute-done.1.refs_0_, bf16[96,1152]{1,0:T(8,128)(2,1)S(1)} %collective-permute-done.8.refs_1_, bf16[96,1152]{1,0:T(8,128)(2,1)S(1)} %collective-permute-done.6.refs_2_, ...), custom_call_target="tpu_custom_call", output_to_operand_aliasing={{}: (5, {})} | custom-call | tf_op jit(solution)/shard_map/pallas_call | solution.py:240
  30.2 0.0 collective-permute-done.7.refs_2_
  30.3 0.3 collective-permute-start.19
  30.5 0.0 collective-permute-done.3.refs_1_
  30.5 1.3 %collective-permute-done.19.refs_3_ = bf16[96,1152]{1,0:T(8,128)(2,1)S(1)} collective-permute-done((bf16[96,1152]{1,0:T(8,128)(2,1)S(1)}, bf16[96,1152]{1,0:T(8,128)(2,1)S(1)}, u32[]{:S(2)}, u32[]{:S(2)}) %collective-permute-start.19) | collective-permute-done | bytes 221216 | tf_op jit(solution)/shard_map/ppermute | solution.py:185
  31.8 7.0 %shard_map.86 = bf16[96,1152]{1,0:T(8,128)(2,1)} custom-call(bf16[96,1152]{1,0:T(8,128)(2,1)S(1)} %collective-permute-done.2.refs_0_, bf16[96,1152]{1,0:T(8,128)(2,1)S(1)} %collective-permute-done.3.refs_1_, bf16[96,1152]{1,0:T(8,128)(2,1)S(1)} %collective-permute-done.7.refs_2_, bf16[96,1152]{1,0:T(8,128)(2,1)S(1)} %collective-permute-done.19.refs_3_, ...), custom_call_target="tpu_custom_call" | custom-call | flops 2038431744 | bytes 5308416 | tf_op jit(solution)/shard_map/pallas_call | solution.py:253
  (14 shorter events, 0.1 us)
Async XLA Ops:
  0.0 5.9 %collective-permute-start.10 = (bf16[96,1152]{1,0:T(8,128)(2,1)}, bf16[96,1152]{1,0:T(8,128)(2,1)S(1)}, u32[]{:S(2)}, u32[]{:S(2)}) collective-permute-start(bf16[96,1152]{1,0:T(8,128)(2,1)} %refs_0_.1), channel_id=1, source_target_pairs={{0,1},{1,0},{2,3},{3,2},{4,5},{5,4},{6,7},{7,6},{8,9},{9,8},{10,11... | collective-permute-start | bytes 663560 | tf_op jit(solution)/shard_map/ppermute | solution.py:185
  0.5 10.5 %collective-permute-start.4 = (bf16[96,1152]{1,0:T(8,128)(2,1)}, bf16[96,1152]{1,0:T(8,128)(2,1)S(1)}, u32[]{:S(2)}, u32[]{:S(2)}) collective-permute-start(bf16[96,1152]{1,0:T(8,128)(2,1)} %refs_0_.1), channel_id=1, source_target_pairs={{0,4},{1,3},{4,8},{5,1},{8,12},{9,5},{12,14},{13,9},{14,10},{15,13... | collective-permute-start | bytes 663560 | tf_op jit(solution)/shard_map/ppermute | solution.py:185
  3.0 8.0 %collective-permute-start = (bf16[96,1152]{1,0:T(8,128)(2,1)}, bf16[96,1152]{1,0:T(8,128)(2,1)S(1)}, u32[]{:S(2)}, u32[]{:S(2)}) collective-permute-start(bf16[96,1152]{1,0:T(8,128)(2,1)} %refs_0_.1), channel_id=1, source_target_pairs={{1,4},{0,3},{5,8},{4,1},{9,12},{8,5},{13,14},{12,9},{15,10},{14,13... | collective-permute-start | bytes 663560 | tf_op jit(solution)/shard_map/ppermute | solution.py:185
  5.9 5.2 %collective-permute-start.11 = (bf16[16,128]{1,0:T(8,128)(2,1)}, bf16[16,128]{1,0:T(8,128)(2,1)S(1)}, u32[]{:S(2)}, u32[]{:S(2)}) collective-permute-start(bf16[16,128]{1,0:T(8,128)(2,1)} %shard_map.82), channel_id=1, source_target_pairs={{0,4},{1,5},{2,6},{3,7},{4,0},{5,1},{6,2},{7,3},{8,12},{9,13},{10,... | collective-permute-start | bytes 12296 | tf_op jit(solution)/shard_map/ppermute | solution.py:185
  6.3 5.3 %collective-permute-start.12 = (bf16[16,128]{1,0:T(8,128)(2,1)}, bf16[16,128]{1,0:T(8,128)(2,1)S(1)}, u32[]{:S(2)}, u32[]{:S(2)}) collective-permute-start(bf16[16,128]{1,0:T(8,128)(2,1)} %shard_map.82), channel_id=1, source_target_pairs={{0,8},{1,9},{2,10},{3,11},{4,12},{5,13},{6,14},{7,15},{8,0},{9,1},... | collective-permute-start | bytes 12296 | tf_op jit(solution)/shard_map/ppermute | solution.py:185
  8.6 5.7 %collective-permute-start.13 = (bf16[16,128]{1,0:T(8,128)(2,1)}, bf16[16,128]{1,0:T(8,128)(2,1)S(1)}, u32[]{:S(2)}, u32[]{:S(2)}) collective-permute-start(bf16[16,128]{1,0:T(8,128)(2,1)} %shard_map.82), channel_id=1, source_target_pairs={{0,12},{1,13},{2,14},{3,15},{4,8},{5,9},{6,10},{7,11},{8,4},{9,5},... | collective-permute-start | bytes 12296 | tf_op jit(solution)/shard_map/ppermute | solution.py:185
  11.0 6.1 %collective-permute-start.5 = (bf16[96,1152]{1,0:T(8,128)(2,1)S(1)}, bf16[96,1152]{1,0:T(8,128)(2,1)S(1)}, u32[]{:S(2)}, u32[]{:S(2)}) collective-permute-start(bf16[96,1152]{1,0:T(8,128)(2,1)S(1)} %collective-permute-done.4.refs_2_), channel_id=1, source_target_pairs={{0,4},{1,3},{4,8},{5,1},{8,12},{9,5},{12,14},{13,9},{14,10},{15,13... | collective-permute-start | bytes 663560 | tf_op jit(solution)/shard_map/ppermute | solution.py:185
  11.0 10.1 %collective-permute-start.16 = (bf16[96,1152]{1,0:T(8,128)(2,1)S(1)}, bf16[96,1152]{1,0:T(8,128)(2,1)S(1)}, u32[]{:S(2)}, u32[]{:S(2)}) collective-permute-start(bf16[96,1152]{1,0:T(8,128)(2,1)S(1)} %collective-permute-done.4.refs_2_), channel_id=1, source_target_pairs={{0,1},{1,0},{2,3},{3,2},{4,5},{5,4},{6,7},{7,6},{8,9},{9,8},{10,11... | collective-permute-start | bytes 663560 | tf_op jit(solution)/shard_map/ppermute | solution.py:185
  11.1 12.0 %collective-permute-start.17 = (bf16[96,1152]{1,0:T(8,128)(2,1)S(1)}, bf16[96,1152]{1,0:T(8,128)(2,1)S(1)}, u32[]{:S(2)}, u32[]{:S(2)}) collective-permute-start(bf16[96,1152]{1,0:T(8,128)(2,1)S(1)} %collective-permute-done.refs_4_), channel_id=1, source_target_pairs={{0,1},{1,0},{2,3},{3,2},{4,5},{5,4},{6,7},{7,6},{8,9},{9,8},{10,11... | collective-permute-start | bytes 663560 | tf_op jit(solution)/shard_map/ppermute | solution.py:185
  11.6 8.1 %collective-permute-start.1 = (bf16[96,1152]{1,0:T(8,128)(2,1)S(1)}, bf16[96,1152]{1,0:T(8,128)(2,1)S(1)}, u32[]{:S(2)}, u32[]{:S(2)}) collective-permute-start(bf16[96,1152]{1,0:T(8,128)(2,1)S(1)} %collective-permute-done.refs_4_), channel_id=1, source_target_pairs={{0,4},{1,3},{4,8},{5,1},{8,12},{9,5},{12,14},{13,9},{14,10},{15,13... | collective-permute-start | bytes 663560 | tf_op jit(solution)/shard_map/ppermute | solution.py:185
  15.0 4.7 %collective-permute-start.14 = (bf16[64,128]{1,0:T(8,128)(2,1)S(1)}, bf16[64,128]{1,0:T(8,128)(2,1)S(1)}, u32[]{:S(2)}, u32[]{:S(2)}) collective-permute-start(bf16[64,128]{1,0:T(8,128)(2,1)S(1)} %pad_maximum_fusion), channel_id=1, source_target_pairs={{0,2},{1,3},{2,0},{3,1},{4,6},{5,7},{6,4},{7,5},{8,10},{9,11},{10,... | collective-permute-start | bytes 49160 | tf_op jit(solution)/shard_map/ppermute | solution.py:185
  17.1 5.9 %collective-permute-start.6 = (bf16[96,1152]{1,0:T(8,128)(2,1)S(1)}, bf16[96,1152]{1,0:T(8,128)(2,1)S(1)}, u32[]{:S(2)}, u32[]{:S(2)}) collective-permute-start(bf16[96,1152]{1,0:T(8,128)(2,1)S(1)} %collective-permute-done.5.refs_6_), channel_id=1, source_target_pairs={{0,4},{1,3},{4,8},{5,1},{8,12},{9,5},{12,14},{13,9},{14,10},{15,13... | collective-permute-start | bytes 663560 | tf_op jit(solution)/shard_map/ppermute | solution.py:185
  19.7 1.3 %collective-permute-start.15 = (bf16[128,128]{1,0:T(8,128)(2,1)S(1)}, bf16[128,128]{1,0:T(8,128)(2,1)S(1)}, u32[]{:S(2)}, u32[]{:S(2)}) collective-permute-start(bf16[128,128]{1,0:T(8,128)(2,1)S(1)} %get-tuple-element.17), channel_id=1, source_target_pairs={{0,1},{1,0},{2,3},{3,2},{4,5},{5,4},{6,7},{7,6},{8,9},{9,8},{10,11... | collective-permute-start | bytes 98312 | tf_op jit(solution)/shard_map/ppermute | solution.py:185
  19.7 6.0 %collective-permute-start.2 = (bf16[96,1152]{1,0:T(8,128)(2,1)S(1)}, bf16[96,1152]{1,0:T(8,128)(2,1)S(1)}, u32[]{:S(2)}, u32[]{:S(2)}) collective-permute-start(bf16[96,1152]{1,0:T(8,128)(2,1)S(1)} %collective-permute-done.1.refs_0_), channel_id=1, source_target_pairs={{0,4},{1,3},{4,8},{5,1},{8,12},{9,5},{12,14},{13,9},{14,10},{15,13... | collective-permute-start | bytes 663560 | tf_op jit(solution)/shard_map/ppermute | solution.py:185
  20.9 5.1 %collective-permute-start.18 = (bf16[96,1152]{1,0:T(8,128)(2,1)S(1)}, bf16[96,1152]{1,0:T(8,128)(2,1)S(1)}, u32[]{:S(2)}, u32[]{:S(2)}) collective-permute-start(bf16[96,1152]{1,0:T(8,128)(2,1)S(1)} %collective-permute-done.5.refs_6_), channel_id=1, source_target_pairs={{0,1},{1,0},{2,3},{3,2},{4,5},{5,4},{6,7},{7,6},{8,9},{9,8},{10,11... | collective-permute-start | bytes 663560 | tf_op jit(solution)/shard_map/ppermute | solution.py:185
  21.1 7.7 %collective-permute-start.8 = (bf16[96,1152]{1,0:T(8,128)(2,1)S(1)}, bf16[96,1152]{1,0:T(8,128)(2,1)S(1)}, u32[]{:S(2)}, u32[]{:S(2)}) collective-permute-start(bf16[96,1152]{1,0:T(8,128)(2,1)S(1)} %collective-permute-done.1.refs_0_), channel_id=1, source_target_pairs={{0,1},{1,0},{2,3},{3,2},{4,5},{5,4},{6,7},{7,6},{8,9},{9,8},{10,11... | collective-permute-start | bytes 663560 | tf_op jit(solution)/shard_map/ppermute | solution.py:185
  23.0 5.7 %collective-permute-start.9 = (bf16[96,1152]{1,0:T(8,128)(2,1)S(1)}, bf16[96,1152]{1,0:T(8,128)(2,1)S(1)}, u32[]{:S(2)}, u32[]{:S(2)}) collective-permute-start(bf16[96,1152]{1,0:T(8,128)(2,1)S(1)} %collective-permute-done.6.refs_2_), channel_id=1, source_target_pairs={{0,1},{1,0},{2,3},{3,2},{4,5},{5,4},{6,7},{7,6},{8,9},{9,8},{10,11... | collective-permute-start | bytes 663560 | tf_op jit(solution)/shard_map/ppermute | solution.py:185
  23.0 7.2 %collective-permute-start.7 = (bf16[96,1152]{1,0:T(8,128)(2,1)S(1)}, bf16[96,1152]{1,0:T(8,128)(2,1)S(1)}, u32[]{:S(2)}, u32[]{:S(2)}) collective-permute-start(bf16[96,1152]{1,0:T(8,128)(2,1)S(1)} %collective-permute-done.6.refs_2_), channel_id=1, source_target_pairs={{0,4},{1,3},{4,8},{5,1},{8,12},{9,5},{12,14},{13,9},{14,10},{15,13... | collective-permute-start | bytes 663560 | tf_op jit(solution)/shard_map/ppermute | solution.py:185
  25.7 4.8 %collective-permute-start.3 = (bf16[96,1152]{1,0:T(8,128)(2,1)S(1)}, bf16[96,1152]{1,0:T(8,128)(2,1)S(1)}, u32[]{:S(2)}, u32[]{:S(2)}) collective-permute-start(bf16[96,1152]{1,0:T(8,128)(2,1)S(1)} %collective-permute-done.2.refs_0_), channel_id=1, source_target_pairs={{0,1},{1,0},{2,3},{3,2},{4,5},{5,4},{6,7},{7,6},{8,9},{9,8},{10,11... | collective-permute-start | bytes 663560 | tf_op jit(solution)/shard_map/ppermute | solution.py:185
  26.0 0.9 %copy-start.4 = (bf16[96,1152]{1,0:T(8,128)(2,1)S(1)}, bf16[96,1152]{1,0:T(8,128)(2,1)}, u32[]{:S(2)}) copy-start(bf16[96,1152]{1,0:T(8,128)(2,1)} %refs_0_.1) | copy-start | bytes 663556
  28.7 3.1 %copy-start = (bf16[1152,576]{0,1:T(8,128)(2,1)S(1)}, bf16[1152,576]{0,1:T(8,128)(2,1)}, u32[]{:S(2)}) copy-start(bf16[1152,576]{0,1:T(8,128)(2,1)} %param.12) | copy-start | bytes 3981316
  28.7 3.1 %copy-start.1 = (bf16[1152,576]{0,1:T(8,128)(2,1)S(1)}, bf16[1152,576]{0,1:T(8,128)(2,1)}, u32[]{:S(2)}) copy-start(bf16[1152,576]{0,1:T(8,128)(2,1)} %param.13) | copy-start | bytes 3981316
  28.7 3.1 %copy-start.2 = (bf16[1152,576]{0,1:T(8,128)(2,1)S(1)}, bf16[1152,576]{0,1:T(8,128)(2,1)}, u32[]{:S(2)}) copy-start(bf16[1152,576]{0,1:T(8,128)(2,1)} %param.14) | copy-start | bytes 3981316
  28.8 3.0 %copy-start.3 = (bf16[576,1152]{1,0:T(8,128)(2,1)S(1)}, bf16[576,1152]{1,0:T(8,128)(2,1)}, u32[]{:S(2)}) copy-start(bf16[576,1152]{1,0:T(8,128)(2,1)} %refs_12_.1) | copy-start | bytes 3981316
  30.3 1.5 %collective-permute-start.19 = (bf16[96,1152]{1,0:T(8,128)(2,1)S(1)}, bf16[96,1152]{1,0:T(8,128)(2,1)S(1)}, u32[]{:S(2)}, u32[]{:S(2)}) collective-permute-start(bf16[96,1152]{1,0:T(8,128)(2,1)S(1)} %collective-permute-done.7.refs_2_), channel_id=1, source_target_pairs={{0,1},{1,0},{2,3},{3,2},{4,5},{5,4},{6,7},{7,6},{8,9},{9,8},{10,11... | collective-permute-start | bytes 663560 | tf_op jit(solution)/shard_map/ppermute | solution.py:185

commit v3 on v2

--- a/solution.py
+++ b/solution.py
@@ -59,7 +59,8 @@
     found = [me, me ^ 1]
     for s in range(1, rows):
         found += [at(d * s, core), at(-d * s, swapped), at(d * s, swapped), at(-d * s, core)]
-    return found + [at(d * rows, core), at(-d * rows, swapped)]
+    found += [at(d * rows, core), at(-d * rows, swapped)]
+    return found[1 : 1 + shards // 2] + [me] + found[1 + shards // 2 :]
 
 
 def flip(x, shards):
@@ -89,7 +90,7 @@
 
 def prep_kernel(
     shards, slots, tok, merged_rows, g_ref,
-    m_ref, inv_ref, bias_ref, pick_ref, gf, dest_row, size_row,
+    m_ref, inv_ref, bias_ref, gf, dest_row, size_row,
 ):
     me = lax.axis_index("ctx")
     me_flipped = flip(me, shards)
@@ -110,21 +111,23 @@
         dest = own.astype(F32) * merged_rows + slot
         dest_row[:, j * tok : (j + 1) * tok] = dest[:, :tok]
         size_row[:, j * tok : (j + 1) * tok] = size[:, :tok]
-    places_iota = lax.broadcasted_iota(jnp.int32, (total, LANES), 0).astype(F32)
-    count = jnp.zeros((total, LANES), F32)
+        if j == shards // 2:
+            mine = dest
+    mine = jnp.broadcast_to(mine, (8, LANES))
+    mine = jnp.transpose(mine, (1, 0))[:tok, 0:1]
+    mine = jnp.broadcast_to(mine, (tok, LANES))
+    slot_of_row = lax.broadcasted_iota(jnp.int32, (total, LANES), 0).astype(F32)
+    slot_of_row = jnp.concatenate([slot_of_row, mine], axis=0)
+    count = jnp.zeros(slot_of_row.shape, F32)
     for b in range(shards * tok // LANES):
         cols = slice(b * LANES, (b + 1) * LANES)
-        piece = jnp.where(places_iota == dest_row[:, cols], size_row[:, cols], 0.0)
+        piece = jnp.where(slot_of_row == dest_row[:, cols], size_row[:, cols], 0.0)
         count = count + piece
         m_ref[:, cols] = piece.astype(BF16)
     inv_ref[...] = 1.0 / jnp.maximum(jnp.sum(count, axis=1, keepdims=True), 1.0)
-    count_row = dot(jnp.ones((8, LANES), BF16), count.astype(BF16), NT)[0:1]
+    count_row = dot(jnp.ones((8, LANES), BF16), count[:total].astype(BF16), NT)[0:1]
     bias = jnp.where(count_row > 0, jnp.log(jnp.maximum(count_row, 1.0)), -1e30)
     bias_ref[...] = bias.astype(BF16).astype(F32)
-    mine = jnp.broadcast_to(dest_row[:, :LANES], (8, LANES))
-    mine = jnp.transpose(mine, (1, 0))[:tok, 0:1]
-    lane = lax.broadcasted_iota(jnp.int32, (tok, total), 1).astype(F32)
-    pick_ref[...] = jnp.where(lane == mine, 1.0, 0.0).astype(BF16)
 
 
 def cost(flops, nbytes):
@@ -147,18 +150,18 @@
 
 def tail_kernel(n_blocks, first, *refs):
     blocks = refs[:n_blocks]
-    (acc_ref, m_ref, inv_ref, bias_ref, pick_ref, wq_ref, wk_ref, wv_ref, wo_ref, out_ref,
+    (acc_ref, m_ref, inv_ref, bias_ref, wq_ref, wk_ref, wv_ref, wo_ref, out_ref,
      tok_s, merged_s, att_s) = refs[n_blocks:]
     gather_blocks(blocks, tok_s)
     acc = acc_ref[...] + dot(m_ref[:, first:], tok_s[...])
     merged_s[...] = (acc * inv_ref[...]).astype(BF16)
-    merged = merged_s[...]
-    picked = dot(pick_ref[...], merged).astype(BF16)
-    q_t = dot(wq_ref[...], picked, NT)
+    total = bias_ref.shape[1]
+    merged = merged_s[:total, :]
+    q_t = dot(wq_ref[...], merged_s[total:, :], NT)
+    k_t = dot(wk_ref[...], merged, NT)
+    v_t = dot(wv_ref[...], merged, NT)
     inverse = 1.0 / math.sqrt(HEAD)
     bias = bias_ref[...]
-    k_t = dot(wk_ref[...], merged, NT)
-    v_t = dot(wv_ref[...], merged, NT)
     for h in range(HEADS):
         rows = slice(h * HEAD, (h + 1) * HEAD)
         scores = dot(q_t[rows].astype(BF16), k_t[rows].astype(BF16), TN) * inverse + bias
@@ -215,54 +218,58 @@
         a = send(a, along)
         if s < shards // 4 - 1:
             b = send(b, along)
-    m, inv, bias, pick = pl.pallas_call(
+    rows = total + tok
+    m, inv, bias = pl.pallas_call(
         functools.partial(prep_kernel, shards, slots, tok, merged_rows),
         out_shape=(
-            jax.ShapeDtypeStruct((total, shards * tok), BF16),
-            jax.ShapeDtypeStruct((total, 1), F32),
+            jax.ShapeDtypeStruct((rows, shards * tok), BF16),
+            jax.ShapeDtypeStruct((rows, 1), F32),
             jax.ShapeDtypeStruct((1, total), F32),
-            jax.ShapeDtypeStruct((tok, total), BF16),
         ),
         in_specs=[vmem],
-        out_specs=(vmem,) * 4,
+        out_specs=(vmem,) * 3,
         scratch_shapes=[
             pltpu.VMEM((shards * META, LANES), F32),
             pltpu.VMEM((1, shards * tok), F32),
             pltpu.VMEM((1, shards * tok), F32),
         ],
         compiler_params=pltpu.CompilerParams(vmem_limit_bytes=VMEM_PREP),
+        cost_estimate=cost(1000, 1000),
     )(jnp.concatenate(metas, axis=0))
-    cuts = [0, shards // 2, shards - 4, shards]
+    blocks = blocks[1 : 1 + shards // 2] + [tokens] + blocks[1 + shards // 2 :]
+    cuts = [0, shards // 2, shards - 1, shards]
     acc = []
     for low, high in zip(cuts[:-2], cuts[1:-1]):
         n = high - low
         acc = [
             pl.pallas_call(
                 functools.partial(merge_kernel, n, low * tok),
-                out_shape=jax.ShapeDtypeStruct((total, width), F32),
+                out_shape=jax.ShapeDtypeStruct((rows, width), F32),
                 in_specs=[vmem] * (n + 1 + len(acc)),
                 out_specs=vmem,
                 scratch_shapes=[pltpu.VMEM((n * tok, width), BF16)],
                 input_output_aliases={n + 1: 0} if acc else {},
                 compiler_params=pltpu.CompilerParams(vmem_limit_bytes=VMEM_MERGE),
+                cost_estimate=cost(1000, 1000),
             )(*blocks[low:high], m, *acc)
         ]
-    blocks += [a, send(a, swap, *acc)]
+        if low == 0:
+            blocks += [a, send(a, swap, *acc)]
     low, high = cuts[-2:]
     n = high - low
     return pl.pallas_call(
         functools.partial(tail_kernel, n, low * tok),
         out_shape=jax.ShapeDtypeStruct((tok, width), BF16),
-        in_specs=[vmem] * (n + 9),
+        in_specs=[vmem] * (n + 8),
         out_specs=vmem,
         scratch_shapes=[
             pltpu.VMEM((n * tok, width), BF16),
-            pltpu.VMEM((total, width), BF16),
+            pltpu.VMEM((rows, width), BF16),
             pltpu.VMEM((tok, HEADS * HEAD), F32),
         ],
         compiler_params=pltpu.CompilerParams(vmem_limit_bytes=VMEM_TAIL),
         cost_estimate=cost(4 * total * width * HEADS * HEAD, 8 * width * HEADS * HEAD),
-    )(*blocks[low:high], *acc, m, inv, bias, pick, w_query.T, w_key.T, w_value.T, w_out)
+    )(*blocks[low:high], *acc, m, inv, bias, w_query.T, w_key.T, w_value.T, w_out)
 
 
 def on_device_exchanged(tokens, owner, slot_map, sizes, w_query, w_key, w_value, w_out):

time: 39.1 us -> 38 us (0.972)
  local copies, waits for them, and re-layouts: 1.73 us -> 0.79 us
  Pallas kernels: 12.9 us -> 13.3 us
    pallas_call x2, Pallas kernels: 3.2 us -> 4.29 us  [on_device_gathered(): pl.pallas_call(functools.partial(merge_kernel, n, low * tok), out_shape=j...]
    unnamed x14, local copies, waits for them, and re-layouts: 1.71 us -> 0.77 us
    pallas_call x1, Pallas kernels: 6.98 us -> 6.27 us  [on_device_gathered(): pl.pallas_call(functools.partial(tail_kernel, n, low * tok), out_shape=ja...]
  transfers between devices with their start and end apart: 20 -> 20, of which waited for: 7 -> 7; matrix products, arithmetic and copies ran while one was open for 4% -> 4% of each run, Pallas kernels for 15% -> 19%
where the time goes in v3:
time: 38 us; the launch traced here: 37.7 us
  Pallas kernels  13.3 us (35%)
  starting transfers between devices  12 us (32%)
  waiting for transfers between devices  10.7 us (28%)
  local copies, waits for them, and re-layouts  0.79 us (2%)
  other arithmetic  0.69 us (2%)
    ppermute x20, starting transfers between devices, send(): return lax.ppermute(x, 'ctx', pairs)  12 us
    ppermute x20, waiting for transfers between devices, send(): return lax.ppermute(x, 'ctx', pairs)  10.7 us
    pallas_call x1, Pallas kernels, on_device_gathered(): pl.pallas_call(functools.partial(tail_kernel, n, low * tok), out_shape=ja...  6.27 us
    pallas_call x2, Pallas kernels, on_device_gathered(): pl.pallas_call(functools.partial(merge_kernel, n, low * tok), out_shape=j...  4.29 us
    pallas_call x1, Pallas kernels, on_device_gathered(): pl.pallas_call(functools.partial(meta_kernel, slots), out_shape=jax.Shape...  1.5 us
    pallas_call x1, Pallas kernels, on_device_gathered(): pl.pallas_call(functools.partial(prep_kernel, shards, slots, tok, merged_...  1.26 us
    unnamed x14, local copies, waits for them, and re-layouts  0.77 us
  transfers between devices with their start and end apart: 20, of which 7 were waited for; matrix products, arithmetic and copies ran while one was open for 4% of the time, Pallas kernels for 19%

profile of v3, /device:TPU:0, one launch (start us, length us, event | category | flops | bytes accessed | tf_op | source)
XLA Modules:
  0.0 37.7 jit_solution(8094152968229036165)
XLA Ops:
  0.0 0.5 %collective-permute-start.4 = (bf16[96,1152]{1,0:T(8,128)(2,1)}, bf16[96,1152]{1,0:T(8,128)(2,1)S(1)}, u32[]{:S(2)}, u32[]{:S(2)}) collective-permute-start(bf16[96,1152]{1,0:T(8,128)(2,1)} %refs_0_.1), channel_id=1, source_target_pairs={{0,1},{1,0},{2,3},{3,2},{4,5},{5,4},{6,7},{7,6},{8,9},{9,8},{10,11... | collective-permute-start | bytes 663560 | tf_op jit(solution)/shard_map/ppermute | solution.py:188
  0.5 2.6 %collective-permute-start = (bf16[96,1152]{1,0:T(8,128)(2,1)}, bf16[96,1152]{1,0:T(8,128)(2,1)S(1)}, u32[]{:S(2)}, u32[]{:S(2)}) collective-permute-start(bf16[96,1152]{1,0:T(8,128)(2,1)} %refs_0_.1), channel_id=1, source_target_pairs={{0,4},{1,3},{4,8},{5,1},{8,12},{9,5},{12,14},{13,9},{14,10},{15,13... | collective-permute-start | bytes 663560 | tf_op jit(solution)/shard_map/ppermute | solution.py:188
  3.0 1.4 %collective-permute-start.6 = (bf16[96,1152]{1,0:T(8,128)(2,1)}, bf16[96,1152]{1,0:T(8,128)(2,1)S(1)}, u32[]{:S(2)}, u32[]{:S(2)}) collective-permute-start(bf16[96,1152]{1,0:T(8,128)(2,1)} %refs_0_.1), channel_id=1, source_target_pairs={{1,4},{0,3},{5,8},{4,1},{9,12},{8,5},{13,14},{12,9},{15,10},{14,13... | collective-permute-start | bytes 663560 | tf_op jit(solution)/shard_map/ppermute | solution.py:188
  4.4 1.5 %shard_map.82 = bf16[16,128]{1,0:T(8,128)(2,1)} custom-call(s32[1,96]{1,0:T(1,128)} %bitcast.10, s32[1,96]{1,0:T(1,128)} %bitcast.11, s32[12,1,16]{2,1,0:T(1,128)} %bitcast.9), custom_call_target="tpu_custom_call" | custom-call | tf_op jit(solution)/shard_map/pallas_call | solution.py:192
  5.9 0.0 collective-permute-done.4.refs_0_
  5.9 0.5 %collective-permute-start.10 = (bf16[16,128]{1,0:T(8,128)(2,1)}, bf16[16,128]{1,0:T(8,128)(2,1)S(1)}, u32[]{:S(2)}, u32[]{:S(2)}) collective-permute-start(bf16[16,128]{1,0:T(8,128)(2,1)} %shard_map.82), channel_id=1, source_target_pairs={{0,4},{1,5},{2,6},{3,7},{4,0},{5,1},{6,2},{7,3},{8,12},{9,13},{10,... | collective-permute-start | bytes 12296 | tf_op jit(solution)/shard_map/ppermute | solution.py:188
  6.3 2.3 %collective-permute-start.11 = (bf16[16,128]{1,0:T(8,128)(2,1)}, bf16[16,128]{1,0:T(8,128)(2,1)S(1)}, u32[]{:S(2)}, u32[]{:S(2)}) collective-permute-start(bf16[16,128]{1,0:T(8,128)(2,1)} %shard_map.82), channel_id=1, source_target_pairs={{0,8},{1,9},{2,10},{3,11},{4,12},{5,13},{6,14},{7,15},{8,0},{9,1},... | collective-permute-start | bytes 12296 | tf_op jit(solution)/shard_map/ppermute | solution.py:188
  8.6 1.6 %collective-permute-start.12 = (bf16[16,128]{1,0:T(8,128)(2,1)}, bf16[16,128]{1,0:T(8,128)(2,1)S(1)}, u32[]{:S(2)}, u32[]{:S(2)}) collective-permute-start(bf16[16,128]{1,0:T(8,128)(2,1)} %shard_map.82), channel_id=1, source_target_pairs={{0,12},{1,13},{2,14},{3,15},{4,8},{5,9},{6,10},{7,11},{8,4},{9,5},... | collective-permute-start | bytes 12296 | tf_op jit(solution)/shard_map/ppermute | solution.py:188
  10.3 0.7 %constant_dynamic-update-slice_fusion.4 = (bf16[128,128]{1,0:T(8,128)(2,1)S(1)}, bf16[256,128]{1,0:T(8,128)(2,1)S(1)}) fusion(bf16[16,128]{1,0:T(8,128)(2,1)} %shard_map.82), kind=kLoop, calls=%fused_computation.4 | loop fusion | bytes 12288
  11.0 0.0 collective-permute-done.refs_1_
  11.0 0.0 collective-permute-start.1
  11.0 0.0 collective-permute-done.6.refs_3_
  11.0 1.1 %collective-permute-start.9 = (bf16[96,1152]{1,0:T(8,128)(2,1)S(1)}, bf16[96,1152]{1,0:T(8,128)(2,1)S(1)}, u32[]{:S(2)}, u32[]{:S(2)}) collective-permute-start(bf16[96,1152]{1,0:T(8,128)(2,1)S(1)} %collective-permute-done.6.refs_3_), channel_id=1, source_target_pairs={{0,4},{1,3},{4,8},{5,1},{8,12},{9,5},{12,14},{13,9},{14,10},{15,13... | collective-permute-start | bytes 663560 | tf_op jit(solution)/shard_map/ppermute | solution.py:188
  12.1 0.0 collective-permute-done.10
  12.1 0.0 collective-permute-done.11
  12.1 2.2 %collective-permute-done.12 = bf16[16,128]{1,0:T(8,128)(2,1)S(1)} collective-permute-done((bf16[16,128]{1,0:T(8,128)(2,1)}, bf16[16,128]{1,0:T(8,128)(2,1)S(1)}, u32[]{:S(2)}, u32[]{:S(2)}) %collective-permute-start.12) | collective-permute-done | bytes 4128 | tf_op jit(solution)/shard_map/ppermute | solution.py:188
  14.3 0.7 %pad_maximum_fusion = bf16[64,128]{1,0:T(8,128)(2,1)S(1)} fusion(bf16[16,128]{1,0:T(8,128)(2,1)S(1)} %collective-permute-done.12, bf16[16,128]{1,0:T(8,128)(2,1)S(1)} %collective-permute-done.11, bf16[16,128]{1,0:T(8,128)(2,1)S(1)} %collective-permute-done.10, bf16[16,128]{1,0:T(8,128)(2,1)} %shard_map.82), kind=kLoop, calls=%fused_computation.11 | loop fusion | flops 65536 | bytes 32768 | tf_op jit(solution)/shard_map/concatenate | solution.py:212
  15.0 0.7 %collective-permute-start.13 = (bf16[64,128]{1,0:T(8,128)(2,1)S(1)}, bf16[64,128]{1,0:T(8,128)(2,1)S(1)}, u32[]{:S(2)}, u32[]{:S(2)}) collective-permute-start(bf16[64,128]{1,0:T(8,128)(2,1)S(1)} %pad_maximum_fusion), channel_id=1, source_target_pairs={{0,2},{1,3},{2,0},{3,1},{4,6},{5,7},{6,4},{7,5},{8,10},{9,11},{10,... | collective-permute-start | bytes 49160 | tf_op jit(solution)/shard_map/ppermute | solution.py:188
  15.8 1.4 %collective-permute-done.1.refs_5_ = bf16[96,1152]{1,0:T(8,128)(2,1)S(1)} collective-permute-done((bf16[96,1152]{1,0:T(8,128)(2,1)S(1)}, bf16[96,1152]{1,0:T(8,128)(2,1)S(1)}, u32[]{:S(2)}, u32[]{:S(2)}) %collective-permute-start.1) | collective-permute-done | bytes 221216 | tf_op jit(solution)/shard_map/ppermute | solution.py:188
  17.1 0.0 collective-permute-start.2
  17.1 2.5 %collective-permute-done.13 = bf16[64,128]{1,0:T(8,128)(2,1)S(1)} collective-permute-done((bf16[64,128]{1,0:T(8,128)(2,1)S(1)}, bf16[64,128]{1,0:T(8,128)(2,1)S(1)}, u32[]{:S(2)}, u32[]{:S(2)}) %collective-permute-start.13) | collective-permute-done | bytes 16416 | tf_op jit(solution)/shard_map/ppermute | solution.py:188
  19.7 0.1 collective-permute-start.14
  19.7 0.5 %collective-permute-start.5 = (bf16[96,1152]{1,0:T(8,128)(2,1)S(1)}, bf16[96,1152]{1,0:T(8,128)(2,1)S(1)}, u32[]{:S(2)}, u32[]{:S(2)}) collective-permute-start(bf16[96,1152]{1,0:T(8,128)(2,1)S(1)} %collective-permute-done.refs_1_), channel_id=1, source_target_pairs={{0,1},{1,0},{2,3},{3,2},{4,5},{5,4},{6,7},{7,6},{8,9},{9,8},{10,11... | collective-permute-start | bytes 663560 | tf_op jit(solution)/shard_map/ppermute | solution.py:188
  20.2 0.1 collective-permute-start.7
  20.3 0.0 collective-permute-done.9.refs_7_
  20.3 0.0 collective-permute-start.18
  20.3 0.6 %collective-permute-done.14 = bf16[128,128]{1,0:T(8,128)(2,1)S(1)} collective-permute-done((bf16[128,128]{1,0:T(8,128)(2,1)S(1)}, bf16[128,128]{1,0:T(8,128)(2,1)S(1)}, u32[]{:S(2)}, u32[]{:S(2)}) %collective-permute-start.14) | collective-permute-done | bytes 32800 | tf_op jit(solution)/shard_map/ppermute | solution.py:188
  20.9 0.2 collective-permute-start.8
  21.1 1.9 %collective-permute-done.2.refs_2_ = bf16[96,1152]{1,0:T(8,128)(2,1)S(1)} collective-permute-done((bf16[96,1152]{1,0:T(8,128)(2,1)S(1)}, bf16[96,1152]{1,0:T(8,128)(2,1)S(1)}, u32[]{:S(2)}, u32[]{:S(2)}) %collective-permute-start.2) | collective-permute-done | bytes 221216 | tf_op jit(solution)/shard_map/ppermute | solution.py:188
  23.0 0.0 collective-permute-start.3
  23.1 1.3 %shard_map.83 = (bf16[864,1536]{1,0:T(8,128)(2,1)S(1)}, f32[864,1]{1,0:T(8,128)S(1)}, f32[1,768]{1,0:T(1,128)S(1)}) custom-call(bf16[256,128]{1,0:T(8,128)(2,1)S(1)} %constant_dynamic-update-slice_fusion.5.g_ref), custom_call_target="tpu_custom_call" | custom-call | flops 1000 | bytes 1000 | tf_op jit(solution)/shard_map/pallas_call | solution.py:222
  24.3 0.0 collective-permute-done.5.refs_2_
  24.3 0.1 collective-permute-start.16
  24.4 0.0 collective-permute-done.7.refs_4_
  24.4 0.5 %collective-permute-start.17 = (bf16[96,1152]{1,0:T(8,128)(2,1)S(1)}, bf16[96,1152]{1,0:T(8,128)(2,1)S(1)}, u32[]{:S(2)}, u32[]{:S(2)}) collective-permute-start(bf16[96,1152]{1,0:T(8,128)(2,1)S(1)} %collective-permute-done.2.refs_2_), channel_id=1, source_target_pairs={{0,1},{1,0},{2,3},{3,2},{4,5},{5,4},{6,7},{7,6},{8,9},{9,8},{10,11... | collective-permute-start | bytes 663560 | tf_op jit(solution)/shard_map/ppermute | solution.py:188
  24.9 1.3 %collective-permute-done.18.refs_4_ = bf16[96,1152]{1,0:T(8,128)(2,1)S(1)} collective-permute-done((bf16[96,1152]{1,0:T(8,128)(2,1)S(1)}, bf16[96,1152]{1,0:T(8,128)(2,1)S(1)}, u32[]{:S(2)}, u32[]{:S(2)}) %collective-permute-start.18) | collective-permute-done | bytes 221216 | tf_op jit(solution)/shard_map/ppermute | solution.py:188
  26.2 0.0 collective-permute-start.19
  26.2 0.0 collective-permute-done.8.refs_6_
  26.3 1.9 %shard_map.84.refs_8_ = f32[864,1152]{1,0:T(8,128)S(1)} custom-call(bf16[96,1152]{1,0:T(8,128)(2,1)S(1)} %collective-permute-done.4.refs_0_, bf16[96,1152]{1,0:T(8,128)(2,1)S(1)} %collective-permute-done.refs_1_, bf16[96,1152]{1,0:T(8,128)(2,1)S(1)} %collective-permute-done.5.refs_2_, bf16[96,1152]{1,0:T(8,128)(2,1)S(1)} %collective-permute-done.6.refs_3_, ...), custom_call_target="tpu_custom_call" | custom-call | flops 1000 | bytes 1000 | tf_op jit(solution)/shard_map/pallas_call | solution.py:245
  28.2 0.0 copy-start
  28.2 0.0 copy-start.1
  28.2 0.0 copy-start.2
  28.2 0.0 copy-start.3
  28.2 0.7 %collective-permute-done.3.refs_6_ = bf16[96,1152]{1,0:T(8,128)(2,1)S(1)} collective-permute-done((bf16[96,1152]{1,0:T(8,128)(2,1)S(1)}, bf16[96,1152]{1,0:T(8,128)(2,1)S(1)}, u32[]{:S(2)}, u32[]{:S(2)}) %collective-permute-start.3) | collective-permute-done | bytes 221216 | tf_op jit(solution)/shard_map/ppermute | solution.py:188
  29.0 0.0 collective-permute-start.15
  29.0 0.0 collective-permute-done.19.refs_5_
  29.0 2.4 %shard_map.85.refs_1_ = f32[864,1152]{1,0:T(8,128)S(1)} custom-call(bf16[96,1152]{1,0:T(8,128)(2,1)S(1)} %copy-done.4, bf16[96,1152]{1,0:T(8,128)(2,1)S(1)} %collective-permute-done.16.refs_1_, bf16[96,1152]{1,0:T(8,128)(2,1)S(1)} %collective-permute-done.2.refs_2_, ...), custom_call_target="tpu_custom_call", output_to_operand_aliasing={{}: (8, {})} | custom-call | flops 1000 | bytes 1000 | tf_op jit(solution)/shard_map/pallas_call | solution.py:245
  31.4 6.3 %shard_map.86 = bf16[96,1152]{1,0:T(8,128)(2,1)} custom-call(bf16[96,1152]{1,0:T(8,128)(2,1)S(1)} %collective-permute-done.15.refs_0_, f32[864,1152]{1,0:T(8,128)S(1)} %shard_map.85.refs_1_, bf16[864,1536]{1,0:T(8,128)(2,1)S(1)} %get-tuple-element.11.refs_8_.refs_7_.refs_2_, f32[864,1]{1,0:T(8,128)S(1)} %get-tuple-element.13.refs_3_, ...), custom_call_target="tpu_custom_call" | custom-call | flops 2038431744 | bytes 5308416 | tf_op jit(solution)/shard_map/pallas_call | solution.py:260
  (14 shorter events, 0.1 us)
Async XLA Ops:
  0.0 5.9 %collective-permute-start.4 = (bf16[96,1152]{1,0:T(8,128)(2,1)}, bf16[96,1152]{1,0:T(8,128)(2,1)S(1)}, u32[]{:S(2)}, u32[]{:S(2)}) collective-permute-start(bf16[96,1152]{1,0:T(8,128)(2,1)} %refs_0_.1), channel_id=1, source_target_pairs={{0,1},{1,0},{2,3},{3,2},{4,5},{5,4},{6,7},{7,6},{8,9},{9,8},{10,11... | collective-permute-start | bytes 663560 | tf_op jit(solution)/shard_map/ppermute | solution.py:188
  0.5 10.5 %collective-permute-start = (bf16[96,1152]{1,0:T(8,128)(2,1)}, bf16[96,1152]{1,0:T(8,128)(2,1)S(1)}, u32[]{:S(2)}, u32[]{:S(2)}) collective-permute-start(bf16[96,1152]{1,0:T(8,128)(2,1)} %refs_0_.1), channel_id=1, source_target_pairs={{0,4},{1,3},{4,8},{5,1},{8,12},{9,5},{12,14},{13,9},{14,10},{15,13... | collective-permute-start | bytes 663560 | tf_op jit(solution)/shard_map/ppermute | solution.py:188
  3.0 8.0 %collective-permute-start.6 = (bf16[96,1152]{1,0:T(8,128)(2,1)}, bf16[96,1152]{1,0:T(8,128)(2,1)S(1)}, u32[]{:S(2)}, u32[]{:S(2)}) collective-permute-start(bf16[96,1152]{1,0:T(8,128)(2,1)} %refs_0_.1), channel_id=1, source_target_pairs={{1,4},{0,3},{5,8},{4,1},{9,12},{8,5},{13,14},{12,9},{15,10},{14,13... | collective-permute-start | bytes 663560 | tf_op jit(solution)/shard_map/ppermute | solution.py:188
  5.9 6.2 %collective-permute-start.10 = (bf16[16,128]{1,0:T(8,128)(2,1)}, bf16[16,128]{1,0:T(8,128)(2,1)S(1)}, u32[]{:S(2)}, u32[]{:S(2)}) collective-permute-start(bf16[16,128]{1,0:T(8,128)(2,1)} %shard_map.82), channel_id=1, source_target_pairs={{0,4},{1,5},{2,6},{3,7},{4,0},{5,1},{6,2},{7,3},{8,12},{9,13},{10,... | collective-permute-start | bytes 12296 | tf_op jit(solution)/shard_map/ppermute | solution.py:188
  6.3 5.8 %collective-permute-start.11 = (bf16[16,128]{1,0:T(8,128)(2,1)}, bf16[16,128]{1,0:T(8,128)(2,1)S(1)}, u32[]{:S(2)}, u32[]{:S(2)}) collective-permute-start(bf16[16,128]{1,0:T(8,128)(2,1)} %shard_map.82), channel_id=1, source_target_pairs={{0,8},{1,9},{2,10},{3,11},{4,12},{5,13},{6,14},{7,15},{8,0},{9,1},... | collective-permute-start | bytes 12296 | tf_op jit(solution)/shard_map/ppermute | solution.py:188
  8.6 5.7 %collective-permute-start.12 = (bf16[16,128]{1,0:T(8,128)(2,1)}, bf16[16,128]{1,0:T(8,128)(2,1)S(1)}, u32[]{:S(2)}, u32[]{:S(2)}) collective-permute-start(bf16[16,128]{1,0:T(8,128)(2,1)} %shard_map.82), channel_id=1, source_target_pairs={{0,12},{1,13},{2,14},{3,15},{4,8},{5,9},{6,10},{7,11},{8,4},{9,5},... | collective-permute-start | bytes 12296 | tf_op jit(solution)/shard_map/ppermute | solution.py:188
  11.0 6.1 %collective-permute-start.1 = (bf16[96,1152]{1,0:T(8,128)(2,1)S(1)}, bf16[96,1152]{1,0:T(8,128)(2,1)S(1)}, u32[]{:S(2)}, u32[]{:S(2)}) collective-permute-start(bf16[96,1152]{1,0:T(8,128)(2,1)S(1)} %collective-permute-done.refs_1_), channel_id=1, source_target_pairs={{0,4},{1,3},{4,8},{5,1},{8,12},{9,5},{12,14},{13,9},{14,10},{15,13... | collective-permute-start | bytes 663560 | tf_op jit(solution)/shard_map/ppermute | solution.py:188
  11.0 9.3 %collective-permute-start.9 = (bf16[96,1152]{1,0:T(8,128)(2,1)S(1)}, bf16[96,1152]{1,0:T(8,128)(2,1)S(1)}, u32[]{:S(2)}, u32[]{:S(2)}) collective-permute-start(bf16[96,1152]{1,0:T(8,128)(2,1)S(1)} %collective-permute-done.6.refs_3_), channel_id=1, source_target_pairs={{0,4},{1,3},{4,8},{5,1},{8,12},{9,5},{12,14},{13,9},{14,10},{15,13... | collective-permute-start | bytes 663560 | tf_op jit(solution)/shard_map/ppermute | solution.py:188
  15.0 4.7 %collective-permute-start.13 = (bf16[64,128]{1,0:T(8,128)(2,1)S(1)}, bf16[64,128]{1,0:T(8,128)(2,1)S(1)}, u32[]{:S(2)}, u32[]{:S(2)}) collective-permute-start(bf16[64,128]{1,0:T(8,128)(2,1)S(1)} %pad_maximum_fusion), channel_id=1, source_target_pairs={{0,2},{1,3},{2,0},{3,1},{4,6},{5,7},{6,4},{7,5},{8,10},{9,11},{10,... | collective-permute-start | bytes 49160 | tf_op jit(solution)/shard_map/ppermute | solution.py:188
  17.1 5.9 %collective-permute-start.2 = (bf16[96,1152]{1,0:T(8,128)(2,1)S(1)}, bf16[96,1152]{1,0:T(8,128)(2,1)S(1)}, u32[]{:S(2)}, u32[]{:S(2)}) collective-permute-start(bf16[96,1152]{1,0:T(8,128)(2,1)S(1)} %collective-permute-done.1.refs_5_), channel_id=1, source_target_pairs={{0,4},{1,3},{4,8},{5,1},{8,12},{9,5},{12,14},{13,9},{14,10},{15,13... | collective-permute-start | bytes 663560 | tf_op jit(solution)/shard_map/ppermute | solution.py:188
  19.7 1.3 %collective-permute-start.14 = (bf16[128,128]{1,0:T(8,128)(2,1)S(1)}, bf16[128,128]{1,0:T(8,128)(2,1)S(1)}, u32[]{:S(2)}, u32[]{:S(2)}) collective-permute-start(bf16[128,128]{1,0:T(8,128)(2,1)S(1)} %get-tuple-element.15), channel_id=1, source_target_pairs={{0,1},{1,0},{2,3},{3,2},{4,5},{5,4},{6,7},{7,6},{8,9},{9,8},{10,11... | collective-permute-start | bytes 98312 | tf_op jit(solution)/shard_map/ppermute | solution.py:188
  19.7 4.6 %collective-permute-start.5 = (bf16[96,1152]{1,0:T(8,128)(2,1)S(1)}, bf16[96,1152]{1,0:T(8,128)(2,1)S(1)}, u32[]{:S(2)}, u32[]{:S(2)}) collective-permute-start(bf16[96,1152]{1,0:T(8,128)(2,1)S(1)} %collective-permute-done.refs_1_), channel_id=1, source_target_pairs={{0,1},{1,0},{2,3},{3,2},{4,5},{5,4},{6,7},{7,6},{8,9},{9,8},{10,11... | collective-permute-start | bytes 663560 | tf_op jit(solution)/shard_map/ppermute | solution.py:188
  20.2 4.2 %collective-permute-start.7 = (bf16[96,1152]{1,0:T(8,128)(2,1)S(1)}, bf16[96,1152]{1,0:T(8,128)(2,1)S(1)}, u32[]{:S(2)}, u32[]{:S(2)}) collective-permute-start(bf16[96,1152]{1,0:T(8,128)(2,1)S(1)} %collective-permute-done.6.refs_3_), channel_id=1, source_target_pairs={{0,1},{1,0},{2,3},{3,2},{4,5},{5,4},{6,7},{7,6},{8,9},{9,8},{10,11... | collective-permute-start | bytes 663560 | tf_op jit(solution)/shard_map/ppermute | solution.py:188
  20.3 5.9 %collective-permute-start.18 = (bf16[96,1152]{1,0:T(8,128)(2,1)S(1)}, bf16[96,1152]{1,0:T(8,128)(2,1)S(1)}, u32[]{:S(2)}, u32[]{:S(2)}) collective-permute-start(bf16[96,1152]{1,0:T(8,128)(2,1)S(1)} %collective-permute-done.9.refs_7_), channel_id=1, source_target_pairs={{0,4},{1,3},{4,8},{5,1},{8,12},{9,5},{12,14},{13,9},{14,10},{15,13... | collective-permute-start | bytes 663560 | tf_op jit(solution)/shard_map/ppermute | solution.py:188
  20.9 5.3 %collective-permute-start.8 = (bf16[96,1152]{1,0:T(8,128)(2,1)S(1)}, bf16[96,1152]{1,0:T(8,128)(2,1)S(1)}, u32[]{:S(2)}, u32[]{:S(2)}) collective-permute-start(bf16[96,1152]{1,0:T(8,128)(2,1)S(1)} %collective-permute-done.1.refs_5_), channel_id=1, source_target_pairs={{0,1},{1,0},{2,3},{3,2},{4,5},{5,4},{6,7},{7,6},{8,9},{9,8},{10,11... | collective-permute-start | bytes 663560 | tf_op jit(solution)/shard_map/ppermute | solution.py:188
  23.0 5.9 %collective-permute-start.3 = (bf16[96,1152]{1,0:T(8,128)(2,1)S(1)}, bf16[96,1152]{1,0:T(8,128)(2,1)S(1)}, u32[]{:S(2)}, u32[]{:S(2)}) collective-permute-start(bf16[96,1152]{1,0:T(8,128)(2,1)S(1)} %collective-permute-done.2.refs_2_), channel_id=1, source_target_pairs={{0,4},{1,3},{4,8},{5,1},{8,12},{9,5},{12,14},{13,9},{14,10},{15,13... | collective-permute-start | bytes 663560 | tf_op jit(solution)/shard_map/ppermute | solution.py:188
  24.3 4.6 %collective-permute-start.16 = (bf16[96,1152]{1,0:T(8,128)(2,1)S(1)}, bf16[96,1152]{1,0:T(8,128)(2,1)S(1)}, u32[]{:S(2)}, u32[]{:S(2)}) collective-permute-start(bf16[96,1152]{1,0:T(8,128)(2,1)S(1)} %collective-permute-done.9.refs_7_), channel_id=1, source_target_pairs={{0,1},{1,0},{2,3},{3,2},{4,5},{5,4},{6,7},{7,6},{8,9},{9,8},{10,11... | collective-permute-start | bytes 663560 | tf_op jit(solution)/shard_map/ppermute | solution.py:188
  24.4 4.6 %collective-permute-start.17 = (bf16[96,1152]{1,0:T(8,128)(2,1)S(1)}, bf16[96,1152]{1,0:T(8,128)(2,1)S(1)}, u32[]{:S(2)}, u32[]{:S(2)}) collective-permute-start(bf16[96,1152]{1,0:T(8,128)(2,1)S(1)} %collective-permute-done.2.refs_2_), channel_id=1, source_target_pairs={{0,1},{1,0},{2,3},{3,2},{4,5},{5,4},{6,7},{7,6},{8,9},{9,8},{10,11... | collective-permute-start | bytes 663560 | tf_op jit(solution)/shard_map/ppermute | solution.py:188
  26.2 2.7 %collective-permute-start.19 = (bf16[96,1152]{1,0:T(8,128)(2,1)S(1)}, bf16[96,1152]{1,0:T(8,128)(2,1)S(1)}, u32[]{:S(2)}, u32[]{:S(2)}) collective-permute-start(bf16[96,1152]{1,0:T(8,128)(2,1)S(1)} %collective-permute-done.18.refs_4_), channel_id=1, source_target_pairs={{0,1},{1,0},{2,3},{3,2},{4,5},{5,4},{6,7},{7,6},{8,9},{9,8},{10,11... | collective-permute-start | bytes 663560 | tf_op jit(solution)/shard_map/ppermute | solution.py:188
  26.3 2.7 %copy-start.4 = (bf16[96,1152]{1,0:T(8,128)(2,1)S(1)}, bf16[96,1152]{1,0:T(8,128)(2,1)}, u32[]{:S(2)}) copy-start(bf16[96,1152]{1,0:T(8,128)(2,1)} %refs_0_.1) | copy-start | bytes 663556
  28.2 3.2 %copy-start = (bf16[1152,576]{0,1:T(8,128)(2,1)S(1)}, bf16[1152,576]{0,1:T(8,128)(2,1)}, u32[]{:S(2)}) copy-start(bf16[1152,576]{0,1:T(8,128)(2,1)} %param.12) | copy-start | bytes 3981316
  28.2 3.2 %copy-start.1 = (bf16[1152,576]{0,1:T(8,128)(2,1)S(1)}, bf16[1152,576]{0,1:T(8,128)(2,1)}, u32[]{:S(2)}) copy-start(bf16[1152,576]{0,1:T(8,128)(2,1)} %param.13) | copy-start | bytes 3981316
  28.2 3.2 %copy-start.2 = (bf16[1152,576]{0,1:T(8,128)(2,1)S(1)}, bf16[1152,576]{0,1:T(8,128)(2,1)}, u32[]{:S(2)}) copy-start(bf16[1152,576]{0,1:T(8,128)(2,1)} %param.14) | copy-start | bytes 3981316
  28.2 3.2 %copy-start.3 = (bf16[576,1152]{1,0:T(8,128)(2,1)S(1)}, bf16[576,1152]{1,0:T(8,128)(2,1)}, u32[]{:S(2)}) copy-start(bf16[576,1152]{1,0:T(8,128)(2,1)} %refs_8_.1) | copy-start | bytes 3981316
  29.0 2.4 %collective-permute-start.15 = (bf16[96,1152]{1,0:T(8,128)(2,1)S(1)}, bf16[96,1152]{1,0:T(8,128)(2,1)S(1)}, u32[]{:S(2)}, u32[]{:S(2)}) collective-permute-start(bf16[96,1152]{1,0:T(8,128)(2,1)S(1)} %collective-permute-done.3.refs_6_), channel_id=1, source_target_pairs={{0,1},{1,0},{2,3},{3,2},{4,5},{5,4},{6,7},{7,6},{8,9},{9,8},{10,11... | collective-permute-start | bytes 663560 | tf_op jit(solution)/shard_map/ppermute | solution.py:188

commit v4 on v3

--- a/solution.py
+++ b/solution.py
@@ -60,7 +60,7 @@
     for s in range(1, rows):
         found += [at(d * s, core), at(-d * s, swapped), at(d * s, swapped), at(-d * s, core)]
     found += [at(d * rows, core), at(-d * rows, swapped)]
-    return found[1 : 1 + shards // 2] + [me] + found[1 + shards // 2 :]
+    return found[1 : 1 + shards - 6] + [me] + found[1 + shards - 6 :]
 
 
 def flip(x, shards):
@@ -111,7 +111,7 @@
         dest = own.astype(F32) * merged_rows + slot
         dest_row[:, j * tok : (j + 1) * tok] = dest[:, :tok]
         size_row[:, j * tok : (j + 1) * tok] = size[:, :tok]
-        if j == shards // 2:
+        if j == shards - 6:
             mine = dest
     mine = jnp.broadcast_to(mine, (8, LANES))
     mine = jnp.transpose(mine, (1, 0))[:tok, 0:1]
@@ -162,13 +162,16 @@
     v_t = dot(wv_ref[...], merged, NT)
     inverse = 1.0 / math.sqrt(HEAD)
     bias = bias_ref[...]
-    for h in range(HEADS):
-        rows = slice(h * HEAD, (h + 1) * HEAD)
-        scores = dot(q_t[rows].astype(BF16), k_t[rows].astype(BF16), TN) * inverse + bias
-        top = jnp.max(scores, axis=1, keepdims=True)
-        expo = jnp.exp(scores - top)
-        whole = jnp.sum(expo, axis=1, keepdims=True)
-        att_s[:, rows] = dot(expo.astype(BF16), v_t[rows].astype(BF16), NT) / whole
+    heads = [slice(h * HEAD, (h + 1) * HEAD) for h in range(HEADS)]
+    scores = [
+        dot(q_t[rows].astype(BF16), k_t[rows].astype(BF16), TN) * inverse + bias for rows in heads
+    ]
+    weights = []
+    for score in scores:
+        expo = jnp.exp(score - jnp.max(score, axis=1, keepdims=True))
+        weights.append((expo.astype(BF16), jnp.sum(expo, axis=1, keepdims=True)))
+    for rows, (expo, whole) in zip(heads, weights):
+        att_s[:, rows] = dot(expo, v_t[rows].astype(BF16), NT) / whole
     out_ref[...] = dot(att_s[...].astype(BF16), wo_ref[...]).astype(BF16)
 
 
@@ -236,8 +239,8 @@
         compiler_params=pltpu.CompilerParams(vmem_limit_bytes=VMEM_PREP),
         cost_estimate=cost(1000, 1000),
     )(jnp.concatenate(metas, axis=0))
-    blocks = blocks[1 : 1 + shards // 2] + [tokens] + blocks[1 + shards // 2 :]
-    cuts = [0, shards // 2, shards - 1, shards]
+    blocks = blocks[1 : 1 + shards - 6] + [tokens] + blocks[1 + shards - 6 :]
+    cuts = [0, shards - 6, shards - 1, shards]
     acc = []
     for low, high in zip(cuts[:-2], cuts[1:-1]):
         n = high - low

time: 38 us -> 37.1 us (0.976)
  Pallas kernels: 13.3 us -> 12.7 us
  waiting for transfers between devices: 10.7 us -> 10.2 us
    pallas_call x1, Pallas kernels: 6.27 us -> 5.46 us  [on_device_gathered(): pl.pallas_call(functools.partial(tail_kernel, n, low * tok), out_shape=ja...]
    ppermute x20, waiting for transfers between devices: 10.7 us -> 10.2 us  [send(): return lax.ppermute(x, 'ctx', pairs)]
  transfers between devices with their start and end apart: 20 -> 20, of which waited for: 7 -> 7; matrix products, arithmetic and copies ran while one was open for 4% -> 4% of each run, Pallas kernels for 19% -> 20%
where the time goes in v4:
time: 37.1 us; the launch traced here: 36.9 us
  Pallas kernels  12.7 us (34%)
  starting transfers between devices  12.2 us (33%)
  waiting for transfers between devices  10.2 us (27%)
  local copies, waits for them, and re-layouts  0.8 us (2%)
  other arithmetic  0.69 us (2%)
    ppermute x20, starting transfers between devices, send(): return lax.ppermute(x, 'ctx', pairs)  12.2 us
    ppermute x20, waiting for transfers between devices, send(): return lax.ppermute(x, 'ctx', pairs)  10.2 us
    pallas_call x1, Pallas kernels, on_device_gathered(): pl.pallas_call(functools.partial(tail_kernel, n, low * tok), out_shape=ja...  5.46 us
    pallas_call x2, Pallas kernels, on_device_gathered(): pl.pallas_call(functools.partial(merge_kernel, n, low * tok), out_shape=j...  4.5 us
    pallas_call x1, Pallas kernels, on_device_gathered(): pl.pallas_call(functools.partial(meta_kernel, slots), out_shape=jax.Shape...  1.5 us
    pallas_call x1, Pallas kernels, on_device_gathered(): pl.pallas_call(functools.partial(prep_kernel, shards, slots, tok, merged_...  1.27 us
    unnamed x14, local copies, waits for them, and re-layouts  0.78 us
  transfers between devices with their start and end apart: 20, of which 7 were waited for; matrix products, arithmetic and copies ran while one was open for 4% of the time, Pallas kernels for 20%

profile of v4, /device:TPU:0, one launch (start us, length us, event | category | flops | bytes accessed | tf_op | source)
XLA Modules:
  0.0 36.9 jit_solution(12129206324572472592)
XLA Ops:
  0.0 0.5 %collective-permute-start.4 = (bf16[96,1152]{1,0:T(8,128)(2,1)}, bf16[96,1152]{1,0:T(8,128)(2,1)S(1)}, u32[]{:S(2)}, u32[]{:S(2)}) collective-permute-start(bf16[96,1152]{1,0:T(8,128)(2,1)} %refs_0_.1), channel_id=1, source_target_pairs={{0,1},{1,0},{2,3},{3,2},{4,5},{5,4},{6,7},{7,6},{8,9},{9,8},{10,11... | collective-permute-start | bytes 663560 | tf_op jit(solution)/shard_map/ppermute | solution.py:191
  0.5 2.6 %collective-permute-start = (bf16[96,1152]{1,0:T(8,128)(2,1)}, bf16[96,1152]{1,0:T(8,128)(2,1)S(1)}, u32[]{:S(2)}, u32[]{:S(2)}) collective-permute-start(bf16[96,1152]{1,0:T(8,128)(2,1)} %refs_0_.1), channel_id=1, source_target_pairs={{0,4},{1,3},{4,8},{5,1},{8,12},{9,5},{12,14},{13,9},{14,10},{15,13... | collective-permute-start | bytes 663560 | tf_op jit(solution)/shard_map/ppermute | solution.py:191
  3.0 1.4 %collective-permute-start.6 = (bf16[96,1152]{1,0:T(8,128)(2,1)}, bf16[96,1152]{1,0:T(8,128)(2,1)S(1)}, u32[]{:S(2)}, u32[]{:S(2)}) collective-permute-start(bf16[96,1152]{1,0:T(8,128)(2,1)} %refs_0_.1), channel_id=1, source_target_pairs={{1,4},{0,3},{5,8},{4,1},{9,12},{8,5},{13,14},{12,9},{15,10},{14,13... | collective-permute-start | bytes 663560 | tf_op jit(solution)/shard_map/ppermute | solution.py:191
  4.4 1.5 %shard_map.82 = bf16[16,128]{1,0:T(8,128)(2,1)} custom-call(s32[1,96]{1,0:T(1,128)} %bitcast.10, s32[1,96]{1,0:T(1,128)} %bitcast.11, s32[12,1,16]{2,1,0:T(1,128)} %bitcast.9), custom_call_target="tpu_custom_call" | custom-call | tf_op jit(solution)/shard_map/pallas_call | solution.py:195
  5.9 0.0 collective-permute-done.4.refs_0_
  5.9 0.5 %collective-permute-start.11 = (bf16[16,128]{1,0:T(8,128)(2,1)}, bf16[16,128]{1,0:T(8,128)(2,1)S(1)}, u32[]{:S(2)}, u32[]{:S(2)}) collective-permute-start(bf16[16,128]{1,0:T(8,128)(2,1)} %shard_map.82), channel_id=1, source_target_pairs={{0,4},{1,5},{2,6},{3,7},{4,0},{5,1},{6,2},{7,3},{8,12},{9,13},{10,... | collective-permute-start | bytes 12296 | tf_op jit(solution)/shard_map/ppermute | solution.py:191
  6.3 2.3 %collective-permute-start.12 = (bf16[16,128]{1,0:T(8,128)(2,1)}, bf16[16,128]{1,0:T(8,128)(2,1)S(1)}, u32[]{:S(2)}, u32[]{:S(2)}) collective-permute-start(bf16[16,128]{1,0:T(8,128)(2,1)} %shard_map.82), channel_id=1, source_target_pairs={{0,8},{1,9},{2,10},{3,11},{4,12},{5,13},{6,14},{7,15},{8,0},{9,1},... | collective-permute-start | bytes 12296 | tf_op jit(solution)/shard_map/ppermute | solution.py:191
  8.6 1.6 %collective-permute-start.13 = (bf16[16,128]{1,0:T(8,128)(2,1)}, bf16[16,128]{1,0:T(8,128)(2,1)S(1)}, u32[]{:S(2)}, u32[]{:S(2)}) collective-permute-start(bf16[16,128]{1,0:T(8,128)(2,1)} %shard_map.82), channel_id=1, source_target_pairs={{0,12},{1,13},{2,14},{3,15},{4,8},{5,9},{6,10},{7,11},{8,4},{9,5},... | collective-permute-start | bytes 12296 | tf_op jit(solution)/shard_map/ppermute | solution.py:191
  10.3 0.7 %constant_dynamic-update-slice_fusion.4 = (bf16[128,128]{1,0:T(8,128)(2,1)S(1)}, bf16[256,128]{1,0:T(8,128)(2,1)S(1)}) fusion(bf16[16,128]{1,0:T(8,128)(2,1)} %shard_map.82), kind=kLoop, calls=%fused_computation.4 | loop fusion | bytes 12288
  11.0 0.0 collective-permute-done.refs_1_
  11.0 0.0 collective-permute-start.1
  11.0 0.0 collective-permute-done.6.refs_3_
  11.0 0.1 collective-permute-start.5
  11.1 0.0 collective-permute-done.11
  11.1 1.2 %collective-permute-start.9 = (bf16[96,1152]{1,0:T(8,128)(2,1)S(1)}, bf16[96,1152]{1,0:T(8,128)(2,1)S(1)}, u32[]{:S(2)}, u32[]{:S(2)}) collective-permute-start(bf16[96,1152]{1,0:T(8,128)(2,1)S(1)} %collective-permute-done.6.refs_3_), channel_id=1, source_target_pairs={{0,4},{1,3},{4,8},{5,1},{8,12},{9,5},{12,14},{13,9},{14,10},{15,13... | collective-permute-start | bytes 663560 | tf_op jit(solution)/shard_map/ppermute | solution.py:191
  12.3 2.1 %collective-permute-done.13 = bf16[16,128]{1,0:T(8,128)(2,1)S(1)} collective-permute-done((bf16[16,128]{1,0:T(8,128)(2,1)}, bf16[16,128]{1,0:T(8,128)(2,1)S(1)}, u32[]{:S(2)}, u32[]{:S(2)}) %collective-permute-start.13) | collective-permute-done | bytes 4128 | tf_op jit(solution)/shard_map/ppermute | solution.py:191
  14.3 0.7 %pad_maximum_fusion = bf16[64,128]{1,0:T(8,128)(2,1)S(1)} fusion(bf16[16,128]{1,0:T(8,128)(2,1)S(1)} %collective-permute-done.13, bf16[16,128]{1,0:T(8,128)(2,1)S(1)} %collective-permute-done.12, bf16[16,128]{1,0:T(8,128)(2,1)S(1)} %collective-permute-done.11, bf16[16,128]{1,0:T(8,128)(2,1)} %shard_map.82), kind=kLoop, calls=%fused_computation.11 | loop fusion | flops 65536 | bytes 32768 | tf_op jit(solution)/shard_map/concatenate | solution.py:215
  15.0 0.7 %collective-permute-start.14 = (bf16[64,128]{1,0:T(8,128)(2,1)S(1)}, bf16[64,128]{1,0:T(8,128)(2,1)S(1)}, u32[]{:S(2)}, u32[]{:S(2)}) collective-permute-start(bf16[64,128]{1,0:T(8,128)(2,1)S(1)} %pad_maximum_fusion), channel_id=1, source_target_pairs={{0,2},{1,3},{2,0},{3,1},{4,6},{5,7},{6,4},{7,5},{8,10},{9,11},{10,... | collective-permute-start | bytes 49160 | tf_op jit(solution)/shard_map/ppermute | solution.py:191
  15.8 1.4 %collective-permute-done.1.refs_5_ = bf16[96,1152]{1,0:T(8,128)(2,1)S(1)} collective-permute-done((bf16[96,1152]{1,0:T(8,128)(2,1)S(1)}, bf16[96,1152]{1,0:T(8,128)(2,1)S(1)}, u32[]{:S(2)}, u32[]{:S(2)}) %collective-permute-start.1) | collective-permute-done | bytes 221216 | tf_op jit(solution)/shard_map/ppermute | solution.py:191
  17.1 2.5 %collective-permute-done.14 = bf16[64,128]{1,0:T(8,128)(2,1)S(1)} collective-permute-done((bf16[64,128]{1,0:T(8,128)(2,1)S(1)}, bf16[64,128]{1,0:T(8,128)(2,1)S(1)}, u32[]{:S(2)}, u32[]{:S(2)}) %collective-permute-start.14) | collective-permute-done | bytes 16416 | tf_op jit(solution)/shard_map/ppermute | solution.py:191
  19.7 0.1 collective-permute-start.15
  19.7 0.5 %collective-permute-start.7 = (bf16[96,1152]{1,0:T(8,128)(2,1)S(1)}, bf16[96,1152]{1,0:T(8,128)(2,1)S(1)}, u32[]{:S(2)}, u32[]{:S(2)}) collective-permute-start(bf16[96,1152]{1,0:T(8,128)(2,1)S(1)} %collective-permute-done.6.refs_3_), channel_id=1, source_target_pairs={{0,1},{1,0},{2,3},{3,2},{4,5},{5,4},{6,7},{7,6},{8,9},{9,8},{10,11... | collective-permute-start | bytes 663560 | tf_op jit(solution)/shard_map/ppermute | solution.py:191
  20.2 0.0 collective-permute-done.9.refs_7_
  20.2 0.0 collective-permute-start.18
  20.2 0.7 %collective-permute-done.15 = bf16[128,128]{1,0:T(8,128)(2,1)S(1)} collective-permute-done((bf16[128,128]{1,0:T(8,128)(2,1)S(1)}, bf16[128,128]{1,0:T(8,128)(2,1)S(1)}, u32[]{:S(2)}, u32[]{:S(2)}) %collective-permute-start.15) | collective-permute-done | bytes 32800 | tf_op jit(solution)/shard_map/ppermute | solution.py:191
  20.9 0.2 collective-permute-start.10
  21.1 0.0 collective-permute-done.5.refs_2_
  21.1 0.3 collective-permute-start.8
  21.4 1.6 %collective-permute-done.2.refs_9_ = bf16[96,1152]{1,0:T(8,128)(2,1)S(1)} collective-permute-done((bf16[96,1152]{1,0:T(8,128)(2,1)S(1)}, bf16[96,1152]{1,0:T(8,128)(2,1)S(1)}, u32[]{:S(2)}, u32[]{:S(2)}) %collective-permute-start.2) | collective-permute-done | bytes 221216 | tf_op jit(solution)/shard_map/ppermute | solution.py:191
  23.0 0.0 collective-permute-start.3
  23.1 1.3 %shard_map.83 = (bf16[864,1536]{1,0:T(8,128)(2,1)S(1)}, f32[864,1]{1,0:T(8,128)S(1)}, f32[1,768]{1,0:T(1,128)S(1)}) custom-call(bf16[256,128]{1,0:T(8,128)(2,1)S(1)} %constant_dynamic-update-slice_fusion.5.g_ref), custom_call_target="tpu_custom_call" | custom-call | flops 1000 | bytes 1000 | tf_op jit(solution)/shard_map/pallas_call | solution.py:225
  24.3 0.0 collective-permute-done.7.refs_4_
  24.3 0.1 collective-permute-start.17
  24.4 1.7 %collective-permute-done.18.refs_2_ = bf16[96,1152]{1,0:T(8,128)(2,1)S(1)} collective-permute-done((bf16[96,1152]{1,0:T(8,128)(2,1)S(1)}, bf16[96,1152]{1,0:T(8,128)(2,1)S(1)}, u32[]{:S(2)}, u32[]{:S(2)}) %collective-permute-start.18) | collective-permute-done | bytes 221216 | tf_op jit(solution)/shard_map/ppermute | solution.py:191
  26.2 0.0 collective-permute-start.19
  26.2 0.0 collective-permute-done.10.refs_8_
  26.2 0.0 collective-permute-done.8.refs_6_
  26.2 0.0 copy-start.4
  26.2 2.5 %shard_map.84.refs_6_ = f32[864,1152]{1,0:T(8,128)S(1)} custom-call(bf16[96,1152]{1,0:T(8,128)(2,1)S(1)} %collective-permute-done.4.refs_0_, bf16[96,1152]{1,0:T(8,128)(2,1)S(1)} %collective-permute-done.refs_1_, bf16[96,1152]{1,0:T(8,128)(2,1)S(1)} %collective-permute-done.5.refs_2_, bf16[96,1152]{1,0:T(8,128)(2,1)S(1)} %collective-permute-done.6.refs_3_, ...), custom_call_target="tpu_custom_call" | custom-call | flops 1000 | bytes 1000 | tf_op jit(solution)/shard_map/pallas_call | solution.py:248
  28.7 0.0 copy-start
  28.7 0.0 copy-start.1
  28.7 0.0 copy-start.2
  28.7 0.0 copy-start.3
  28.8 0.2 collective-permute-done.3.refs_4_
  29.0 0.4 collective-permute-start.16
  29.3 0.0 collective-permute-done.17.refs_1_
  29.3 2.0 %shard_map.85.refs_1_ = f32[864,1152]{1,0:T(8,128)S(1)} custom-call(bf16[96,1152]{1,0:T(8,128)(2,1)S(1)} %copy-done.4, bf16[96,1152]{1,0:T(8,128)(2,1)S(1)} %collective-permute-done.17.refs_1_, bf16[96,1152]{1,0:T(8,128)(2,1)S(1)} %collective-permute-done.18.refs_2_, ...), custom_call_target="tpu_custom_call", output_to_operand_aliasing={{}: (6, {})} | custom-call | flops 1000 | bytes 1000 | tf_op jit(solution)/shard_map/pallas_call | solution.py:248
  31.4 5.5 %shard_map.86 = bf16[96,1152]{1,0:T(8,128)(2,1)} custom-call(bf16[96,1152]{1,0:T(8,128)(2,1)S(1)} %collective-permute-done.16.refs_0_, f32[864,1152]{1,0:T(8,128)S(1)} %shard_map.85.refs_1_, bf16[864,1536]{1,0:T(8,128)(2,1)S(1)} %get-tuple-element.11.refs_10_.refs_5_.refs_2_, f32[864,1]{1,0:T(8,128)S(1)} %get-tuple-element.13.refs_3_, ...), custom_call_target="tpu_custom_call" | custom-call | flops 2038431744 | bytes 5308416 | tf_op jit(solution)/shard_map/pallas_call | solution.py:263
  (14 shorter events, 0.1 us)
Async XLA Ops:
  0.0 5.9 %collective-permute-start.4 = (bf16[96,1152]{1,0:T(8,128)(2,1)}, bf16[96,1152]{1,0:T(8,128)(2,1)S(1)}, u32[]{:S(2)}, u32[]{:S(2)}) collective-permute-start(bf16[96,1152]{1,0:T(8,128)(2,1)} %refs_0_.1), channel_id=1, source_target_pairs={{0,1},{1,0},{2,3},{3,2},{4,5},{5,4},{6,7},{7,6},{8,9},{9,8},{10,11... | collective-permute-start | bytes 663560 | tf_op jit(solution)/shard_map/ppermute | solution.py:191
  0.5 10.5 %collective-permute-start = (bf16[96,1152]{1,0:T(8,128)(2,1)}, bf16[96,1152]{1,0:T(8,128)(2,1)S(1)}, u32[]{:S(2)}, u32[]{:S(2)}) collective-permute-start(bf16[96,1152]{1,0:T(8,128)(2,1)} %refs_0_.1), channel_id=1, source_target_pairs={{0,4},{1,3},{4,8},{5,1},{8,12},{9,5},{12,14},{13,9},{14,10},{15,13... | collective-permute-start | bytes 663560 | tf_op jit(solution)/shard_map/ppermute | solution.py:191
  3.0 8.0 %collective-permute-start.6 = (bf16[96,1152]{1,0:T(8,128)(2,1)}, bf16[96,1152]{1,0:T(8,128)(2,1)S(1)}, u32[]{:S(2)}, u32[]{:S(2)}) collective-permute-start(bf16[96,1152]{1,0:T(8,128)(2,1)} %refs_0_.1), channel_id=1, source_target_pairs={{1,4},{0,3},{5,8},{4,1},{9,12},{8,5},{13,14},{12,9},{15,10},{14,13... | collective-permute-start | bytes 663560 | tf_op jit(solution)/shard_map/ppermute | solution.py:191
  5.9 5.2 %collective-permute-start.11 = (bf16[16,128]{1,0:T(8,128)(2,1)}, bf16[16,128]{1,0:T(8,128)(2,1)S(1)}, u32[]{:S(2)}, u32[]{:S(2)}) collective-permute-start(bf16[16,128]{1,0:T(8,128)(2,1)} %shard_map.82), channel_id=1, source_target_pairs={{0,4},{1,5},{2,6},{3,7},{4,0},{5,1},{6,2},{7,3},{8,12},{9,13},{10,... | collective-permute-start | bytes 12296 | tf_op jit(solution)/shard_map/ppermute | solution.py:191
  6.3 5.9 %collective-permute-start.12 = (bf16[16,128]{1,0:T(8,128)(2,1)}, bf16[16,128]{1,0:T(8,128)(2,1)S(1)}, u32[]{:S(2)}, u32[]{:S(2)}) collective-permute-start(bf16[16,128]{1,0:T(8,128)(2,1)} %shard_map.82), channel_id=1, source_target_pairs={{0,8},{1,9},{2,10},{3,11},{4,12},{5,13},{6,14},{7,15},{8,0},{9,1},... | collective-permute-start | bytes 12296 | tf_op jit(solution)/shard_map/ppermute | solution.py:191
  8.6 5.7 %collective-permute-start.13 = (bf16[16,128]{1,0:T(8,128)(2,1)}, bf16[16,128]{1,0:T(8,128)(2,1)S(1)}, u32[]{:S(2)}, u32[]{:S(2)}) collective-permute-start(bf16[16,128]{1,0:T(8,128)(2,1)} %shard_map.82), channel_id=1, source_target_pairs={{0,12},{1,13},{2,14},{3,15},{4,8},{5,9},{6,10},{7,11},{8,4},{9,5},... | collective-permute-start | bytes 12296 | tf_op jit(solution)/shard_map/ppermute | solution.py:191
  11.0 6.1 %collective-permute-start.1 = (bf16[96,1152]{1,0:T(8,128)(2,1)S(1)}, bf16[96,1152]{1,0:T(8,128)(2,1)S(1)}, u32[]{:S(2)}, u32[]{:S(2)}) collective-permute-start(bf16[96,1152]{1,0:T(8,128)(2,1)S(1)} %collective-permute-done.refs_1_), channel_id=1, source_target_pairs={{0,4},{1,3},{4,8},{5,1},{8,12},{9,5},{12,14},{13,9},{14,10},{15,13... | collective-permute-start | bytes 663560 | tf_op jit(solution)/shard_map/ppermute | solution.py:191
  11.0 10.1 %collective-permute-start.5 = (bf16[96,1152]{1,0:T(8,128)(2,1)S(1)}, bf16[96,1152]{1,0:T(8,128)(2,1)S(1)}, u32[]{:S(2)}, u32[]{:S(2)}) collective-permute-start(bf16[96,1152]{1,0:T(8,128)(2,1)S(1)} %collective-permute-done.refs_1_), channel_id=1, source_target_pairs={{0,1},{1,0},{2,3},{3,2},{4,5},{5,4},{6,7},{7,6},{8,9},{9,8},{10,11... | collective-permute-start | bytes 663560 | tf_op jit(solution)/shard_map/ppermute | solution.py:191
  11.1 9.1 %collective-permute-start.9 = (bf16[96,1152]{1,0:T(8,128)(2,1)S(1)}, bf16[96,1152]{1,0:T(8,128)(2,1)S(1)}, u32[]{:S(2)}, u32[]{:S(2)}) collective-permute-start(bf16[96,1152]{1,0:T(8,128)(2,1)S(1)} %collective-permute-done.6.refs_3_), channel_id=1, source_target_pairs={{0,4},{1,3},{4,8},{5,1},{8,12},{9,5},{12,14},{13,9},{14,10},{15,13... | collective-permute-start | bytes 663560 | tf_op jit(solution)/shard_map/ppermute | solution.py:191
  15.0 4.7 %collective-permute-start.14 = (bf16[64,128]{1,0:T(8,128)(2,1)S(1)}, bf16[64,128]{1,0:T(8,128)(2,1)S(1)}, u32[]{:S(2)}, u32[]{:S(2)}) collective-permute-start(bf16[64,128]{1,0:T(8,128)(2,1)S(1)} %pad_maximum_fusion), channel_id=1, source_target_pairs={{0,2},{1,3},{2,0},{3,1},{4,6},{5,7},{6,4},{7,5},{8,10},{9,11},{10,... | collective-permute-start | bytes 49160 | tf_op jit(solution)/shard_map/ppermute | solution.py:191
  17.1 5.9 %collective-permute-start.2 = (bf16[96,1152]{1,0:T(8,128)(2,1)S(1)}, bf16[96,1152]{1,0:T(8,128)(2,1)S(1)}, u32[]{:S(2)}, u32[]{:S(2)}) collective-permute-start(bf16[96,1152]{1,0:T(8,128)(2,1)S(1)} %collective-permute-done.1.refs_5_), channel_id=1, source_target_pairs={{0,4},{1,3},{4,8},{5,1},{8,12},{9,5},{12,14},{13,9},{14,10},{15,13... | collective-permute-start | bytes 663560 | tf_op jit(solution)/shard_map/ppermute | solution.py:191
  19.7 1.3 %collective-permute-start.15 = (bf16[128,128]{1,0:T(8,128)(2,1)S(1)}, bf16[128,128]{1,0:T(8,128)(2,1)S(1)}, u32[]{:S(2)}, u32[]{:S(2)}) collective-permute-start(bf16[128,128]{1,0:T(8,128)(2,1)S(1)} %get-tuple-element.15), channel_id=1, source_target_pairs={{0,1},{1,0},{2,3},{3,2},{4,5},{5,4},{6,7},{7,6},{8,9},{9,8},{10,11... | collective-permute-start | bytes 98312 | tf_op jit(solution)/shard_map/ppermute | solution.py:191
  19.7 4.6 %collective-permute-start.7 = (bf16[96,1152]{1,0:T(8,128)(2,1)S(1)}, bf16[96,1152]{1,0:T(8,128)(2,1)S(1)}, u32[]{:S(2)}, u32[]{:S(2)}) collective-permute-start(bf16[96,1152]{1,0:T(8,128)(2,1)S(1)} %collective-permute-done.6.refs_3_), channel_id=1, source_target_pairs={{0,1},{1,0},{2,3},{3,2},{4,5},{5,4},{6,7},{7,6},{8,9},{9,8},{10,11... | collective-permute-start | bytes 663560 | tf_op jit(solution)/shard_map/ppermute | solution.py:191
  20.2 5.9 %collective-permute-start.18 = (bf16[96,1152]{1,0:T(8,128)(2,1)S(1)}, bf16[96,1152]{1,0:T(8,128)(2,1)S(1)}, u32[]{:S(2)}, u32[]{:S(2)}) collective-permute-start(bf16[96,1152]{1,0:T(8,128)(2,1)S(1)} %collective-permute-done.9.refs_7_), channel_id=1, source_target_pairs={{0,4},{1,3},{4,8},{5,1},{8,12},{9,5},{12,14},{13,9},{14,10},{15,13... | collective-permute-start | bytes 663560 | tf_op jit(solution)/shard_map/ppermute | solution.py:191
  20.9 5.2 %collective-permute-start.10 = (bf16[96,1152]{1,0:T(8,128)(2,1)S(1)}, bf16[96,1152]{1,0:T(8,128)(2,1)S(1)}, u32[]{:S(2)}, u32[]{:S(2)}) collective-permute-start(bf16[96,1152]{1,0:T(8,128)(2,1)S(1)} %collective-permute-done.9.refs_7_), channel_id=1, source_target_pairs={{0,1},{1,0},{2,3},{3,2},{4,5},{5,4},{6,7},{7,6},{8,9},{9,8},{10,11... | collective-permute-start | bytes 663560 | tf_op jit(solution)/shard_map/ppermute | solution.py:191
  21.1 5.1 %collective-permute-start.8 = (bf16[96,1152]{1,0:T(8,128)(2,1)S(1)}, bf16[96,1152]{1,0:T(8,128)(2,1)S(1)}, u32[]{:S(2)}, u32[]{:S(2)}) collective-permute-start(bf16[96,1152]{1,0:T(8,128)(2,1)S(1)} %collective-permute-done.1.refs_5_), channel_id=1, source_target_pairs={{0,1},{1,0},{2,3},{3,2},{4,5},{5,4},{6,7},{7,6},{8,9},{9,8},{10,11... | collective-permute-start | bytes 663560 | tf_op jit(solution)/shard_map/ppermute | solution.py:191
  23.0 5.9 %collective-permute-start.3 = (bf16[96,1152]{1,0:T(8,128)(2,1)S(1)}, bf16[96,1152]{1,0:T(8,128)(2,1)S(1)}, u32[]{:S(2)}, u32[]{:S(2)}) collective-permute-start(bf16[96,1152]{1,0:T(8,128)(2,1)S(1)} %collective-permute-done.2.refs_9_), channel_id=1, source_target_pairs={{0,4},{1,3},{4,8},{5,1},{8,12},{9,5},{12,14},{13,9},{14,10},{15,13... | collective-permute-start | bytes 663560 | tf_op jit(solution)/shard_map/ppermute | solution.py:191
  24.3 5.0 %collective-permute-start.17 = (bf16[96,1152]{1,0:T(8,128)(2,1)S(1)}, bf16[96,1152]{1,0:T(8,128)(2,1)S(1)}, u32[]{:S(2)}, u32[]{:S(2)}) collective-permute-start(bf16[96,1152]{1,0:T(8,128)(2,1)S(1)} %collective-permute-done.2.refs_9_), channel_id=1, source_target_pairs={{0,1},{1,0},{2,3},{3,2},{4,5},{5,4},{6,7},{7,6},{8,9},{9,8},{10,11... | collective-permute-start | bytes 663560 | tf_op jit(solution)/shard_map/ppermute | solution.py:191
  26.2 3.2 %collective-permute-start.19 = (bf16[96,1152]{1,0:T(8,128)(2,1)S(1)}, bf16[96,1152]{1,0:T(8,128)(2,1)S(1)}, u32[]{:S(2)}, u32[]{:S(2)}) collective-permute-start(bf16[96,1152]{1,0:T(8,128)(2,1)S(1)} %collective-permute-done.18.refs_2_), channel_id=1, source_target_pairs={{0,1},{1,0},{2,3},{3,2},{4,5},{5,4},{6,7},{7,6},{8,9},{9,8},{10,11... | collective-permute-start | bytes 663560 | tf_op jit(solution)/shard_map/ppermute | solution.py:191
  26.2 3.2 %copy-start.4 = (bf16[96,1152]{1,0:T(8,128)(2,1)S(1)}, bf16[96,1152]{1,0:T(8,128)(2,1)}, u32[]{:S(2)}) copy-start(bf16[96,1152]{1,0:T(8,128)(2,1)} %refs_0_.1) | copy-start | bytes 663556
  28.7 2.6 %copy-start = (bf16[1152,576]{0,1:T(8,128)(2,1)S(1)}, bf16[1152,576]{0,1:T(8,128)(2,1)}, u32[]{:S(2)}) copy-start(bf16[1152,576]{0,1:T(8,128)(2,1)} %param.12) | copy-start | bytes 3981316
  28.7 2.6 %copy-start.1 = (bf16[1152,576]{0,1:T(8,128)(2,1)S(1)}, bf16[1152,576]{0,1:T(8,128)(2,1)}, u32[]{:S(2)}) copy-start(bf16[1152,576]{0,1:T(8,128)(2,1)} %param.13) | copy-start | bytes 3981316
  28.7 2.6 %copy-start.2 = (bf16[1152,576]{0,1:T(8,128)(2,1)S(1)}, bf16[1152,576]{0,1:T(8,128)(2,1)}, u32[]{:S(2)}) copy-start(bf16[1152,576]{0,1:T(8,128)(2,1)} %param.14) | copy-start | bytes 3981316
  28.7 2.6 %copy-start.3 = (bf16[576,1152]{1,0:T(8,128)(2,1)S(1)}, bf16[576,1152]{1,0:T(8,128)(2,1)}, u32[]{:S(2)}) copy-start(bf16[576,1152]{1,0:T(8,128)(2,1)} %refs_8_.1) | copy-start | bytes 3981316
  29.0 2.4 %collective-permute-start.16 = (bf16[96,1152]{1,0:T(8,128)(2,1)S(1)}, bf16[96,1152]{1,0:T(8,128)(2,1)S(1)}, u32[]{:S(2)}, u32[]{:S(2)}) collective-permute-start(bf16[96,1152]{1,0:T(8,128)(2,1)S(1)} %collective-permute-done.3.refs_4_), channel_id=1, source_target_pairs={{0,1},{1,0},{2,3},{3,2},{4,5},{5,4},{6,7},{7,6},{8,9},{9,8},{10,11... | collective-permute-start | bytes 663560 | tf_op jit(solution)/shard_map/ppermute | solution.py:191

commit v5 on v4

--- a/solution.py
+++ b/solution.py
@@ -13,6 +13,7 @@
 META = 16
 LANES = 128
 GATHERED_MAX = 8 << 20
+VMEM_META = 2 << 20
 VMEM_PREP = 16 << 20
 VMEM_MERGE = 12 << 20
 VMEM_TAIL = 20 << 20
@@ -67,20 +68,17 @@
     return x % 2 * (shards // 2) + x // 2 % 2 * (shards // 4) + x // 4
 
 
-def meta_kernel(slots, owner_ref, sizes_ref, map_ref, out_ref):
-    tok = owner_ref.shape[1]
-
-    def wide(x):
-        x = x.astype(F32)
-        return jnp.concatenate([x, jnp.zeros((1, LANES - x.shape[1]), F32)], axis=1)
-
-    row = wide(owner_ref[...])
+def meta_kernel(slots, tok, given_ref, out_ref):
+
+    given = [given_ref[r].astype(F32) for r in range(slots + 2)]
+    lane = lax.broadcasted_iota(jnp.int32, (1, LANES), 1)
+    row = jnp.where(lane < tok, given[slots], -1.0)
     column = jnp.transpose(jnp.broadcast_to(row, (8, LANES)), (1, 0))[:, 0:1]
     first = lax.broadcasted_iota(jnp.int32, (LANES, LANES), 0)
     second = lax.broadcasted_iota(jnp.int32, (LANES, LANES), 1)
     earlier = (first < second) & (column == row)
     rank = jnp.sum(jnp.where(earlier, 1.0, 0.0), axis=0, keepdims=True)
-    rows = [wide(map_ref[r]) for r in range(slots)] + [row, rank, wide(sizes_ref[...])]
+    rows = given[: slots + 1] + [rank, given[slots + 1]]
     sub = lax.broadcasted_iota(jnp.int32, (META, LANES), 0)
     out = jnp.zeros((META, LANES), F32)
     for r, x in enumerate(rows):
@@ -192,12 +190,24 @@
 
     a, b = send(tokens, along), send(tokens, across)
     other = send(tokens, swap)
+    given = jnp.concatenate(
+        [
+            jnp.pad(x, ((0, 0), (0, 0), (0, LANES - x.shape[2])))
+            for x in (
+                jnp.transpose(slot_map, (2, 0, 1)),
+                owner.reshape(1, 1, tok),
+                sizes.reshape(1, 1, tok),
+            )
+        ],
+        axis=0,
+    )
     meta = pl.pallas_call(
-        functools.partial(meta_kernel, slots),
+        functools.partial(meta_kernel, slots, tok),
         out_shape=jax.ShapeDtypeStruct((META, LANES), BF16),
-        in_specs=[vmem] * 3,
+        in_specs=[vmem],
         out_specs=vmem,
-    )(owner.reshape(1, tok), sizes.reshape(1, tok), jnp.transpose(slot_map, (2, 0, 1)))
+        compiler_params=pltpu.CompilerParams(vmem_limit_bytes=VMEM_META),
+    )(given)
     metas = [meta]
     bit = shards // 2
 

time: 37.1 us -> 35.8 us (0.965)
  starting transfers between devices: 12.2 us -> 14.7 us
  waiting for transfers between devices: 10.2 us -> 8.56 us
  Pallas kernels: 12.7 us -> 11.4 us
  local copies, waits for them, and re-layouts: 0.8 us -> 0.08 us
    ppermute x20, starting transfers between devices: 12.2 us -> 14.7 us  [send(): return lax.ppermute(x, 'ctx', pairs)]
    ppermute x20, waiting for transfers between devices: 10.2 us -> 8.56 us  [send(): return lax.ppermute(x, 'ctx', pairs)]
    pallas_call x1, Pallas kernels: 1.5 us -> 0.18 us  [on_device_gathered(): pl.pallas_call(functools.partial(meta_kernel, slots, tok), out_shape=jax....]
    concatenate x0 -> x1, other arithmetic: none -> 0.73 us  [on_device_gathered(): jnp.concatenate([jnp.pad(x, ((0, 0), (0, 0), (0, LANES - x.shape[2]))) fo...]
    unnamed x14, local copies, waits for them, and re-layouts: 0.78 us -> 0.06 us
    concatenate x1, other arithmetic: 0.69 us -> 0.01 us  [on_device_gathered(): jnp.concatenate([meta] + [xor(meta, d, *(other,)) for d in range(4, shard...]
  transfers between devices with their start and end apart: 20 -> 20, of which waited for: 7 -> 7; matrix products, arithmetic and copies ran while one was open for 4% -> 2% of each run, Pallas kernels for 20% -> 17%
where the time goes in v5:
time: 35.8 us; the launch traced here: 35.6 us
  starting transfers between devices  14.7 us (41%)
  Pallas kernels  11.4 us (32%)
  waiting for transfers between devices  8.56 us (24%)
  other arithmetic  0.73 us (2%)
    ppermute x20, starting transfers between devices, send(): return lax.ppermute(x, 'ctx', pairs)  14.7 us
    ppermute x20, waiting for transfers between devices, send(): return lax.ppermute(x, 'ctx', pairs)  8.56 us
    pallas_call x1, Pallas kernels, on_device_gathered(): pl.pallas_call(functools.partial(tail_kernel, n, low * tok), out_shape=ja...  5.46 us
    pallas_call x2, Pallas kernels, on_device_gathered(): pl.pallas_call(functools.partial(merge_kernel, n, low * tok), out_shape=j...  4.5 us
    pallas_call x1, Pallas kernels, on_device_gathered(): pl.pallas_call(functools.partial(prep_kernel, shards, slots, tok, merged_...  1.27 us
    concatenate x1, other arithmetic, on_device_gathered(): jnp.concatenate([jnp.pad(x, ((0, 0), (0, 0), (0, LANES - x.shape[2]))) fo...  0.73 us
  transfers between devices with their start and end apart: 20, of which 7 were waited for; matrix products, arithmetic and copies ran while one was open for 2% of the time, Pallas kernels for 17%

profile of v5, /device:TPU:0, one launch (start us, length us, event | category | flops | bytes accessed | tf_op | source)
XLA Modules:
  0.0 35.6 jit_solution(283887448403616179)
XLA Ops:
  0.0 0.5 %collective-permute-start.4 = (bf16[96,1152]{1,0:T(8,128)(2,1)}, bf16[96,1152]{1,0:T(8,128)(2,1)S(1)}, u32[]{:S(2)}, u32[]{:S(2)}) collective-permute-start(bf16[96,1152]{1,0:T(8,128)(2,1)} %refs_0_.1), channel_id=1, source_target_pairs={{0,1},{1,0},{2,3},{3,2},{4,5},{5,4},{6,7},{7,6},{8,9},{9,8},{10,11... | collective-permute-start | bytes 663560 | tf_op jit(solution)/shard_map/ppermute | solution.py:189
  0.5 2.6 %collective-permute-start = (bf16[96,1152]{1,0:T(8,128)(2,1)}, bf16[96,1152]{1,0:T(8,128)(2,1)S(1)}, u32[]{:S(2)}, u32[]{:S(2)}) collective-permute-start(bf16[96,1152]{1,0:T(8,128)(2,1)} %refs_0_.1), channel_id=1, source_target_pairs={{0,4},{1,3},{4,8},{5,1},{8,12},{9,5},{12,14},{13,9},{14,10},{15,13... | collective-permute-start | bytes 663560 | tf_op jit(solution)/shard_map/ppermute | solution.py:189
  3.0 1.4 %collective-permute-start.6 = (bf16[96,1152]{1,0:T(8,128)(2,1)}, bf16[96,1152]{1,0:T(8,128)(2,1)S(1)}, u32[]{:S(2)}, u32[]{:S(2)}) collective-permute-start(bf16[96,1152]{1,0:T(8,128)(2,1)} %refs_0_.1), channel_id=1, source_target_pairs={{1,4},{0,3},{5,8},{4,1},{9,12},{8,5},{13,14},{12,9},{15,10},{14,13... | collective-permute-start | bytes 663560 | tf_op jit(solution)/shard_map/ppermute | solution.py:189
  4.4 0.7 %pad_add_fusion.given_ref = s32[14,1,128]{2,1,0:T(1,128)S(1)} fusion(s32[1,1,96]{2,1,0:T(1,128)} %bitcast.10, s32[1,1,96]{2,1,0:T(1,128)} %bitcast.11, s32[12,1,16]{2,1,0:T(1,128)} %bitcast.9), kind=kLoop, calls=%fused_computation.12 | loop fusion | flops 3584 | bytes 8704 | tf_op jit(solution)/shard_map/concatenate | solution.py:193
  5.1 0.2 shard_map.82
  5.3 0.0 collective-permute-done.4.refs_0_
  5.3 0.5 %collective-permute-start.11 = (bf16[16,128]{1,0:T(8,128)(2,1)S(1)}, bf16[16,128]{1,0:T(8,128)(2,1)S(1)}, u32[]{:S(2)}, u32[]{:S(2)}) collective-permute-start(bf16[16,128]{1,0:T(8,128)(2,1)S(1)} %shard_map.82), channel_id=1, source_target_pairs={{0,4},{1,5},{2,6},{3,7},{4,0},{5,1},{6,2},{7,3},{8,12},{9,13},{10,... | collective-permute-start | bytes 12296 | tf_op jit(solution)/shard_map/ppermute | solution.py:189
  5.8 2.3 %collective-permute-start.12 = (bf16[16,128]{1,0:T(8,128)(2,1)S(1)}, bf16[16,128]{1,0:T(8,128)(2,1)S(1)}, u32[]{:S(2)}, u32[]{:S(2)}) collective-permute-start(bf16[16,128]{1,0:T(8,128)(2,1)S(1)} %shard_map.82), channel_id=1, source_target_pairs={{0,8},{1,9},{2,10},{3,11},{4,12},{5,13},{6,14},{7,15},{8,0},{9,1},... | collective-permute-start | bytes 12296 | tf_op jit(solution)/shard_map/ppermute | solution.py:189
  8.1 1.6 %collective-permute-start.13 = (bf16[16,128]{1,0:T(8,128)(2,1)S(1)}, bf16[16,128]{1,0:T(8,128)(2,1)S(1)}, u32[]{:S(2)}, u32[]{:S(2)}) collective-permute-start(bf16[16,128]{1,0:T(8,128)(2,1)S(1)} %shard_map.82), channel_id=1, source_target_pairs={{0,12},{1,13},{2,14},{3,15},{4,8},{5,9},{6,10},{7,11},{8,4},{9,5},... | collective-permute-start | bytes 12296 | tf_op jit(solution)/shard_map/ppermute | solution.py:189
  9.8 0.0 collective-permute-done.refs_1_
  9.8 0.8 %collective-permute-start.1 = (bf16[96,1152]{1,0:T(8,128)(2,1)S(1)}, bf16[96,1152]{1,0:T(8,128)(2,1)S(1)}, u32[]{:S(2)}, u32[]{:S(2)}) collective-permute-start(bf16[96,1152]{1,0:T(8,128)(2,1)S(1)} %collective-permute-done.refs_1_), channel_id=1, source_target_pairs={{0,4},{1,3},{4,8},{5,1},{8,12},{9,5},{12,14},{13,9},{14,10},{15,13... | collective-permute-start | bytes 663560 | tf_op jit(solution)/shard_map/ppermute | solution.py:189
  10.5 0.0 collective-permute-done.6.refs_3_
  10.5 0.0 collective-permute-start.5
  10.6 1.6 %collective-permute-start.9 = (bf16[96,1152]{1,0:T(8,128)(2,1)S(1)}, bf16[96,1152]{1,0:T(8,128)(2,1)S(1)}, u32[]{:S(2)}, u32[]{:S(2)}) collective-permute-start(bf16[96,1152]{1,0:T(8,128)(2,1)S(1)} %collective-permute-done.6.refs_3_), channel_id=1, source_target_pairs={{0,4},{1,3},{4,8},{5,1},{8,12},{9,5},{12,14},{13,9},{14,10},{15,13... | collective-permute-start | bytes 663560 | tf_op jit(solution)/shard_map/ppermute | solution.py:189
  12.2 0.0 collective-permute-done.12
  12.2 1.4 %collective-permute-done.13 = bf16[16,128]{1,0:T(8,128)(2,1)S(1)} collective-permute-done((bf16[16,128]{1,0:T(8,128)(2,1)S(1)}, bf16[16,128]{1,0:T(8,128)(2,1)S(1)}, u32[]{:S(2)}, u32[]{:S(2)}) %collective-permute-start.13) | collective-permute-done | bytes 4128 | tf_op jit(solution)/shard_map/ppermute | solution.py:189
  13.6 0.7 %collective-permute-start.14 = (bf16[64,128]{1,0:T(8,128)(2,1)S(1)}, bf16[64,128]{1,0:T(8,128)(2,1)S(1)}, u32[]{:S(2)}, u32[]{:S(2)}) collective-permute-start(bf16[64,128]{1,0:T(8,128)(2,1)S(1)} %pad_maximum_fusion), channel_id=1, source_target_pairs={{0,2},{1,3},{2,0},{3,1},{4,6},{5,7},{6,4},{7,5},{8,10},{9,11},{10,... | collective-permute-start | bytes 49160 | tf_op jit(solution)/shard_map/ppermute | solution.py:189
  14.3 1.5 %collective-permute-done.1.refs_5_ = bf16[96,1152]{1,0:T(8,128)(2,1)S(1)} collective-permute-done((bf16[96,1152]{1,0:T(8,128)(2,1)S(1)}, bf16[96,1152]{1,0:T(8,128)(2,1)S(1)}, u32[]{:S(2)}, u32[]{:S(2)}) %collective-permute-start.1) | collective-permute-done | bytes 221216 | tf_op jit(solution)/shard_map/ppermute | solution.py:189
  15.9 0.6 %collective-permute-start.2 = (bf16[96,1152]{1,0:T(8,128)(2,1)S(1)}, bf16[96,1152]{1,0:T(8,128)(2,1)S(1)}, u32[]{:S(2)}, u32[]{:S(2)}) collective-permute-start(bf16[96,1152]{1,0:T(8,128)(2,1)S(1)} %collective-permute-done.1.refs_5_), channel_id=1, source_target_pairs={{0,4},{1,3},{4,8},{5,1},{8,12},{9,5},{12,14},{13,9},{14,10},{15,13... | collective-permute-start | bytes 663560 | tf_op jit(solution)/shard_map/ppermute | solution.py:189
  16.5 1.9 %collective-permute-done.14 = bf16[64,128]{1,0:T(8,128)(2,1)S(1)} collective-permute-done((bf16[64,128]{1,0:T(8,128)(2,1)S(1)}, bf16[64,128]{1,0:T(8,128)(2,1)S(1)}, u32[]{:S(2)}, u32[]{:S(2)}) %collective-permute-start.14) | collective-permute-done | bytes 16416 | tf_op jit(solution)/shard_map/ppermute | solution.py:189
  18.4 0.1 collective-permute-start.15
  18.5 0.5 %collective-permute-start.7 = (bf16[96,1152]{1,0:T(8,128)(2,1)S(1)}, bf16[96,1152]{1,0:T(8,128)(2,1)S(1)}, u32[]{:S(2)}, u32[]{:S(2)}) collective-permute-start(bf16[96,1152]{1,0:T(8,128)(2,1)S(1)} %collective-permute-done.6.refs_3_), channel_id=1, source_target_pairs={{0,1},{1,0},{2,3},{3,2},{4,5},{5,4},{6,7},{7,6},{8,9},{9,8},{10,11... | collective-permute-start | bytes 663560 | tf_op jit(solution)/shard_map/ppermute | solution.py:189
  19.0 0.0 collective-permute-done.9.refs_7_
  19.0 0.0 collective-permute-start.18
  19.0 0.7 %collective-permute-done.15 = bf16[128,128]{1,0:T(8,128)(2,1)S(1)} collective-permute-done((bf16[128,128]{1,0:T(8,128)(2,1)S(1)}, bf16[128,128]{1,0:T(8,128)(2,1)S(1)}, u32[]{:S(2)}, u32[]{:S(2)}) %collective-permute-start.15) | collective-permute-done | bytes 32800 | tf_op jit(solution)/shard_map/ppermute | solution.py:189
  19.7 0.2 collective-permute-start.10
  19.9 0.0 collective-permute-done.5.refs_2_
  19.9 0.3 collective-permute-start.8
  20.2 1.6 %collective-permute-done.2.refs_9_ = bf16[96,1152]{1,0:T(8,128)(2,1)S(1)} collective-permute-done((bf16[96,1152]{1,0:T(8,128)(2,1)S(1)}, bf16[96,1152]{1,0:T(8,128)(2,1)S(1)}, u32[]{:S(2)}, u32[]{:S(2)}) %collective-permute-start.2) | collective-permute-done | bytes 221216 | tf_op jit(solution)/shard_map/ppermute | solution.py:189
  21.8 0.6 %collective-permute-start.3 = (bf16[96,1152]{1,0:T(8,128)(2,1)S(1)}, bf16[96,1152]{1,0:T(8,128)(2,1)S(1)}, u32[]{:S(2)}, u32[]{:S(2)}) collective-permute-start(bf16[96,1152]{1,0:T(8,128)(2,1)S(1)} %collective-permute-done.2.refs_9_), channel_id=1, source_target_pairs={{0,4},{1,3},{4,8},{5,1},{8,12},{9,5},{12,14},{13,9},{14,10},{15,13... | collective-permute-start | bytes 663560 | tf_op jit(solution)/shard_map/ppermute | solution.py:189
  22.4 1.3 %shard_map.83 = (bf16[864,1536]{1,0:T(8,128)(2,1)S(1)}, f32[864,1]{1,0:T(8,128)S(1)}, f32[1,768]{1,0:T(1,128)S(1)}) custom-call(bf16[256,128]{1,0:T(8,128)(2,1)S(1)} %constant_dynamic-update-slice_fusion.5.g_ref), custom_call_target="tpu_custom_call" | custom-call | flops 1000 | bytes 1000 | tf_op jit(solution)/shard_map/pallas_call | solution.py:235
  23.7 0.0 collective-permute-done.7.refs_4_
  23.7 0.1 collective-permute-start.17
  23.8 1.2 %collective-permute-done.18.refs_2_ = bf16[96,1152]{1,0:T(8,128)(2,1)S(1)} collective-permute-done((bf16[96,1152]{1,0:T(8,128)(2,1)S(1)}, bf16[96,1152]{1,0:T(8,128)(2,1)S(1)}, u32[]{:S(2)}, u32[]{:S(2)}) %collective-permute-start.18) | collective-permute-done | bytes 221216 | tf_op jit(solution)/shard_map/ppermute | solution.py:189
  24.9 0.0 collective-permute-done.10.refs_8_
  24.9 0.0 collective-permute-done.8.refs_6_
  24.9 0.0 copy-start.4
  25.0 2.5 %shard_map.84.refs_6_ = f32[864,1152]{1,0:T(8,128)S(1)} custom-call(bf16[96,1152]{1,0:T(8,128)(2,1)S(1)} %collective-permute-done.4.refs_0_, bf16[96,1152]{1,0:T(8,128)(2,1)S(1)} %collective-permute-done.refs_1_, bf16[96,1152]{1,0:T(8,128)(2,1)S(1)} %collective-permute-done.5.refs_2_, bf16[96,1152]{1,0:T(8,128)(2,1)S(1)} %collective-permute-done.6.refs_3_, ...), custom_call_target="tpu_custom_call" | custom-call | flops 1000 | bytes 1000 | tf_op jit(solution)/shard_map/pallas_call | solution.py:258
  27.5 0.0 copy-start
  27.5 0.0 copy-start.1
  27.5 0.0 copy-start.2
  27.5 0.0 copy-start.3
  27.5 0.2 collective-permute-done.3.refs_4_
  27.7 0.4 collective-permute-start.16
  28.1 0.0 collective-permute-done.19.refs_3_
  28.1 2.0 %shard_map.85.refs_1_ = f32[864,1152]{1,0:T(8,128)S(1)} custom-call(bf16[96,1152]{1,0:T(8,128)(2,1)S(1)} %copy-done.4, bf16[96,1152]{1,0:T(8,128)(2,1)S(1)} %collective-permute-done.17.refs_1_, bf16[96,1152]{1,0:T(8,128)(2,1)S(1)} %collective-permute-done.18.refs_2_, ...), custom_call_target="tpu_custom_call", output_to_operand_aliasing={{}: (6, {})} | custom-call | flops 1000 | bytes 1000 | tf_op jit(solution)/shard_map/pallas_call | solution.py:258
  30.1 0.0 collective-permute-done.16.refs_0_
  30.2 5.5 %shard_map.86 = bf16[96,1152]{1,0:T(8,128)(2,1)} custom-call(bf16[96,1152]{1,0:T(8,128)(2,1)S(1)} %collective-permute-done.16.refs_0_, f32[864,1152]{1,0:T(8,128)S(1)} %shard_map.85.refs_1_, bf16[864,1536]{1,0:T(8,128)(2,1)S(1)} %get-tuple-element.11.refs_10_.refs_5_.refs_2_, f32[864,1]{1,0:T(8,128)S(1)} %get-tuple-element.13.refs_3_, ...), custom_call_target="tpu_custom_call" | custom-call | flops 2038431744 | bytes 5308416 | tf_op jit(solution)/shard_map/pallas_call | solution.py:273
  (15 shorter events, 0.1 us)
Async XLA Ops:
  0.0 5.3 %collective-permute-start.4 = (bf16[96,1152]{1,0:T(8,128)(2,1)}, bf16[96,1152]{1,0:T(8,128)(2,1)S(1)}, u32[]{:S(2)}, u32[]{:S(2)}) collective-permute-start(bf16[96,1152]{1,0:T(8,128)(2,1)} %refs_0_.1), channel_id=1, source_target_pairs={{0,1},{1,0},{2,3},{3,2},{4,5},{5,4},{6,7},{7,6},{8,9},{9,8},{10,11... | collective-permute-start | bytes 663560 | tf_op jit(solution)/shard_map/ppermute | solution.py:189
  0.5 9.3 %collective-permute-start = (bf16[96,1152]{1,0:T(8,128)(2,1)}, bf16[96,1152]{1,0:T(8,128)(2,1)S(1)}, u32[]{:S(2)}, u32[]{:S(2)}) collective-permute-start(bf16[96,1152]{1,0:T(8,128)(2,1)} %refs_0_.1), channel_id=1, source_target_pairs={{0,4},{1,3},{4,8},{5,1},{8,12},{9,5},{12,14},{13,9},{14,10},{15,13... | collective-permute-start | bytes 663560 | tf_op jit(solution)/shard_map/ppermute | solution.py:189
  3.0 7.5 %collective-permute-start.6 = (bf16[96,1152]{1,0:T(8,128)(2,1)}, bf16[96,1152]{1,0:T(8,128)(2,1)S(1)}, u32[]{:S(2)}, u32[]{:S(2)}) collective-permute-start(bf16[96,1152]{1,0:T(8,128)(2,1)} %refs_0_.1), channel_id=1, source_target_pairs={{1,4},{0,3},{5,8},{4,1},{9,12},{8,5},{13,14},{12,9},{15,10},{14,13... | collective-permute-start | bytes 663560 | tf_op jit(solution)/shard_map/ppermute | solution.py:189
  5.3 5.2 %collective-permute-start.11 = (bf16[16,128]{1,0:T(8,128)(2,1)S(1)}, bf16[16,128]{1,0:T(8,128)(2,1)S(1)}, u32[]{:S(2)}, u32[]{:S(2)}) collective-permute-start(bf16[16,128]{1,0:T(8,128)(2,1)S(1)} %shard_map.82), channel_id=1, source_target_pairs={{0,4},{1,5},{2,6},{3,7},{4,0},{5,1},{6,2},{7,3},{8,12},{9,13},{10,... | collective-permute-start | bytes 12296 | tf_op jit(solution)/shard_map/ppermute | solution.py:189
  5.8 6.4 %collective-permute-start.12 = (bf16[16,128]{1,0:T(8,128)(2,1)S(1)}, bf16[16,128]{1,0:T(8,128)(2,1)S(1)}, u32[]{:S(2)}, u32[]{:S(2)}) collective-permute-start(bf16[16,128]{1,0:T(8,128)(2,1)S(1)} %shard_map.82), channel_id=1, source_target_pairs={{0,8},{1,9},{2,10},{3,11},{4,12},{5,13},{6,14},{7,15},{8,0},{9,1},... | collective-permute-start | bytes 12296 | tf_op jit(solution)/shard_map/ppermute | solution.py:189
  8.1 5.4 %collective-permute-start.13 = (bf16[16,128]{1,0:T(8,128)(2,1)S(1)}, bf16[16,128]{1,0:T(8,128)(2,1)S(1)}, u32[]{:S(2)}, u32[]{:S(2)}) collective-permute-start(bf16[16,128]{1,0:T(8,128)(2,1)S(1)} %shard_map.82), channel_id=1, source_target_pairs={{0,12},{1,13},{2,14},{3,15},{4,8},{5,9},{6,10},{7,11},{8,4},{9,5},... | collective-permute-start | bytes 12296 | tf_op jit(solution)/shard_map/ppermute | solution.py:189
  9.8 6.1 %collective-permute-start.1 = (bf16[96,1152]{1,0:T(8,128)(2,1)S(1)}, bf16[96,1152]{1,0:T(8,128)(2,1)S(1)}, u32[]{:S(2)}, u32[]{:S(2)}) collective-permute-start(bf16[96,1152]{1,0:T(8,128)(2,1)S(1)} %collective-permute-done.refs_1_), channel_id=1, source_target_pairs={{0,4},{1,3},{4,8},{5,1},{8,12},{9,5},{12,14},{13,9},{14,10},{15,13... | collective-permute-start | bytes 663560 | tf_op jit(solution)/shard_map/ppermute | solution.py:189
  10.5 9.3 %collective-permute-start.5 = (bf16[96,1152]{1,0:T(8,128)(2,1)S(1)}, bf16[96,1152]{1,0:T(8,128)(2,1)S(1)}, u32[]{:S(2)}, u32[]{:S(2)}) collective-permute-start(bf16[96,1152]{1,0:T(8,128)(2,1)S(1)} %collective-permute-done.refs_1_), channel_id=1, source_target_pairs={{0,1},{1,0},{2,3},{3,2},{4,5},{5,4},{6,7},{7,6},{8,9},{9,8},{10,11... | collective-permute-start | bytes 663560 | tf_op jit(solution)/shard_map/ppermute | solution.py:189
  10.6 8.4 %collective-permute-start.9 = (bf16[96,1152]{1,0:T(8,128)(2,1)S(1)}, bf16[96,1152]{1,0:T(8,128)(2,1)S(1)}, u32[]{:S(2)}, u32[]{:S(2)}) collective-permute-start(bf16[96,1152]{1,0:T(8,128)(2,1)S(1)} %collective-permute-done.6.refs_3_), channel_id=1, source_target_pairs={{0,4},{1,3},{4,8},{5,1},{8,12},{9,5},{12,14},{13,9},{14,10},{15,13... | collective-permute-start | bytes 663560 | tf_op jit(solution)/shard_map/ppermute | solution.py:189
  13.6 4.8 %collective-permute-start.14 = (bf16[64,128]{1,0:T(8,128)(2,1)S(1)}, bf16[64,128]{1,0:T(8,128)(2,1)S(1)}, u32[]{:S(2)}, u32[]{:S(2)}) collective-permute-start(bf16[64,128]{1,0:T(8,128)(2,1)S(1)} %pad_maximum_fusion), channel_id=1, source_target_pairs={{0,2},{1,3},{2,0},{3,1},{4,6},{5,7},{6,4},{7,5},{8,10},{9,11},{10,... | collective-permute-start | bytes 49160 | tf_op jit(solution)/shard_map/ppermute | solution.py:189
  15.9 5.9 %collective-permute-start.2 = (bf16[96,1152]{1,0:T(8,128)(2,1)S(1)}, bf16[96,1152]{1,0:T(8,128)(2,1)S(1)}, u32[]{:S(2)}, u32[]{:S(2)}) collective-permute-start(bf16[96,1152]{1,0:T(8,128)(2,1)S(1)} %collective-permute-done.1.refs_5_), channel_id=1, source_target_pairs={{0,4},{1,3},{4,8},{5,1},{8,12},{9,5},{12,14},{13,9},{14,10},{15,13... | collective-permute-start | bytes 663560 | tf_op jit(solution)/shard_map/ppermute | solution.py:189
  18.4 1.3 %collective-permute-start.15 = (bf16[128,128]{1,0:T(8,128)(2,1)S(1)}, bf16[128,128]{1,0:T(8,128)(2,1)S(1)}, u32[]{:S(2)}, u32[]{:S(2)}) collective-permute-start(bf16[128,128]{1,0:T(8,128)(2,1)S(1)} %get-tuple-element.15), channel_id=1, source_target_pairs={{0,1},{1,0},{2,3},{3,2},{4,5},{5,4},{6,7},{7,6},{8,9},{9,8},{10,11... | collective-permute-start | bytes 98312 | tf_op jit(solution)/shard_map/ppermute | solution.py:189
  18.5 5.2 %collective-permute-start.7 = (bf16[96,1152]{1,0:T(8,128)(2,1)S(1)}, bf16[96,1152]{1,0:T(8,128)(2,1)S(1)}, u32[]{:S(2)}, u32[]{:S(2)}) collective-permute-start(bf16[96,1152]{1,0:T(8,128)(2,1)S(1)} %collective-permute-done.6.refs_3_), channel_id=1, source_target_pairs={{0,1},{1,0},{2,3},{3,2},{4,5},{5,4},{6,7},{7,6},{8,9},{9,8},{10,11... | collective-permute-start | bytes 663560 | tf_op jit(solution)/shard_map/ppermute | solution.py:189
  19.0 5.9 %collective-permute-start.18 = (bf16[96,1152]{1,0:T(8,128)(2,1)S(1)}, bf16[96,1152]{1,0:T(8,128)(2,1)S(1)}, u32[]{:S(2)}, u32[]{:S(2)}) collective-permute-start(bf16[96,1152]{1,0:T(8,128)(2,1)S(1)} %collective-permute-done.9.refs_7_), channel_id=1, source_target_pairs={{0,4},{1,3},{4,8},{5,1},{8,12},{9,5},{12,14},{13,9},{14,10},{15,13... | collective-permute-start | bytes 663560 | tf_op jit(solution)/shard_map/ppermute | solution.py:189
  19.7 5.2 %collective-permute-start.10 = (bf16[96,1152]{1,0:T(8,128)(2,1)S(1)}, bf16[96,1152]{1,0:T(8,128)(2,1)S(1)}, u32[]{:S(2)}, u32[]{:S(2)}) collective-permute-start(bf16[96,1152]{1,0:T(8,128)(2,1)S(1)} %collective-permute-done.9.refs_7_), channel_id=1, source_target_pairs={{0,1},{1,0},{2,3},{3,2},{4,5},{5,4},{6,7},{7,6},{8,9},{9,8},{10,11... | collective-permute-start | bytes 663560 | tf_op jit(solution)/shard_map/ppermute | solution.py:189
  19.9 5.1 %collective-permute-start.8 = (bf16[96,1152]{1,0:T(8,128)(2,1)S(1)}, bf16[96,1152]{1,0:T(8,128)(2,1)S(1)}, u32[]{:S(2)}, u32[]{:S(2)}) collective-permute-start(bf16[96,1152]{1,0:T(8,128)(2,1)S(1)} %collective-permute-done.1.refs_5_), channel_id=1, source_target_pairs={{0,1},{1,0},{2,3},{3,2},{4,5},{5,4},{6,7},{7,6},{8,9},{9,8},{10,11... | collective-permute-start | bytes 663560 | tf_op jit(solution)/shard_map/ppermute | solution.py:189
  21.8 5.9 %collective-permute-start.3 = (bf16[96,1152]{1,0:T(8,128)(2,1)S(1)}, bf16[96,1152]{1,0:T(8,128)(2,1)S(1)}, u32[]{:S(2)}, u32[]{:S(2)}) collective-permute-start(bf16[96,1152]{1,0:T(8,128)(2,1)S(1)} %collective-permute-done.2.refs_9_), channel_id=1, source_target_pairs={{0,4},{1,3},{4,8},{5,1},{8,12},{9,5},{12,14},{13,9},{14,10},{15,13... | collective-permute-start | bytes 663560 | tf_op jit(solution)/shard_map/ppermute | solution.py:189
  23.7 4.4 %collective-permute-start.17 = (bf16[96,1152]{1,0:T(8,128)(2,1)S(1)}, bf16[96,1152]{1,0:T(8,128)(2,1)S(1)}, u32[]{:S(2)}, u32[]{:S(2)}) collective-permute-start(bf16[96,1152]{1,0:T(8,128)(2,1)S(1)} %collective-permute-done.2.refs_9_), channel_id=1, source_target_pairs={{0,1},{1,0},{2,3},{3,2},{4,5},{5,4},{6,7},{7,6},{8,9},{9,8},{10,11... | collective-permute-start | bytes 663560 | tf_op jit(solution)/shard_map/ppermute | solution.py:189
  24.9 3.2 %collective-permute-start.19 = (bf16[96,1152]{1,0:T(8,128)(2,1)S(1)}, bf16[96,1152]{1,0:T(8,128)(2,1)S(1)}, u32[]{:S(2)}, u32[]{:S(2)}) collective-permute-start(bf16[96,1152]{1,0:T(8,128)(2,1)S(1)} %collective-permute-done.18.refs_2_), channel_id=1, source_target_pairs={{0,1},{1,0},{2,3},{3,2},{4,5},{5,4},{6,7},{7,6},{8,9},{9,8},{10,11... | collective-permute-start | bytes 663560 | tf_op jit(solution)/shard_map/ppermute | solution.py:189
  24.9 3.2 %copy-start.4 = (bf16[96,1152]{1,0:T(8,128)(2,1)S(1)}, bf16[96,1152]{1,0:T(8,128)(2,1)}, u32[]{:S(2)}) copy-start(bf16[96,1152]{1,0:T(8,128)(2,1)} %refs_0_.1) | copy-start | bytes 663556
  27.5 2.6 %copy-start = (bf16[1152,576]{0,1:T(8,128)(2,1)S(1)}, bf16[1152,576]{0,1:T(8,128)(2,1)}, u32[]{:S(2)}) copy-start(bf16[1152,576]{0,1:T(8,128)(2,1)} %param.12) | copy-start | bytes 3981316
  27.5 2.6 %copy-start.1 = (bf16[1152,576]{0,1:T(8,128)(2,1)S(1)}, bf16[1152,576]{0,1:T(8,128)(2,1)}, u32[]{:S(2)}) copy-start(bf16[1152,576]{0,1:T(8,128)(2,1)} %param.13) | copy-start | bytes 3981316
  27.5 2.6 %copy-start.2 = (bf16[1152,576]{0,1:T(8,128)(2,1)S(1)}, bf16[1152,576]{0,1:T(8,128)(2,1)}, u32[]{:S(2)}) copy-start(bf16[1152,576]{0,1:T(8,128)(2,1)} %param.14) | copy-start | bytes 3981316
  27.5 2.6 %copy-start.3 = (bf16[576,1152]{1,0:T(8,128)(2,1)S(1)}, bf16[576,1152]{1,0:T(8,128)(2,1)}, u32[]{:S(2)}) copy-start(bf16[576,1152]{1,0:T(8,128)(2,1)} %refs_8_.1) | copy-start | bytes 3981316
  27.7 2.4 %collective-permute-start.16 = (bf16[96,1152]{1,0:T(8,128)(2,1)S(1)}, bf16[96,1152]{1,0:T(8,128)(2,1)S(1)}, u32[]{:S(2)}, u32[]{:S(2)}) collective-permute-start(bf16[96,1152]{1,0:T(8,128)(2,1)S(1)} %collective-permute-done.3.refs_4_), channel_id=1, source_target_pairs={{0,1},{1,0},{2,3},{3,2},{4,5},{5,4},{6,7},{7,6},{8,9},{9,8},{10,11... | collective-permute-start | bytes 663560 | tf_op jit(solution)/shard_map/ppermute | solution.py:189

commit v6 on v5

--- a/solution.py
+++ b/solution.py
@@ -87,7 +87,7 @@
 
 
 def prep_kernel(
-    shards, slots, tok, merged_rows, g_ref,
+    shards, slots, tok, merged_rows, starts, g_ref,
     m_ref, inv_ref, bias_ref, gf, dest_row, size_row,
 ):
     me = lax.axis_index("ctx")
@@ -98,6 +98,8 @@
     places = shards * META
     bucket = lax.broadcasted_iota(jnp.int32, (places, LANES), 0)
     sender_iota = lax.broadcasted_iota(jnp.int32, (shards, LANES), 0)
+    dest_row[...] = jnp.full(dest_row.shape, -1.0, F32)
+    size_row[...] = jnp.zeros(size_row.shape, F32)
     for j, e in enumerate(senders(shards, me)):
         base = flip(e ^ me, shards) * META
         own = gf[pl.ds(base + slots, 1), :].astype(jnp.int32)
@@ -107,8 +109,8 @@
         found = dot(by_sender, hot)
         slot = jnp.sum(jnp.where(sender_iota == e, found, 0.0), axis=0, keepdims=True)
         dest = own.astype(F32) * merged_rows + slot
-        dest_row[:, j * tok : (j + 1) * tok] = dest[:, :tok]
-        size_row[:, j * tok : (j + 1) * tok] = size[:, :tok]
+        dest_row[:, starts[j] : starts[j] + tok] = dest[:, :tok]
+        size_row[:, starts[j] : starts[j] + tok] = size[:, :tok]
         if j == shards - 6:
             mine = dest
     mine = jnp.broadcast_to(mine, (8, LANES))
@@ -117,7 +119,7 @@
     slot_of_row = lax.broadcasted_iota(jnp.int32, (total, LANES), 0).astype(F32)
     slot_of_row = jnp.concatenate([slot_of_row, mine], axis=0)
     count = jnp.zeros(slot_of_row.shape, F32)
-    for b in range(shards * tok // LANES):
+    for b in range(m_ref.shape[1] // LANES):
         cols = slice(b * LANES, (b + 1) * LANES)
         piece = jnp.where(slot_of_row == dest_row[:, cols], size_row[:, cols], 0.0)
         count = count + piece
@@ -151,7 +153,7 @@
     (acc_ref, m_ref, inv_ref, bias_ref, wq_ref, wk_ref, wv_ref, wo_ref, out_ref,
      tok_s, merged_s, att_s) = refs[n_blocks:]
     gather_blocks(blocks, tok_s)
-    acc = acc_ref[...] + dot(m_ref[:, first:], tok_s[...])
+    acc = acc_ref[...] + dot(m_ref[:, first : first + tok_s.shape[0]], tok_s[...])
     merged_s[...] = (acc * inv_ref[...]).astype(BF16)
     total = bias_ref.shape[1]
     merged = merged_s[:total, :]
@@ -232,10 +234,15 @@
         if s < shards // 4 - 1:
             b = send(b, along)
     rows = total + tok
+    cuts = [0, shards - 6, shards - 1, shards]
+    starts, lanes = [], 0
+    for low, high in zip(cuts[:-1], cuts[1:]):
+        starts += [lanes + i * tok for i in range(high - low)]
+        lanes += -(-(high - low) * tok // LANES) * LANES
     m, inv, bias = pl.pallas_call(
-        functools.partial(prep_kernel, shards, slots, tok, merged_rows),
+        functools.partial(prep_kernel, shards, slots, tok, merged_rows, tuple(starts)),
         out_shape=(
-            jax.ShapeDtypeStruct((rows, shards * tok), BF16),
+            jax.ShapeDtypeStruct((rows, lanes), BF16),
             jax.ShapeDtypeStruct((rows, 1), F32),
             jax.ShapeDtypeStruct((1, total), F32),
         ),
@@ -243,20 +250,19 @@
         out_specs=(vmem,) * 3,
         scratch_shapes=[
             pltpu.VMEM((shards * META, LANES), F32),
-            pltpu.VMEM((1, shards * tok), F32),
-            pltpu.VMEM((1, shards * tok), F32),
+            pltpu.VMEM((1, lanes), F32),
+            pltpu.VMEM((1, lanes), F32),
         ],
         compiler_params=pltpu.CompilerParams(vmem_limit_bytes=VMEM_PREP),
         cost_estimate=cost(1000, 1000),
     )(jnp.concatenate(metas, axis=0))
     blocks = blocks[1 : 1 + shards - 6] + [tokens] + blocks[1 + shards - 6 :]
-    cuts = [0, shards - 6, shards - 1, shards]
     acc = []
     for low, high in zip(cuts[:-2], cuts[1:-1]):
         n = high - low
         acc = [
             pl.pallas_call(
-                functools.partial(merge_kernel, n, low * tok),
+                functools.partial(merge_kernel, n, starts[low]),
                 out_shape=jax.ShapeDtypeStruct((rows, width), F32),
                 in_specs=[vmem] * (n + 1 + len(acc)),
                 out_specs=vmem,
@@ -271,7 +277,7 @@
     low, high = cuts[-2:]
     n = high - low
     return pl.pallas_call(
-        functools.partial(tail_kernel, n, low * tok),
+        functools.partial(tail_kernel, n, starts[low]),
         out_shape=jax.ShapeDtypeStruct((tok, width), BF16),
         in_specs=[vmem] * (n + 8),
         out_specs=vmem,

time: 35.8 us -> 35.7 us (level)
  transfers between devices with their start and end apart: 20 -> 20, of which waited for: 7 -> 7; matrix products, arithmetic and copies ran while one was open for 2% -> 2% of each run, Pallas kernels for 17% -> 16%
where the time goes in v6:
time: 35.7 us; the launch traced here: 35.4 us
  starting transfers between devices  14.7 us (41%)
  Pallas kernels  11.2 us (31%)
  waiting for transfers between devices  8.49 us (24%)
  other arithmetic  0.73 us (2%)
    ppermute x20, starting transfers between devices, send(): return lax.ppermute(x, 'ctx', pairs)  14.7 us
    ppermute x20, waiting for transfers between devices, send(): return lax.ppermute(x, 'ctx', pairs)  8.49 us
    pallas_call x1, Pallas kernels, on_device_gathered(): pl.pallas_call(functools.partial(tail_kernel, n, starts[low]), out_shape=...  5.41 us
    pallas_call x2, Pallas kernels, on_device_gathered(): pl.pallas_call(functools.partial(merge_kernel, n, starts[low]), out_shape...  4.3 us
    pallas_call x1, Pallas kernels, on_device_gathered(): pl.pallas_call(functools.partial(prep_kernel, shards, slots, tok, merged_...  1.33 us
    concatenate x1, other arithmetic, on_device_gathered(): jnp.concatenate([jnp.pad(x, ((0, 0), (0, 0), (0, LANES - x.shape[2]))) fo...  0.73 us
  transfers between devices with their start and end apart: 20, of which 7 were waited for; matrix products, arithmetic and copies ran while one was open for 2% of the time, Pallas kernels for 16%

profile of v6, /device:TPU:0, one launch (start us, length us, event | category | flops | bytes accessed | tf_op | source)
XLA Modules:
  0.0 35.4 jit_solution(18442420989032763797)
XLA Ops:
  0.0 0.5 %collective-permute-start.4 = (bf16[96,1152]{1,0:T(8,128)(2,1)}, bf16[96,1152]{1,0:T(8,128)(2,1)S(1)}, u32[]{:S(2)}, u32[]{:S(2)}) collective-permute-start(bf16[96,1152]{1,0:T(8,128)(2,1)} %refs_0_.1), channel_id=1, source_target_pairs={{0,1},{1,0},{2,3},{3,2},{4,5},{5,4},{6,7},{7,6},{8,9},{9,8},{10,11... | collective-permute-start | bytes 663560 | tf_op jit(solution)/shard_map/ppermute | solution.py:191
  0.5 2.6 %collective-permute-start = (bf16[96,1152]{1,0:T(8,128)(2,1)}, bf16[96,1152]{1,0:T(8,128)(2,1)S(1)}, u32[]{:S(2)}, u32[]{:S(2)}) collective-permute-start(bf16[96,1152]{1,0:T(8,128)(2,1)} %refs_0_.1), channel_id=1, source_target_pairs={{0,4},{1,3},{4,8},{5,1},{8,12},{9,5},{12,14},{13,9},{14,10},{15,13... | collective-permute-start | bytes 663560 | tf_op jit(solution)/shard_map/ppermute | solution.py:191
  3.0 1.4 %collective-permute-start.6 = (bf16[96,1152]{1,0:T(8,128)(2,1)}, bf16[96,1152]{1,0:T(8,128)(2,1)S(1)}, u32[]{:S(2)}, u32[]{:S(2)}) collective-permute-start(bf16[96,1152]{1,0:T(8,128)(2,1)} %refs_0_.1), channel_id=1, source_target_pairs={{1,4},{0,3},{5,8},{4,1},{9,12},{8,5},{13,14},{12,9},{15,10},{14,13... | collective-permute-start | bytes 663560 | tf_op jit(solution)/shard_map/ppermute | solution.py:191
  4.4 0.7 %pad_add_fusion.given_ref = s32[14,1,128]{2,1,0:T(1,128)S(1)} fusion(s32[1,1,96]{2,1,0:T(1,128)} %bitcast.10, s32[1,1,96]{2,1,0:T(1,128)} %bitcast.11, s32[12,1,16]{2,1,0:T(1,128)} %bitcast.9), kind=kLoop, calls=%fused_computation.12 | loop fusion | flops 3584 | bytes 8704 | tf_op jit(solution)/shard_map/concatenate | solution.py:195
  5.1 0.2 shard_map.82
  5.3 0.0 collective-permute-done.4.refs_0_
  5.3 0.5 %collective-permute-start.11 = (bf16[16,128]{1,0:T(8,128)(2,1)S(1)}, bf16[16,128]{1,0:T(8,128)(2,1)S(1)}, u32[]{:S(2)}, u32[]{:S(2)}) collective-permute-start(bf16[16,128]{1,0:T(8,128)(2,1)S(1)} %shard_map.82), channel_id=1, source_target_pairs={{0,4},{1,5},{2,6},{3,7},{4,0},{5,1},{6,2},{7,3},{8,12},{9,13},{10,... | collective-permute-start | bytes 12296 | tf_op jit(solution)/shard_map/ppermute | solution.py:191
  5.8 2.3 %collective-permute-start.12 = (bf16[16,128]{1,0:T(8,128)(2,1)S(1)}, bf16[16,128]{1,0:T(8,128)(2,1)S(1)}, u32[]{:S(2)}, u32[]{:S(2)}) collective-permute-start(bf16[16,128]{1,0:T(8,128)(2,1)S(1)} %shard_map.82), channel_id=1, source_target_pairs={{0,8},{1,9},{2,10},{3,11},{4,12},{5,13},{6,14},{7,15},{8,0},{9,1},... | collective-permute-start | bytes 12296 | tf_op jit(solution)/shard_map/ppermute | solution.py:191
  8.1 1.6 %collective-permute-start.13 = (bf16[16,128]{1,0:T(8,128)(2,1)S(1)}, bf16[16,128]{1,0:T(8,128)(2,1)S(1)}, u32[]{:S(2)}, u32[]{:S(2)}) collective-permute-start(bf16[16,128]{1,0:T(8,128)(2,1)S(1)} %shard_map.82), channel_id=1, source_target_pairs={{0,12},{1,13},{2,14},{3,15},{4,8},{5,9},{6,10},{7,11},{8,4},{9,5},... | collective-permute-start | bytes 12296 | tf_op jit(solution)/shard_map/ppermute | solution.py:191
  9.8 0.0 collective-permute-done.refs_1_
  9.8 0.8 %collective-permute-start.1 = (bf16[96,1152]{1,0:T(8,128)(2,1)S(1)}, bf16[96,1152]{1,0:T(8,128)(2,1)S(1)}, u32[]{:S(2)}, u32[]{:S(2)}) collective-permute-start(bf16[96,1152]{1,0:T(8,128)(2,1)S(1)} %collective-permute-done.refs_1_), channel_id=1, source_target_pairs={{0,4},{1,3},{4,8},{5,1},{8,12},{9,5},{12,14},{13,9},{14,10},{15,13... | collective-permute-start | bytes 663560 | tf_op jit(solution)/shard_map/ppermute | solution.py:191
  10.5 0.0 collective-permute-done.6.refs_3_
  10.5 0.0 collective-permute-start.5
  10.5 0.0 collective-permute-done.11
  10.6 1.6 %collective-permute-start.9 = (bf16[96,1152]{1,0:T(8,128)(2,1)S(1)}, bf16[96,1152]{1,0:T(8,128)(2,1)S(1)}, u32[]{:S(2)}, u32[]{:S(2)}) collective-permute-start(bf16[96,1152]{1,0:T(8,128)(2,1)S(1)} %collective-permute-done.6.refs_3_), channel_id=1, source_target_pairs={{0,4},{1,3},{4,8},{5,1},{8,12},{9,5},{12,14},{13,9},{14,10},{15,13... | collective-permute-start | bytes 663560 | tf_op jit(solution)/shard_map/ppermute | solution.py:191
  12.2 0.0 collective-permute-done.12
  12.2 1.4 %collective-permute-done.13 = bf16[16,128]{1,0:T(8,128)(2,1)S(1)} collective-permute-done((bf16[16,128]{1,0:T(8,128)(2,1)S(1)}, bf16[16,128]{1,0:T(8,128)(2,1)S(1)}, u32[]{:S(2)}, u32[]{:S(2)}) %collective-permute-start.13) | collective-permute-done | bytes 4128 | tf_op jit(solution)/shard_map/ppermute | solution.py:191
  13.6 0.7 %collective-permute-start.14 = (bf16[64,128]{1,0:T(8,128)(2,1)S(1)}, bf16[64,128]{1,0:T(8,128)(2,1)S(1)}, u32[]{:S(2)}, u32[]{:S(2)}) collective-permute-start(bf16[64,128]{1,0:T(8,128)(2,1)S(1)} %pad_maximum_fusion), channel_id=1, source_target_pairs={{0,2},{1,3},{2,0},{3,1},{4,6},{5,7},{6,4},{7,5},{8,10},{9,11},{10,... | collective-permute-start | bytes 49160 | tf_op jit(solution)/shard_map/ppermute | solution.py:191
  14.3 1.5 %collective-permute-done.1.refs_5_ = bf16[96,1152]{1,0:T(8,128)(2,1)S(1)} collective-permute-done((bf16[96,1152]{1,0:T(8,128)(2,1)S(1)}, bf16[96,1152]{1,0:T(8,128)(2,1)S(1)}, u32[]{:S(2)}, u32[]{:S(2)}) %collective-permute-start.1) | collective-permute-done | bytes 221216 | tf_op jit(solution)/shard_map/ppermute | solution.py:191
  15.9 0.6 %collective-permute-start.2 = (bf16[96,1152]{1,0:T(8,128)(2,1)S(1)}, bf16[96,1152]{1,0:T(8,128)(2,1)S(1)}, u32[]{:S(2)}, u32[]{:S(2)}) collective-permute-start(bf16[96,1152]{1,0:T(8,128)(2,1)S(1)} %collective-permute-done.1.refs_5_), channel_id=1, source_target_pairs={{0,4},{1,3},{4,8},{5,1},{8,12},{9,5},{12,14},{13,9},{14,10},{15,13... | collective-permute-start | bytes 663560 | tf_op jit(solution)/shard_map/ppermute | solution.py:191
  16.5 1.9 %collective-permute-done.14 = bf16[64,128]{1,0:T(8,128)(2,1)S(1)} collective-permute-done((bf16[64,128]{1,0:T(8,128)(2,1)S(1)}, bf16[64,128]{1,0:T(8,128)(2,1)S(1)}, u32[]{:S(2)}, u32[]{:S(2)}) %collective-permute-start.14) | collective-permute-done | bytes 16416 | tf_op jit(solution)/shard_map/ppermute | solution.py:191
  18.4 0.1 collective-permute-start.15
  18.5 0.5 %collective-permute-start.7 = (bf16[96,1152]{1,0:T(8,128)(2,1)S(1)}, bf16[96,1152]{1,0:T(8,128)(2,1)S(1)}, u32[]{:S(2)}, u32[]{:S(2)}) collective-permute-start(bf16[96,1152]{1,0:T(8,128)(2,1)S(1)} %collective-permute-done.6.refs_3_), channel_id=1, source_target_pairs={{0,1},{1,0},{2,3},{3,2},{4,5},{5,4},{6,7},{7,6},{8,9},{9,8},{10,11... | collective-permute-start | bytes 663560 | tf_op jit(solution)/shard_map/ppermute | solution.py:191
  19.0 0.0 collective-permute-done.9.refs_7_
  19.0 0.7 %collective-permute-done.15 = bf16[128,128]{1,0:T(8,128)(2,1)S(1)} collective-permute-done((bf16[128,128]{1,0:T(8,128)(2,1)S(1)}, bf16[128,128]{1,0:T(8,128)(2,1)S(1)}, u32[]{:S(2)}, u32[]{:S(2)}) %collective-permute-start.15) | collective-permute-done | bytes 32800 | tf_op jit(solution)/shard_map/ppermute | solution.py:191
  19.7 0.2 collective-permute-start.10
  19.9 0.0 collective-permute-done.5.refs_2_
  19.9 0.3 collective-permute-start.8
  20.2 1.6 %collective-permute-done.2.refs_9_ = bf16[96,1152]{1,0:T(8,128)(2,1)S(1)} collective-permute-done((bf16[96,1152]{1,0:T(8,128)(2,1)S(1)}, bf16[96,1152]{1,0:T(8,128)(2,1)S(1)}, u32[]{:S(2)}, u32[]{:S(2)}) %collective-permute-start.2) | collective-permute-done | bytes 221216 | tf_op jit(solution)/shard_map/ppermute | solution.py:191
  21.8 0.6 %collective-permute-start.3 = (bf16[96,1152]{1,0:T(8,128)(2,1)S(1)}, bf16[96,1152]{1,0:T(8,128)(2,1)S(1)}, u32[]{:S(2)}, u32[]{:S(2)}) collective-permute-start(bf16[96,1152]{1,0:T(8,128)(2,1)S(1)} %collective-permute-done.2.refs_9_), channel_id=1, source_target_pairs={{0,4},{1,3},{4,8},{5,1},{8,12},{9,5},{12,14},{13,9},{14,10},{15,13... | collective-permute-start | bytes 663560 | tf_op jit(solution)/shard_map/ppermute | solution.py:191
  22.4 1.3 %shard_map.83 = (bf16[864,1664]{1,0:T(8,128)(2,1)S(1)}, f32[864,1]{1,0:T(8,128)S(1)}, f32[1,768]{1,0:T(1,128)S(1)}) custom-call(bf16[256,128]{1,0:T(8,128)(2,1)S(1)} %constant_dynamic-update-slice_fusion.5.g_ref), custom_call_target="tpu_custom_call" | custom-call | flops 1000 | bytes 1000 | tf_op jit(solution)/shard_map/pallas_call | solution.py:242
  23.8 0.0 collective-permute-done.7.refs_4_
  23.8 0.1 collective-permute-start.17
  23.8 1.1 %collective-permute-done.18.refs_2_ = bf16[96,1152]{1,0:T(8,128)(2,1)S(1)} collective-permute-done((bf16[96,1152]{1,0:T(8,128)(2,1)S(1)}, bf16[96,1152]{1,0:T(8,128)(2,1)S(1)}, u32[]{:S(2)}, u32[]{:S(2)}) %collective-permute-start.18) | collective-permute-done | bytes 221216 | tf_op jit(solution)/shard_map/ppermute | solution.py:191
  24.9 0.0 collective-permute-start.19
  24.9 0.0 collective-permute-done.10.refs_8_
  24.9 0.0 copy-start.4
  25.0 2.5 %shard_map.84.refs_6_ = f32[864,1152]{1,0:T(8,128)S(1)} custom-call(bf16[96,1152]{1,0:T(8,128)(2,1)S(1)} %collective-permute-done.4.refs_0_, bf16[96,1152]{1,0:T(8,128)(2,1)S(1)} %collective-permute-done.refs_1_, bf16[96,1152]{1,0:T(8,128)(2,1)S(1)} %collective-permute-done.5.refs_2_, bf16[96,1152]{1,0:T(8,128)(2,1)S(1)} %collective-permute-done.6.refs_3_, ...), custom_call_target="tpu_custom_call" | custom-call | flops 1000 | bytes 1000 | tf_op jit(solution)/shard_map/pallas_call | solution.py:264
  27.5 0.0 copy-start
  27.5 0.0 copy-start.1
  27.5 0.0 copy-start.2
  27.5 0.0 copy-start.3
  27.5 0.2 collective-permute-done.3.refs_4_
  27.7 0.4 %collective-permute-start.16 = (bf16[96,1152]{1,0:T(8,128)(2,1)S(1)}, bf16[96,1152]{1,0:T(8,128)(2,1)S(1)}, u32[]{:S(2)}, u32[]{:S(2)}) collective-permute-start(bf16[96,1152]{1,0:T(8,128)(2,1)S(1)} %collective-permute-done.3.refs_4_), channel_id=1, source_target_pairs={{0,1},{1,0},{2,3},{3,2},{4,5},{5,4},{6,7},{7,6},{8,9},{9,8},{10,11... | collective-permute-start | bytes 663560 | tf_op jit(solution)/shard_map/ppermute | solution.py:191
  28.1 1.8 %shard_map.85.refs_1_ = f32[864,1152]{1,0:T(8,128)S(1)} custom-call(bf16[96,1152]{1,0:T(8,128)(2,1)S(1)} %copy-done.4, bf16[96,1152]{1,0:T(8,128)(2,1)S(1)} %collective-permute-done.17.refs_1_, bf16[96,1152]{1,0:T(8,128)(2,1)S(1)} %collective-permute-done.18.refs_2_, ...), custom_call_target="tpu_custom_call", output_to_operand_aliasing={{}: (6, {})} | custom-call | flops 1000 | bytes 1000 | tf_op jit(solution)/shard_map/pallas_call | solution.py:264
  29.9 0.0 collective-permute-done.16.refs_0_
  29.9 0.1 copy-done.3
  30.0 5.4 %shard_map.86 = bf16[96,1152]{1,0:T(8,128)(2,1)} custom-call(bf16[96,1152]{1,0:T(8,128)(2,1)S(1)} %collective-permute-done.16.refs_0_, f32[864,1152]{1,0:T(8,128)S(1)} %shard_map.85.refs_1_, bf16[864,1664]{1,0:T(8,128)(2,1)S(1)} %get-tuple-element.11.refs_10_.refs_5_.refs_2_, f32[864,1]{1,0:T(8,128)S(1)} %get-tuple-element.13.refs_3_, ...), custom_call_target="tpu_custom_call" | custom-call | flops 2038431744 | bytes 5308416 | tf_op jit(solution)/shard_map/pallas_call | solution.py:279
  (15 shorter events, 0.1 us)
Async XLA Ops:
  0.0 5.3 %collective-permute-start.4 = (bf16[96,1152]{1,0:T(8,128)(2,1)}, bf16[96,1152]{1,0:T(8,128)(2,1)S(1)}, u32[]{:S(2)}, u32[]{:S(2)}) collective-permute-start(bf16[96,1152]{1,0:T(8,128)(2,1)} %refs_0_.1), channel_id=1, source_target_pairs={{0,1},{1,0},{2,3},{3,2},{4,5},{5,4},{6,7},{7,6},{8,9},{9,8},{10,11... | collective-permute-start | bytes 663560 | tf_op jit(solution)/shard_map/ppermute | solution.py:191
  0.5 9.3 %collective-permute-start = (bf16[96,1152]{1,0:T(8,128)(2,1)}, bf16[96,1152]{1,0:T(8,128)(2,1)S(1)}, u32[]{:S(2)}, u32[]{:S(2)}) collective-permute-start(bf16[96,1152]{1,0:T(8,128)(2,1)} %refs_0_.1), channel_id=1, source_target_pairs={{0,4},{1,3},{4,8},{5,1},{8,12},{9,5},{12,14},{13,9},{14,10},{15,13... | collective-permute-start | bytes 663560 | tf_op jit(solution)/shard_map/ppermute | solution.py:191
  3.0 7.5 %collective-permute-start.6 = (bf16[96,1152]{1,0:T(8,128)(2,1)}, bf16[96,1152]{1,0:T(8,128)(2,1)S(1)}, u32[]{:S(2)}, u32[]{:S(2)}) collective-permute-start(bf16[96,1152]{1,0:T(8,128)(2,1)} %refs_0_.1), channel_id=1, source_target_pairs={{1,4},{0,3},{5,8},{4,1},{9,12},{8,5},{13,14},{12,9},{15,10},{14,13... | collective-permute-start | bytes 663560 | tf_op jit(solution)/shard_map/ppermute | solution.py:191
  5.3 5.2 %collective-permute-start.11 = (bf16[16,128]{1,0:T(8,128)(2,1)S(1)}, bf16[16,128]{1,0:T(8,128)(2,1)S(1)}, u32[]{:S(2)}, u32[]{:S(2)}) collective-permute-start(bf16[16,128]{1,0:T(8,128)(2,1)S(1)} %shard_map.82), channel_id=1, source_target_pairs={{0,4},{1,5},{2,6},{3,7},{4,0},{5,1},{6,2},{7,3},{8,12},{9,13},{10,... | collective-permute-start | bytes 12296 | tf_op jit(solution)/shard_map/ppermute | solution.py:191
  5.8 6.4 %collective-permute-start.12 = (bf16[16,128]{1,0:T(8,128)(2,1)S(1)}, bf16[16,128]{1,0:T(8,128)(2,1)S(1)}, u32[]{:S(2)}, u32[]{:S(2)}) collective-permute-start(bf16[16,128]{1,0:T(8,128)(2,1)S(1)} %shard_map.82), channel_id=1, source_target_pairs={{0,8},{1,9},{2,10},{3,11},{4,12},{5,13},{6,14},{7,15},{8,0},{9,1},... | collective-permute-start | bytes 12296 | tf_op jit(solution)/shard_map/ppermute | solution.py:191
  8.1 5.4 %collective-permute-start.13 = (bf16[16,128]{1,0:T(8,128)(2,1)S(1)}, bf16[16,128]{1,0:T(8,128)(2,1)S(1)}, u32[]{:S(2)}, u32[]{:S(2)}) collective-permute-start(bf16[16,128]{1,0:T(8,128)(2,1)S(1)} %shard_map.82), channel_id=1, source_target_pairs={{0,12},{1,13},{2,14},{3,15},{4,8},{5,9},{6,10},{7,11},{8,4},{9,5},... | collective-permute-start | bytes 12296 | tf_op jit(solution)/shard_map/ppermute | solution.py:191
  9.8 6.1 %collective-permute-start.1 = (bf16[96,1152]{1,0:T(8,128)(2,1)S(1)}, bf16[96,1152]{1,0:T(8,128)(2,1)S(1)}, u32[]{:S(2)}, u32[]{:S(2)}) collective-permute-start(bf16[96,1152]{1,0:T(8,128)(2,1)S(1)} %collective-permute-done.refs_1_), channel_id=1, source_target_pairs={{0,4},{1,3},{4,8},{5,1},{8,12},{9,5},{12,14},{13,9},{14,10},{15,13... | collective-permute-start | bytes 663560 | tf_op jit(solution)/shard_map/ppermute | solution.py:191
  10.5 9.3 %collective-permute-start.5 = (bf16[96,1152]{1,0:T(8,128)(2,1)S(1)}, bf16[96,1152]{1,0:T(8,128)(2,1)S(1)}, u32[]{:S(2)}, u32[]{:S(2)}) collective-permute-start(bf16[96,1152]{1,0:T(8,128)(2,1)S(1)} %collective-permute-done.refs_1_), channel_id=1, source_target_pairs={{0,1},{1,0},{2,3},{3,2},{4,5},{5,4},{6,7},{7,6},{8,9},{9,8},{10,11... | collective-permute-start | bytes 663560 | tf_op jit(solution)/shard_map/ppermute | solution.py:191
  10.6 8.4 %collective-permute-start.9 = (bf16[96,1152]{1,0:T(8,128)(2,1)S(1)}, bf16[96,1152]{1,0:T(8,128)(2,1)S(1)}, u32[]{:S(2)}, u32[]{:S(2)}) collective-permute-start(bf16[96,1152]{1,0:T(8,128)(2,1)S(1)} %collective-permute-done.6.refs_3_), channel_id=1, source_target_pairs={{0,4},{1,3},{4,8},{5,1},{8,12},{9,5},{12,14},{13,9},{14,10},{15,13... | collective-permute-start | bytes 663560 | tf_op jit(solution)/shard_map/ppermute | solution.py:191
  13.6 4.8 %collective-permute-start.14 = (bf16[64,128]{1,0:T(8,128)(2,1)S(1)}, bf16[64,128]{1,0:T(8,128)(2,1)S(1)}, u32[]{:S(2)}, u32[]{:S(2)}) collective-permute-start(bf16[64,128]{1,0:T(8,128)(2,1)S(1)} %pad_maximum_fusion), channel_id=1, source_target_pairs={{0,2},{1,3},{2,0},{3,1},{4,6},{5,7},{6,4},{7,5},{8,10},{9,11},{10,... | collective-permute-start | bytes 49160 | tf_op jit(solution)/shard_map/ppermute | solution.py:191
  15.9 5.9 %collective-permute-start.2 = (bf16[96,1152]{1,0:T(8,128)(2,1)S(1)}, bf16[96,1152]{1,0:T(8,128)(2,1)S(1)}, u32[]{:S(2)}, u32[]{:S(2)}) collective-permute-start(bf16[96,1152]{1,0:T(8,128)(2,1)S(1)} %collective-permute-done.1.refs_5_), channel_id=1, source_target_pairs={{0,4},{1,3},{4,8},{5,1},{8,12},{9,5},{12,14},{13,9},{14,10},{15,13... | collective-permute-start | bytes 663560 | tf_op jit(solution)/shard_map/ppermute | solution.py:191
  18.4 1.3 %collective-permute-start.15 = (bf16[128,128]{1,0:T(8,128)(2,1)S(1)}, bf16[128,128]{1,0:T(8,128)(2,1)S(1)}, u32[]{:S(2)}, u32[]{:S(2)}) collective-permute-start(bf16[128,128]{1,0:T(8,128)(2,1)S(1)} %get-tuple-element.15), channel_id=1, source_target_pairs={{0,1},{1,0},{2,3},{3,2},{4,5},{5,4},{6,7},{7,6},{8,9},{9,8},{10,11... | collective-permute-start | bytes 98312 | tf_op jit(solution)/shard_map/ppermute | solution.py:191
  18.5 5.3 %collective-permute-start.7 = (bf16[96,1152]{1,0:T(8,128)(2,1)S(1)}, bf16[96,1152]{1,0:T(8,128)(2,1)S(1)}, u32[]{:S(2)}, u32[]{:S(2)}) collective-permute-start(bf16[96,1152]{1,0:T(8,128)(2,1)S(1)} %collective-permute-done.6.refs_3_), channel_id=1, source_target_pairs={{0,1},{1,0},{2,3},{3,2},{4,5},{5,4},{6,7},{7,6},{8,9},{9,8},{10,11... | collective-permute-start | bytes 663560 | tf_op jit(solution)/shard_map/ppermute | solution.py:191
  19.0 5.9 %collective-permute-start.18 = (bf16[96,1152]{1,0:T(8,128)(2,1)S(1)}, bf16[96,1152]{1,0:T(8,128)(2,1)S(1)}, u32[]{:S(2)}, u32[]{:S(2)}) collective-permute-start(bf16[96,1152]{1,0:T(8,128)(2,1)S(1)} %collective-permute-done.9.refs_7_), channel_id=1, source_target_pairs={{0,4},{1,3},{4,8},{5,1},{8,12},{9,5},{12,14},{13,9},{14,10},{15,13... | collective-permute-start | bytes 663560 | tf_op jit(solution)/shard_map/ppermute | solution.py:191
  19.7 5.2 %collective-permute-start.10 = (bf16[96,1152]{1,0:T(8,128)(2,1)S(1)}, bf16[96,1152]{1,0:T(8,128)(2,1)S(1)}, u32[]{:S(2)}, u32[]{:S(2)}) collective-permute-start(bf16[96,1152]{1,0:T(8,128)(2,1)S(1)} %collective-permute-done.9.refs_7_), channel_id=1, source_target_pairs={{0,1},{1,0},{2,3},{3,2},{4,5},{5,4},{6,7},{7,6},{8,9},{9,8},{10,11... | collective-permute-start | bytes 663560 | tf_op jit(solution)/shard_map/ppermute | solution.py:191
  19.9 5.1 %collective-permute-start.8 = (bf16[96,1152]{1,0:T(8,128)(2,1)S(1)}, bf16[96,1152]{1,0:T(8,128)(2,1)S(1)}, u32[]{:S(2)}, u32[]{:S(2)}) collective-permute-start(bf16[96,1152]{1,0:T(8,128)(2,1)S(1)} %collective-permute-done.1.refs_5_), channel_id=1, source_target_pairs={{0,1},{1,0},{2,3},{3,2},{4,5},{5,4},{6,7},{7,6},{8,9},{9,8},{10,11... | collective-permute-start | bytes 663560 | tf_op jit(solution)/shard_map/ppermute | solution.py:191
  21.8 5.9 %collective-permute-start.3 = (bf16[96,1152]{1,0:T(8,128)(2,1)S(1)}, bf16[96,1152]{1,0:T(8,128)(2,1)S(1)}, u32[]{:S(2)}, u32[]{:S(2)}) collective-permute-start(bf16[96,1152]{1,0:T(8,128)(2,1)S(1)} %collective-permute-done.2.refs_9_), channel_id=1, source_target_pairs={{0,4},{1,3},{4,8},{5,1},{8,12},{9,5},{12,14},{13,9},{14,10},{15,13... | collective-permute-start | bytes 663560 | tf_op jit(solution)/shard_map/ppermute | solution.py:191
  23.8 4.3 %collective-permute-start.17 = (bf16[96,1152]{1,0:T(8,128)(2,1)S(1)}, bf16[96,1152]{1,0:T(8,128)(2,1)S(1)}, u32[]{:S(2)}, u32[]{:S(2)}) collective-permute-start(bf16[96,1152]{1,0:T(8,128)(2,1)S(1)} %collective-permute-done.2.refs_9_), channel_id=1, source_target_pairs={{0,1},{1,0},{2,3},{3,2},{4,5},{5,4},{6,7},{7,6},{8,9},{9,8},{10,11... | collective-permute-start | bytes 663560 | tf_op jit(solution)/shard_map/ppermute | solution.py:191
  24.9 3.2 %collective-permute-start.19 = (bf16[96,1152]{1,0:T(8,128)(2,1)S(1)}, bf16[96,1152]{1,0:T(8,128)(2,1)S(1)}, u32[]{:S(2)}, u32[]{:S(2)}) collective-permute-start(bf16[96,1152]{1,0:T(8,128)(2,1)S(1)} %collective-permute-done.18.refs_2_), channel_id=1, source_target_pairs={{0,1},{1,0},{2,3},{3,2},{4,5},{5,4},{6,7},{7,6},{8,9},{9,8},{10,11... | collective-permute-start | bytes 663560 | tf_op jit(solution)/shard_map/ppermute | solution.py:191
  24.9 3.2 %copy-start.4 = (bf16[96,1152]{1,0:T(8,128)(2,1)S(1)}, bf16[96,1152]{1,0:T(8,128)(2,1)}, u32[]{:S(2)}) copy-start(bf16[96,1152]{1,0:T(8,128)(2,1)} %refs_0_.1) | copy-start | bytes 663556
  27.5 2.4 %copy-start = (bf16[1152,576]{0,1:T(8,128)(2,1)S(1)}, bf16[1152,576]{0,1:T(8,128)(2,1)}, u32[]{:S(2)}) copy-start(bf16[1152,576]{0,1:T(8,128)(2,1)} %param.12) | copy-start | bytes 3981316
  27.5 2.4 %copy-start.1 = (bf16[1152,576]{0,1:T(8,128)(2,1)S(1)}, bf16[1152,576]{0,1:T(8,128)(2,1)}, u32[]{:S(2)}) copy-start(bf16[1152,576]{0,1:T(8,128)(2,1)} %param.13) | copy-start | bytes 3981316
  27.5 2.4 %copy-start.2 = (bf16[1152,576]{0,1:T(8,128)(2,1)S(1)}, bf16[1152,576]{0,1:T(8,128)(2,1)}, u32[]{:S(2)}) copy-start(bf16[1152,576]{0,1:T(8,128)(2,1)} %param.14) | copy-start | bytes 3981316
  27.5 2.5 %copy-start.3 = (bf16[576,1152]{1,0:T(8,128)(2,1)S(1)}, bf16[576,1152]{1,0:T(8,128)(2,1)}, u32[]{:S(2)}) copy-start(bf16[576,1152]{1,0:T(8,128)(2,1)} %refs_8_.1) | copy-start | bytes 3981316
  27.7 2.2 %collective-permute-start.16 = (bf16[96,1152]{1,0:T(8,128)(2,1)S(1)}, bf16[96,1152]{1,0:T(8,128)(2,1)S(1)}, u32[]{:S(2)}, u32[]{:S(2)}) collective-permute-start(bf16[96,1152]{1,0:T(8,128)(2,1)S(1)} %collective-permute-done.3.refs_4_), channel_id=1, source_target_pairs={{0,1},{1,0},{2,3},{3,2},{4,5},{5,4},{6,7},{7,6},{8,9},{9,8},{10,11... | collective-permute-start | bytes 663560 | tf_op jit(solution)/shard_map/ppermute | solution.py:191

commit v7 on v6

--- a/solution.py
+++ b/solution.py
@@ -234,7 +234,7 @@
         if s < shards // 4 - 1:
             b = send(b, along)
     rows = total + tok
-    cuts = [0, shards - 6, shards - 1, shards]
+    cuts = [0, shards - 6, shards - 4, shards]
     starts, lanes = [], 0
     for low, high in zip(cuts[:-1], cuts[1:]):
         starts += [lanes + i * tok for i in range(high - low)]

time: 35.7 us -> 39.1 us (1.095)
  starting transfers between devices: 14.7 us -> 19.9 us
  waiting for transfers between devices: 8.49 us -> 6.28 us
  local copies, waits for them, and re-layouts: 0.14 us -> 0.99 us
  Pallas kernels: 11.2 us -> 10.8 us
    ppermute x20, starting transfers between devices: 14.7 us -> 19.9 us  [send(): return lax.ppermute(x, 'ctx', pairs)]
    ppermute x20, waiting for transfers between devices: 8.49 us -> 6.28 us  [send(): return lax.ppermute(x, 'ctx', pairs)]
    pallas_call x2, Pallas kernels: 4.3 us -> 3.28 us  [on_device_gathered(): pl.pallas_call(functools.partial(merge_kernel, n, starts[low]), out_shape...]
    unnamed x14, local copies, waits for them, and re-layouts: 0.12 us -> 0.98 us
    pallas_call x1, Pallas kernels: 5.41 us -> 6.04 us  [on_device_gathered(): pl.pallas_call(functools.partial(tail_kernel, n, starts[low]), out_shape=...]
  transfers between devices with their start and end apart: 20 -> 20, of which waited for: 7 -> 4; matrix products, arithmetic and copies ran while one was open for 2% -> 2% of each run, Pallas kernels for 16% -> 12%
where the time goes in v7:
time: 39.1 us; the launch traced here: 38.9 us
  starting transfers between devices  19.9 us (51%)
  Pallas kernels  10.8 us (28%)
  waiting for transfers between devices  6.28 us (16%)
  local copies, waits for them, and re-layouts  0.99 us (3%)
  other arithmetic  0.73 us (2%)
    ppermute x20, starting transfers between devices, send(): return lax.ppermute(x, 'ctx', pairs)  19.9 us
    ppermute x20, waiting for transfers between devices, send(): return lax.ppermute(x, 'ctx', pairs)  6.28 us
    pallas_call x1, Pallas kernels, on_device_gathered(): pl.pallas_call(functools.partial(tail_kernel, n, starts[low]), out_shape=...  6.04 us
    pallas_call x2, Pallas kernels, on_device_gathered(): pl.pallas_call(functools.partial(merge_kernel, n, starts[low]), out_shape...  3.28 us
    pallas_call x1, Pallas kernels, on_device_gathered(): pl.pallas_call(functools.partial(prep_kernel, shards, slots, tok, merged_...  1.33 us
    unnamed x14, local copies, waits for them, and re-layouts  0.98 us
  transfers between devices with their start and end apart: 20, of which 4 were waited for; matrix products, arithmetic and copies ran while one was open for 2% of the time, Pallas kernels for 12%

profile of v7, /device:TPU:0, one launch (start us, length us, event | category | flops | bytes accessed | tf_op | source)
XLA Modules:
  0.0 38.9 jit_solution(8819331549021049092)
XLA Ops:
  0.0 0.5 %collective-permute-start.8 = (bf16[96,1152]{1,0:T(8,128)(2,1)}, bf16[96,1152]{1,0:T(8,128)(2,1)S(1)}, u32[]{:S(2)}, u32[]{:S(2)}) collective-permute-start(bf16[96,1152]{1,0:T(8,128)(2,1)} %refs_0_.1), channel_id=1, source_target_pairs={{0,1},{1,0},{2,3},{3,2},{4,5},{5,4},{6,7},{7,6},{8,9},{9,8},{10,11... | collective-permute-start | bytes 663560 | tf_op jit(solution)/shard_map/ppermute | solution.py:191
  0.5 2.6 %collective-permute-start.4 = (bf16[96,1152]{1,0:T(8,128)(2,1)}, bf16[96,1152]{1,0:T(8,128)(2,1)S(1)}, u32[]{:S(2)}, u32[]{:S(2)}) collective-permute-start(bf16[96,1152]{1,0:T(8,128)(2,1)} %refs_0_.1), channel_id=1, source_target_pairs={{0,4},{1,3},{4,8},{5,1},{8,12},{9,5},{12,14},{13,9},{14,10},{15,13... | collective-permute-start | bytes 663560 | tf_op jit(solution)/shard_map/ppermute | solution.py:191
  3.0 1.4 %collective-permute-start = (bf16[96,1152]{1,0:T(8,128)(2,1)}, bf16[96,1152]{1,0:T(8,128)(2,1)S(1)}, u32[]{:S(2)}, u32[]{:S(2)}) collective-permute-start(bf16[96,1152]{1,0:T(8,128)(2,1)} %refs_0_.1), channel_id=1, source_target_pairs={{1,4},{0,3},{5,8},{4,1},{9,12},{8,5},{13,14},{12,9},{15,10},{14,13... | collective-permute-start | bytes 663560 | tf_op jit(solution)/shard_map/ppermute | solution.py:191
  4.4 0.7 %pad_add_fusion.given_ref = s32[14,1,128]{2,1,0:T(1,128)S(1)} fusion(s32[1,1,96]{2,1,0:T(1,128)} %bitcast.10, s32[1,1,96]{2,1,0:T(1,128)} %bitcast.11, s32[12,1,16]{2,1,0:T(1,128)} %bitcast.9), kind=kLoop, calls=%fused_computation.12 | loop fusion | flops 3584 | bytes 8704 | tf_op jit(solution)/shard_map/concatenate | solution.py:195
  5.1 0.2 shard_map.82
  5.3 0.0 collective-permute-done.8.refs_0_
  5.3 0.5 %collective-permute-start.13 = (bf16[16,128]{1,0:T(8,128)(2,1)S(1)}, bf16[16,128]{1,0:T(8,128)(2,1)S(1)}, u32[]{:S(2)}, u32[]{:S(2)}) collective-permute-start(bf16[16,128]{1,0:T(8,128)(2,1)S(1)} %shard_map.82), channel_id=1, source_target_pairs={{0,4},{1,5},{2,6},{3,7},{4,0},{5,1},{6,2},{7,3},{8,12},{9,13},{10,... | collective-permute-start | bytes 12296 | tf_op jit(solution)/shard_map/ppermute | solution.py:191
  5.8 2.3 %collective-permute-start.14 = (bf16[16,128]{1,0:T(8,128)(2,1)S(1)}, bf16[16,128]{1,0:T(8,128)(2,1)S(1)}, u32[]{:S(2)}, u32[]{:S(2)}) collective-permute-start(bf16[16,128]{1,0:T(8,128)(2,1)S(1)} %shard_map.82), channel_id=1, source_target_pairs={{0,8},{1,9},{2,10},{3,11},{4,12},{5,13},{6,14},{7,15},{8,0},{9,1},... | collective-permute-start | bytes 12296 | tf_op jit(solution)/shard_map/ppermute | solution.py:191
  8.1 1.6 %collective-permute-start.15 = (bf16[16,128]{1,0:T(8,128)(2,1)S(1)}, bf16[16,128]{1,0:T(8,128)(2,1)S(1)}, u32[]{:S(2)}, u32[]{:S(2)}) collective-permute-start(bf16[16,128]{1,0:T(8,128)(2,1)S(1)} %shard_map.82), channel_id=1, source_target_pairs={{0,12},{1,13},{2,14},{3,15},{4,8},{5,9},{6,10},{7,11},{8,4},{9,5},... | collective-permute-start | bytes 12296 | tf_op jit(solution)/shard_map/ppermute | solution.py:191
  9.8 0.0 collective-permute-done.refs_3_
  9.8 1.8 %collective-permute-start.1 = (bf16[96,1152]{1,0:T(8,128)(2,1)S(1)}, bf16[96,1152]{1,0:T(8,128)(2,1)S(1)}, u32[]{:S(2)}, u32[]{:S(2)}) collective-permute-start(bf16[96,1152]{1,0:T(8,128)(2,1)S(1)} %collective-permute-done.refs_3_), channel_id=1, source_target_pairs={{0,4},{1,3},{4,8},{5,1},{8,12},{9,5},{12,14},{13,9},{14,10},{15,13... | collective-permute-start | bytes 663560 | tf_op jit(solution)/shard_map/ppermute | solution.py:191
  11.6 0.0 collective-permute-done.4.refs_1_
  11.6 0.0 collective-permute-start.10
  11.6 0.0 collective-permute-done.13
  11.6 1.8 %collective-permute-start.5 = (bf16[96,1152]{1,0:T(8,128)(2,1)S(1)}, bf16[96,1152]{1,0:T(8,128)(2,1)S(1)}, u32[]{:S(2)}, u32[]{:S(2)}) collective-permute-start(bf16[96,1152]{1,0:T(8,128)(2,1)S(1)} %collective-permute-done.4.refs_1_), channel_id=1, source_target_pairs={{0,4},{1,3},{4,8},{5,1},{8,12},{9,5},{12,14},{13,9},{14,10},{15,13... | collective-permute-start | bytes 663560 | tf_op jit(solution)/shard_map/ppermute | solution.py:191
  13.4 0.3 collective-permute-done.15
  13.6 0.7 %collective-permute-start.16 = (bf16[64,128]{1,0:T(8,128)(2,1)S(1)}, bf16[64,128]{1,0:T(8,128)(2,1)S(1)}, u32[]{:S(2)}, u32[]{:S(2)}) collective-permute-start(bf16[64,128]{1,0:T(8,128)(2,1)S(1)} %pad_maximum_fusion), channel_id=1, source_target_pairs={{0,2},{1,3},{2,0},{3,1},{4,6},{5,7},{6,4},{7,5},{8,10},{9,11},{10,... | collective-permute-start | bytes 49160 | tf_op jit(solution)/shard_map/ppermute | solution.py:191
  14.3 3.9 %collective-permute-done.5.refs_5_ = bf16[96,1152]{1,0:T(8,128)(2,1)S(1)} collective-permute-done((bf16[96,1152]{1,0:T(8,128)(2,1)S(1)}, bf16[96,1152]{1,0:T(8,128)(2,1)S(1)}, u32[]{:S(2)}, u32[]{:S(2)}) %collective-permute-start.5) | collective-permute-done | bytes 221216 | tf_op jit(solution)/shard_map/ppermute | solution.py:191
  18.2 1.6 %collective-permute-start.6 = (bf16[96,1152]{1,0:T(8,128)(2,1)S(1)}, bf16[96,1152]{1,0:T(8,128)(2,1)S(1)}, u32[]{:S(2)}, u32[]{:S(2)}) collective-permute-start(bf16[96,1152]{1,0:T(8,128)(2,1)S(1)} %collective-permute-done.5.refs_5_), channel_id=1, source_target_pairs={{0,4},{1,3},{4,8},{5,1},{8,12},{9,5},{12,14},{13,9},{14,10},{15,13... | collective-permute-start | bytes 663560 | tf_op jit(solution)/shard_map/ppermute | solution.py:191
  19.9 0.0 collective-permute-done.16
  19.9 0.1 collective-permute-start.17
  20.0 0.5 %collective-permute-start.9 = (bf16[96,1152]{1,0:T(8,128)(2,1)S(1)}, bf16[96,1152]{1,0:T(8,128)(2,1)S(1)}, u32[]{:S(2)}, u32[]{:S(2)}) collective-permute-start(bf16[96,1152]{1,0:T(8,128)(2,1)S(1)} %collective-permute-done.4.refs_1_), channel_id=1, source_target_pairs={{0,1},{1,0},{2,3},{3,2},{4,5},{5,4},{6,7},{7,6},{8,9},{9,8},{10,11... | collective-permute-start | bytes 663560 | tf_op jit(solution)/shard_map/ppermute | solution.py:191
  20.5 1.7 %collective-permute-start.2 = (bf16[96,1152]{1,0:T(8,128)(2,1)S(1)}, bf16[96,1152]{1,0:T(8,128)(2,1)S(1)}, u32[]{:S(2)}, u32[]{:S(2)}) collective-permute-start(bf16[96,1152]{1,0:T(8,128)(2,1)S(1)} %collective-permute-done.1.refs_7_), channel_id=1, source_target_pairs={{0,4},{1,3},{4,8},{5,1},{8,12},{9,5},{12,14},{13,9},{14,10},{15,13... | collective-permute-start | bytes 663560 | tf_op jit(solution)/shard_map/ppermute | solution.py:191
  22.2 0.0 collective-permute-done.17
  22.2 0.0 collective-permute-start.11
  22.2 0.0 collective-permute-done.10.refs_4_
  22.2 0.5 %collective-permute-start.12 = (bf16[96,1152]{1,0:T(8,128)(2,1)S(1)}, bf16[96,1152]{1,0:T(8,128)(2,1)S(1)}, u32[]{:S(2)}, u32[]{:S(2)}) collective-permute-start(bf16[96,1152]{1,0:T(8,128)(2,1)S(1)} %collective-permute-done.1.refs_7_), channel_id=1, source_target_pairs={{0,1},{1,0},{2,3},{3,2},{4,5},{5,4},{6,7},{7,6},{8,9},{9,8},{10,11... | collective-permute-start | bytes 663560 | tf_op jit(solution)/shard_map/ppermute | solution.py:191
  22.7 1.5 %collective-permute-done.6.refs_9_ = bf16[96,1152]{1,0:T(8,128)(2,1)S(1)} collective-permute-done((bf16[96,1152]{1,0:T(8,128)(2,1)S(1)}, bf16[96,1152]{1,0:T(8,128)(2,1)S(1)}, u32[]{:S(2)}, u32[]{:S(2)}) %collective-permute-start.6) | collective-permute-done | bytes 221216 | tf_op jit(solution)/shard_map/ppermute | solution.py:191
  24.2 1.6 %collective-permute-start.7 = (bf16[96,1152]{1,0:T(8,128)(2,1)S(1)}, bf16[96,1152]{1,0:T(8,128)(2,1)S(1)}, u32[]{:S(2)}, u32[]{:S(2)}) collective-permute-start(bf16[96,1152]{1,0:T(8,128)(2,1)S(1)} %collective-permute-done.6.refs_9_), channel_id=1, source_target_pairs={{0,4},{1,3},{4,8},{5,1},{8,12},{9,5},{12,14},{13,9},{14,10},{15,13... | collective-permute-start | bytes 663560 | tf_op jit(solution)/shard_map/ppermute | solution.py:191
  25.8 1.3 %shard_map.83 = (bf16[864,1664]{1,0:T(8,128)(2,1)S(1)}, f32[864,1]{1,0:T(8,128)S(1)}, f32[1,768]{1,0:T(1,128)S(1)}) custom-call(bf16[256,128]{1,0:T(8,128)(2,1)S(1)} %constant_dynamic-update-slice_fusion.5.g_ref), custom_call_target="tpu_custom_call" | custom-call | flops 1000 | bytes 1000 | tf_op jit(solution)/shard_map/pallas_call | solution.py:242
  27.2 0.0 collective-permute-done.9.refs_2_
  27.2 0.1 collective-permute-start.19
  27.3 0.5 %collective-permute-start.3 = (bf16[96,1152]{1,0:T(8,128)(2,1)S(1)}, bf16[96,1152]{1,0:T(8,128)(2,1)S(1)}, u32[]{:S(2)}, u32[]{:S(2)}) collective-permute-start(bf16[96,1152]{1,0:T(8,128)(2,1)S(1)} %collective-permute-done.2.refs_0_), channel_id=1, source_target_pairs={{0,1},{1,0},{2,3},{3,2},{4,5},{5,4},{6,7},{7,6},{8,9},{9,8},{10,11... | collective-permute-start | bytes 663560 | tf_op jit(solution)/shard_map/ppermute | solution.py:191
  27.8 0.0 collective-permute-done.12.refs_8_
  27.8 2.5 %shard_map.84.refs_3_ = f32[864,1152]{1,0:T(8,128)S(1)} custom-call(bf16[96,1152]{1,0:T(8,128)(2,1)S(1)} %collective-permute-done.8.refs_0_, bf16[96,1152]{1,0:T(8,128)(2,1)S(1)} %collective-permute-done.4.refs_1_, bf16[96,1152]{1,0:T(8,128)(2,1)S(1)} %collective-permute-done.9.refs_2_, bf16[96,1152]{1,0:T(8,128)(2,1)S(1)} %collective-permute-done.refs_3_, ...), custom_call_target="tpu_custom_call" | custom-call | flops 1000 | bytes 1000 | tf_op jit(solution)/shard_map/pallas_call | solution.py:264
  30.3 0.0 copy-start
  30.3 0.0 copy-start.1
  30.3 0.0 copy-start.2
  30.3 0.0 copy-start.3
  30.3 0.0 collective-permute-done.7.refs_2_
  30.4 0.2 collective-permute-start.18
  30.5 0.8 %shard_map.85.refs_4_ = f32[864,1152]{1,0:T(8,128)S(1)} custom-call(bf16[96,1152]{1,0:T(8,128)(2,1)S(1)} %copy-done.4, bf16[96,1152]{1,0:T(8,128)(2,1)S(1)} %collective-permute-done.19.refs_1_, bf16[864,1664]{1,0:T(8,128)(2,1)S(1)} %get-tuple-element.11.refs_10_.refs_2_.refs_5_, f32[864,1152]{1,0:T(8,128)S(1)} %shard_map.84.refs_3_), custom_call_target="tpu_custom_call", output_to_operand_aliasing={{}: (3, {})} | custom-call | flops 1000 | bytes 1000 | tf_op jit(solution)/shard_map/pallas_call | solution.py:264
  31.3 0.0 collective-permute-done.3.refs_1_
  31.3 0.6 %collective-permute-done.18.refs_3_ = bf16[96,1152]{1,0:T(8,128)(2,1)S(1)} collective-permute-done((bf16[96,1152]{1,0:T(8,128)(2,1)S(1)}, bf16[96,1152]{1,0:T(8,128)(2,1)S(1)}, u32[]{:S(2)}, u32[]{:S(2)}) %collective-permute-start.18) | collective-permute-done | bytes 221216 | tf_op jit(solution)/shard_map/ppermute | solution.py:191
  31.9 0.1 copy-done.1
  32.0 0.4 %copy-done.2 = bf16[1152,576]{0,1:T(8,128)(2,1)S(1)} copy-done((bf16[1152,576]{0,1:T(8,128)(2,1)S(1)}, bf16[1152,576]{0,1:T(8,128)(2,1)}, u32[]{:S(2)}) %copy-start.2) | copy-done | bytes 1327128
  32.4 0.4 %copy-done.3 = bf16[576,1152]{1,0:T(8,128)(2,1)S(1)} copy-done((bf16[576,1152]{1,0:T(8,128)(2,1)S(1)}, bf16[576,1152]{1,0:T(8,128)(2,1)}, u32[]{:S(2)}) %copy-start.3) | copy-done | bytes 1327128
  32.8 6.0 %shard_map.86 = bf16[96,1152]{1,0:T(8,128)(2,1)} custom-call(bf16[96,1152]{1,0:T(8,128)(2,1)S(1)} %collective-permute-done.2.refs_0_, bf16[96,1152]{1,0:T(8,128)(2,1)S(1)} %collective-permute-done.3.refs_1_, bf16[96,1152]{1,0:T(8,128)(2,1)S(1)} %collective-permute-done.7.refs_2_, bf16[96,1152]{1,0:T(8,128)(2,1)S(1)} %collective-permute-done.18.refs_3_, ...), custom_call_target="tpu_custom_call" | custom-call | flops 2038431744 | bytes 5308416 | tf_op jit(solution)/shard_map/pallas_call | solution.py:279
  (15 shorter events, 0.1 us)
Async XLA Ops:
  0.0 5.3 %collective-permute-start.8 = (bf16[96,1152]{1,0:T(8,128)(2,1)}, bf16[96,1152]{1,0:T(8,128)(2,1)S(1)}, u32[]{:S(2)}, u32[]{:S(2)}) collective-permute-start(bf16[96,1152]{1,0:T(8,128)(2,1)} %refs_0_.1), channel_id=1, source_target_pairs={{0,1},{1,0},{2,3},{3,2},{4,5},{5,4},{6,7},{7,6},{8,9},{9,8},{10,11... | collective-permute-start | bytes 663560 | tf_op jit(solution)/shard_map/ppermute | solution.py:191
  0.5 11.1 %collective-permute-start.4 = (bf16[96,1152]{1,0:T(8,128)(2,1)}, bf16[96,1152]{1,0:T(8,128)(2,1)S(1)}, u32[]{:S(2)}, u32[]{:S(2)}) collective-permute-start(bf16[96,1152]{1,0:T(8,128)(2,1)} %refs_0_.1), channel_id=1, source_target_pairs={{0,4},{1,3},{4,8},{5,1},{8,12},{9,5},{12,14},{13,9},{14,10},{15,13... | collective-permute-start | bytes 663560 | tf_op jit(solution)/shard_map/ppermute | solution.py:191
  3.0 6.7 %collective-permute-start = (bf16[96,1152]{1,0:T(8,128)(2,1)}, bf16[96,1152]{1,0:T(8,128)(2,1)S(1)}, u32[]{:S(2)}, u32[]{:S(2)}) collective-permute-start(bf16[96,1152]{1,0:T(8,128)(2,1)} %refs_0_.1), channel_id=1, source_target_pairs={{1,4},{0,3},{5,8},{4,1},{9,12},{8,5},{13,14},{12,9},{15,10},{14,13... | collective-permute-start | bytes 663560 | tf_op jit(solution)/shard_map/ppermute | solution.py:191
  5.3 6.3 %collective-permute-start.13 = (bf16[16,128]{1,0:T(8,128)(2,1)S(1)}, bf16[16,128]{1,0:T(8,128)(2,1)S(1)}, u32[]{:S(2)}, u32[]{:S(2)}) collective-permute-start(bf16[16,128]{1,0:T(8,128)(2,1)S(1)} %shard_map.82), channel_id=1, source_target_pairs={{0,4},{1,5},{2,6},{3,7},{4,0},{5,1},{6,2},{7,3},{8,12},{9,13},{10,... | collective-permute-start | bytes 12296 | tf_op jit(solution)/shard_map/ppermute | solution.py:191
  5.8 7.5 %collective-permute-start.14 = (bf16[16,128]{1,0:T(8,128)(2,1)S(1)}, bf16[16,128]{1,0:T(8,128)(2,1)S(1)}, u32[]{:S(2)}, u32[]{:S(2)}) collective-permute-start(bf16[16,128]{1,0:T(8,128)(2,1)S(1)} %shard_map.82), channel_id=1, source_target_pairs={{0,8},{1,9},{2,10},{3,11},{4,12},{5,13},{6,14},{7,15},{8,0},{9,1},... | collective-permute-start | bytes 12296 | tf_op jit(solution)/shard_map/ppermute | solution.py:191
  8.1 5.5 %collective-permute-start.15 = (bf16[16,128]{1,0:T(8,128)(2,1)S(1)}, bf16[16,128]{1,0:T(8,128)(2,1)S(1)}, u32[]{:S(2)}, u32[]{:S(2)}) collective-permute-start(bf16[16,128]{1,0:T(8,128)(2,1)S(1)} %shard_map.82), channel_id=1, source_target_pairs={{0,12},{1,13},{2,14},{3,15},{4,8},{5,9},{6,10},{7,11},{8,4},{9,5},... | collective-permute-start | bytes 12296 | tf_op jit(solution)/shard_map/ppermute | solution.py:191
  9.8 10.7 %collective-permute-start.1 = (bf16[96,1152]{1,0:T(8,128)(2,1)S(1)}, bf16[96,1152]{1,0:T(8,128)(2,1)S(1)}, u32[]{:S(2)}, u32[]{:S(2)}) collective-permute-start(bf16[96,1152]{1,0:T(8,128)(2,1)S(1)} %collective-permute-done.refs_3_), channel_id=1, source_target_pairs={{0,4},{1,3},{4,8},{5,1},{8,12},{9,5},{12,14},{13,9},{14,10},{15,13... | collective-permute-start | bytes 663560 | tf_op jit(solution)/shard_map/ppermute | solution.py:191
  11.6 10.6 %collective-permute-start.10 = (bf16[96,1152]{1,0:T(8,128)(2,1)S(1)}, bf16[96,1152]{1,0:T(8,128)(2,1)S(1)}, u32[]{:S(2)}, u32[]{:S(2)}) collective-permute-start(bf16[96,1152]{1,0:T(8,128)(2,1)S(1)} %collective-permute-done.refs_3_), channel_id=1, source_target_pairs={{0,1},{1,0},{2,3},{3,2},{4,5},{5,4},{6,7},{7,6},{8,9},{9,8},{10,11... | collective-permute-start | bytes 663560 | tf_op jit(solution)/shard_map/ppermute | solution.py:191
  11.6 6.6 %collective-permute-start.5 = (bf16[96,1152]{1,0:T(8,128)(2,1)S(1)}, bf16[96,1152]{1,0:T(8,128)(2,1)S(1)}, u32[]{:S(2)}, u32[]{:S(2)}) collective-permute-start(bf16[96,1152]{1,0:T(8,128)(2,1)S(1)} %collective-permute-done.4.refs_1_), channel_id=1, source_target_pairs={{0,4},{1,3},{4,8},{5,1},{8,12},{9,5},{12,14},{13,9},{14,10},{15,13... | collective-permute-start | bytes 663560 | tf_op jit(solution)/shard_map/ppermute | solution.py:191
  13.6 6.3 %collective-permute-start.16 = (bf16[64,128]{1,0:T(8,128)(2,1)S(1)}, bf16[64,128]{1,0:T(8,128)(2,1)S(1)}, u32[]{:S(2)}, u32[]{:S(2)}) collective-permute-start(bf16[64,128]{1,0:T(8,128)(2,1)S(1)} %pad_maximum_fusion), channel_id=1, source_target_pairs={{0,2},{1,3},{2,0},{3,1},{4,6},{5,7},{6,4},{7,5},{8,10},{9,11},{10,... | collective-permute-start | bytes 49160 | tf_op jit(solution)/shard_map/ppermute | solution.py:191
  18.2 5.9 %collective-permute-start.6 = (bf16[96,1152]{1,0:T(8,128)(2,1)S(1)}, bf16[96,1152]{1,0:T(8,128)(2,1)S(1)}, u32[]{:S(2)}, u32[]{:S(2)}) collective-permute-start(bf16[96,1152]{1,0:T(8,128)(2,1)S(1)} %collective-permute-done.5.refs_5_), channel_id=1, source_target_pairs={{0,4},{1,3},{4,8},{5,1},{8,12},{9,5},{12,14},{13,9},{14,10},{15,13... | collective-permute-start | bytes 663560 | tf_op jit(solution)/shard_map/ppermute | solution.py:191
  19.9 2.3 %collective-permute-start.17 = (bf16[128,128]{1,0:T(8,128)(2,1)S(1)}, bf16[128,128]{1,0:T(8,128)(2,1)S(1)}, u32[]{:S(2)}, u32[]{:S(2)}) collective-permute-start(bf16[128,128]{1,0:T(8,128)(2,1)S(1)} %get-tuple-element.15), channel_id=1, source_target_pairs={{0,1},{1,0},{2,3},{3,2},{4,5},{5,4},{6,7},{7,6},{8,9},{9,8},{10,11... | collective-permute-start | bytes 98312 | tf_op jit(solution)/shard_map/ppermute | solution.py:191
  20.0 7.2 %collective-permute-start.9 = (bf16[96,1152]{1,0:T(8,128)(2,1)S(1)}, bf16[96,1152]{1,0:T(8,128)(2,1)S(1)}, u32[]{:S(2)}, u32[]{:S(2)}) collective-permute-start(bf16[96,1152]{1,0:T(8,128)(2,1)S(1)} %collective-permute-done.4.refs_1_), channel_id=1, source_target_pairs={{0,1},{1,0},{2,3},{3,2},{4,5},{5,4},{6,7},{7,6},{8,9},{9,8},{10,11... | collective-permute-start | bytes 663560 | tf_op jit(solution)/shard_map/ppermute | solution.py:191
  20.5 6.8 %collective-permute-start.2 = (bf16[96,1152]{1,0:T(8,128)(2,1)S(1)}, bf16[96,1152]{1,0:T(8,128)(2,1)S(1)}, u32[]{:S(2)}, u32[]{:S(2)}) collective-permute-start(bf16[96,1152]{1,0:T(8,128)(2,1)S(1)} %collective-permute-done.1.refs_7_), channel_id=1, source_target_pairs={{0,4},{1,3},{4,8},{5,1},{8,12},{9,5},{12,14},{13,9},{14,10},{15,13... | collective-permute-start | bytes 663560 | tf_op jit(solution)/shard_map/ppermute | solution.py:191
  22.2 5.6 %collective-permute-start.11 = (bf16[96,1152]{1,0:T(8,128)(2,1)S(1)}, bf16[96,1152]{1,0:T(8,128)(2,1)S(1)}, u32[]{:S(2)}, u32[]{:S(2)}) collective-permute-start(bf16[96,1152]{1,0:T(8,128)(2,1)S(1)} %collective-permute-done.5.refs_5_), channel_id=1, source_target_pairs={{0,1},{1,0},{2,3},{3,2},{4,5},{5,4},{6,7},{7,6},{8,9},{9,8},{10,11... | collective-permute-start | bytes 663560 | tf_op jit(solution)/shard_map/ppermute | solution.py:191
  22.2 5.6 %collective-permute-start.12 = (bf16[96,1152]{1,0:T(8,128)(2,1)S(1)}, bf16[96,1152]{1,0:T(8,128)(2,1)S(1)}, u32[]{:S(2)}, u32[]{:S(2)}) collective-permute-start(bf16[96,1152]{1,0:T(8,128)(2,1)S(1)} %collective-permute-done.1.refs_7_), channel_id=1, source_target_pairs={{0,1},{1,0},{2,3},{3,2},{4,5},{5,4},{6,7},{7,6},{8,9},{9,8},{10,11... | collective-permute-start | bytes 663560 | tf_op jit(solution)/shard_map/ppermute | solution.py:191
  24.2 6.2 %collective-permute-start.7 = (bf16[96,1152]{1,0:T(8,128)(2,1)S(1)}, bf16[96,1152]{1,0:T(8,128)(2,1)S(1)}, u32[]{:S(2)}, u32[]{:S(2)}) collective-permute-start(bf16[96,1152]{1,0:T(8,128)(2,1)S(1)} %collective-permute-done.6.refs_9_), channel_id=1, source_target_pairs={{0,4},{1,3},{4,8},{5,1},{8,12},{9,5},{12,14},{13,9},{14,10},{15,13... | collective-permute-start | bytes 663560 | tf_op jit(solution)/shard_map/ppermute | solution.py:191
  27.2 3.3 %collective-permute-start.19 = (bf16[96,1152]{1,0:T(8,128)(2,1)S(1)}, bf16[96,1152]{1,0:T(8,128)(2,1)S(1)}, u32[]{:S(2)}, u32[]{:S(2)}) collective-permute-start(bf16[96,1152]{1,0:T(8,128)(2,1)S(1)} %collective-permute-done.6.refs_9_), channel_id=1, source_target_pairs={{0,1},{1,0},{2,3},{3,2},{4,5},{5,4},{6,7},{7,6},{8,9},{9,8},{10,11... | collective-permute-start | bytes 663560 | tf_op jit(solution)/shard_map/ppermute | solution.py:191
  27.3 4.0 %collective-permute-start.3 = (bf16[96,1152]{1,0:T(8,128)(2,1)S(1)}, bf16[96,1152]{1,0:T(8,128)(2,1)S(1)}, u32[]{:S(2)}, u32[]{:S(2)}) collective-permute-start(bf16[96,1152]{1,0:T(8,128)(2,1)S(1)} %collective-permute-done.2.refs_0_), channel_id=1, source_target_pairs={{0,1},{1,0},{2,3},{3,2},{4,5},{5,4},{6,7},{7,6},{8,9},{9,8},{10,11... | collective-permute-start | bytes 663560 | tf_op jit(solution)/shard_map/ppermute | solution.py:191
  27.8 2.7 %copy-start.4 = (bf16[96,1152]{1,0:T(8,128)(2,1)S(1)}, bf16[96,1152]{1,0:T(8,128)(2,1)}, u32[]{:S(2)}) copy-start(bf16[96,1152]{1,0:T(8,128)(2,1)} %refs_0_.1) | copy-start | bytes 663556
  30.3 1.6 %copy-start = (bf16[1152,576]{0,1:T(8,128)(2,1)S(1)}, bf16[1152,576]{0,1:T(8,128)(2,1)}, u32[]{:S(2)}) copy-start(bf16[1152,576]{0,1:T(8,128)(2,1)} %param.12) | copy-start | bytes 3981316
  30.3 1.7 %copy-start.1 = (bf16[1152,576]{0,1:T(8,128)(2,1)S(1)}, bf16[1152,576]{0,1:T(8,128)(2,1)}, u32[]{:S(2)}) copy-start(bf16[1152,576]{0,1:T(8,128)(2,1)} %param.13) | copy-start | bytes 3981316
  30.3 2.1 %copy-start.2 = (bf16[1152,576]{0,1:T(8,128)(2,1)S(1)}, bf16[1152,576]{0,1:T(8,128)(2,1)}, u32[]{:S(2)}) copy-start(bf16[1152,576]{0,1:T(8,128)(2,1)} %param.14) | copy-start | bytes 3981316
  30.3 2.5 %copy-start.3 = (bf16[576,1152]{1,0:T(8,128)(2,1)S(1)}, bf16[576,1152]{1,0:T(8,128)(2,1)}, u32[]{:S(2)}) copy-start(bf16[576,1152]{1,0:T(8,128)(2,1)} %refs_11_.1) | copy-start | bytes 3981316
  30.4 1.5 %collective-permute-start.18 = (bf16[96,1152]{1,0:T(8,128)(2,1)S(1)}, bf16[96,1152]{1,0:T(8,128)(2,1)S(1)}, u32[]{:S(2)}, u32[]{:S(2)}) collective-permute-start(bf16[96,1152]{1,0:T(8,128)(2,1)S(1)} %collective-permute-done.7.refs_2_), channel_id=1, source_target_pairs={{0,1},{1,0},{2,3},{3,2},{4,5},{5,4},{6,7},{7,6},{8,9},{9,8},{10,11... | collective-permute-start | bytes 663560 | tf_op jit(solution)/shard_map/ppermute | solution.py:191
